TPU v7x, 32 devices: a whole 2x2x4 slice. The times are simulated.
32 devices in a mesh: fsdp: 2 (over x), rows: 16 (over z, y, core).
Axes of the slice: x: 2, y: 2, z: 4, core: 2. Of those that a mesh axis runs over, the one named last changes fastest.
Arguments:
- residual_target: float32 [2, 12, 128, 512], P('fsdp', None, 'rows'), may hold values from -40 to 40
- conditioning: float32 [2, 12, 128, 512], P('fsdp', None, 'rows'), may hold values from -20 to 20
- noise_sample: float32 [2, 12, 128, 512], P('fsdp', None, 'rows'), may hold values from -20 to 20
- noise_level: int32 [2], P('fsdp'), may hold values from 0 to 63
- input_kernel: float32 [9, 64, 24], P(None, 'fsdp'), may hold values from -0.4375 to 0.4375
- first_kernel: float32 [9, 64, 64], P(None, 'fsdp'), may hold values from -0.25 to 0.25
- second_kernel: float32 [9, 64, 64], P(None, 'fsdp'), may hold values from -0.25 to 0.25
- down_kernel: float32 [9, 128, 64], P(None, 'fsdp'), may hold values from -0.25 to 0.25
- coarse_kernel: float32 [9, 128, 128], P(None, 'fsdp'), may hold values from -0.1875 to 0.1875
- upward_kernel: float32 [9, 64, 128], P(None, 'fsdp'), may hold values from -0.1875 to 0.1875
- output_kernel: float32 [9, 12, 64], P(None, None, 'fsdp'), may hold values from -0.25 to 0.25
- embed_matrix: float32 [128, 64], P('fsdp'), may hold values from -0.5 to 0.5
Outputs:
- denoised: float32 [2, 12, 128, 512], P('fsdp', None, 'rows')
- loss_value: float32 [], replicated
- input_grad: float32 [9, 64, 24], P(None, 'fsdp')
- first_grad: float32 [9, 64, 64], P(None, 'fsdp')
- second_grad: float32 [9, 64, 64], P(None, 'fsdp')
- down_grad: float32 [9, 128, 64], P(None, 'fsdp')
- coarse_grad: float32 [9, 128, 128], P(None, 'fsdp')
- upward_grad: float32 [9, 64, 128], P(None, 'fsdp')
- output_grad: float32 [9, 12, 64], P(None, None, 'fsdp')
- embed_grad: float32 [128, 64], P('fsdp')
All inputs are finite; a program needn't handle non-finite values.
Results may differ from a plain program's by a relative error of at most 0.03.
Values may be sent and summed in bfloat16 or wider, within the bound.
No kernel may reach another device: no remote copies, remote signals or barrier semaphores. Data moves between devices by JAX's collectives and lax.ppermute only.
A program may use at most 128 MiB of HBM per device.

v0:
```python
import functools

import jax
import jax.numpy as jnp
from jax import lax
from jax.experimental import pallas as pl
from jax.experimental.pallas import tpu as pltpu
from jax.sharding import PartitionSpec as P

GROUPS = 32
STEPS = 64

sigma_low = 0.002
sigma_high = 80.0
sigma_data = 0.5
rho_power = 7.0
eps_norm = 1e-05

F32 = jnp.float32
BF16 = jnp.bfloat16

HALF = 256
ROWS = 8
CROWS = 4
FAR = 7
LIMIT = 24 * 1024 * 1024


def preconditions(level_index):
    ramp_value = level_index.astype(jnp.float32) / (STEPS - 1)
    top_root = sigma_high ** (1.0 / rho_power)
    bottom = sigma_low ** (1.0 / rho_power)
    sigma_level = (top_root + ramp_value * (bottom - top_root)) ** rho_power
    sigma_total = sigma_level * sigma_level + sigma_data * sigma_data
    skip_scale = sigma_data * sigma_data / sigma_total
    out_scale = sigma_level * sigma_data * lax.rsqrt(sigma_total)
    in_scale = lax.rsqrt(sigma_total)
    weight = sigma_total / (sigma_level * sigma_data) ** 2
    return (sigma_level, skip_scale, out_scale, in_scale, weight)


def embedding(sigma_level, features):
    half_count = features // 2
    ramp_steps = jnp.arange(half_count, dtype=jnp.float32) / half_count
    frequency = 64.0 * 0.01**ramp_steps
    phase_angle = 0.25 * jnp.log(sigma_level) * frequency
    return jnp.concatenate([jnp.cos(phase_angle), jnp.sin(phase_angle)]).astype(jnp.bfloat16)


class Source:
    def __init__(self, spot, copies, first):
        self.spot, self.copies, self.first = spot, copies, first
        self.shape = spot.shape
        for _, copy in copies:
            copy.start()

    def wait(self, stage):
        for when, copy in self.copies:
            if when == stage:
                copy.wait()


class Sink:
    def __init__(self, spot, copies, first):
        self.spot, self.copies, self.first = spot, copies, first
        self.shape = spot.shape
        self.started = []

    def done(self, index):
        for last, copy in self.copies:
            if last == index:
                copy.start()
                self.started.append(copy)

    def finish(self):
        for _, copy in self.copies:
            if not any(copy is other for other in self.started):
                copy.start()
                self.started.append(copy)


def spot(ref, index):
    if len(ref.shape) == 3:
        return (index - getattr(ref, "first", 0),)
    start = index - getattr(ref, "first", 0)
    return (slice(None), slice(start * HALF, (start + 1) * HALF))


def row(ref, index):
    return getattr(ref, "spot", ref)[spot(ref, index)]


def put(ref, index, value):
    getattr(ref, "spot", ref)[spot(ref, index)] = value
    if isinstance(ref, Sink):
        ref.done(index)


def whole(ref):
    return ref.spot[...]


def give(ref, value):
    ref.spot[...] = value
    ref.finish()


def lane(shape):
    return lax.broadcasted_iota(jnp.int32, shape, 1)


def from_left(value):
    moved = pltpu.roll(value, 1, 1)
    return jnp.where(lane(value.shape) == 0, 0.0, moved)


def from_right(value):
    moved = pltpu.roll(value, value.shape[1] - 1, 1)
    return jnp.where(lane(value.shape) == value.shape[1] - 1, 0.0, moved)


def mm(left, right):
    return jnp.dot(left, right, preferred_element_type=F32)


def mm_nt(left, right):
    return lax.dot_general(left, right, (((1,), (1,)), ((), ())), preferred_element_type=F32)


def fine_taps(value):
    half = value.shape[0] // 2
    even, odd = value[:half], value[half:]
    return jnp.concatenate([from_left(odd), value, from_right(even)], axis=0).astype(BF16)


def coarse_taps(value):
    return jnp.concatenate([from_left(value), value, from_right(value)], axis=0).astype(BF16)


def fine_untap(taps):
    size = taps.shape[0] // 4
    even = taps[size : 2 * size] + from_left(taps[3 * size :])
    odd = taps[2 * size : 3 * size] + from_right(taps[:size])
    return jnp.concatenate([even, odd], axis=0)


def coarse_untap(taps):
    size = taps.shape[0] // 3
    return taps[size : 2 * size] + from_right(taps[:size]) + from_left(taps[2 * size :])


def spread(parts, first, last):
    out = {}
    for i in range(first, last + 1):
        size = parts[i - 1].shape[0] // 3
        out[i] = parts[i - 1][:size] + parts[i][size : 2 * size] + parts[i + 1][2 * size :]
    return out


def stack_rows(g, r):
    return jnp.concatenate([g[r + 1], g[r], g[r - 1]], axis=0)


def same_group(size, fine):
    left = lax.broadcasted_iota(jnp.int32, (size, size), 0)
    right = lax.broadcasted_iota(jnp.int32, (size, size), 1)
    if fine:
        half = size // 2
        left, right = left % half, right % half
        per = half // GROUPS
    else:
        per = size // GROUPS
    return left // per == right // per


def total_stats(stats):
    total = stats.spot[0]
    for index in range(1, stats.shape[0]):
        total = total + stats.spot[index]
    return total


def group_sums(stats, fine):
    total = total_stats(stats)
    member = same_group(128, fine)
    first = jnp.sum(jnp.where(member, total[0:1, :], 0.0), axis=1, keepdims=True)
    second = jnp.sum(jnp.where(member, total[1:2, :], 0.0), axis=1, keepdims=True)
    return first, second


def norm_columns(stats_ref, fine, members):
    first, second = group_sums(stats_ref, fine)
    mean = first / members
    inverse = lax.rsqrt(second / members - mean * mean + eps_norm)
    return mean, inverse


def back_columns(stats_ref, fine, members):
    first, second = group_sums(stats_ref, fine)
    return first / members, second / members


def to_row(column):
    size = column.shape[0]
    diagonal = lax.broadcasted_iota(jnp.int32, (size, size), 0) == lax.broadcasted_iota(
        jnp.int32, (size, size), 1
    )
    return jnp.sum(jnp.where(diagonal, column, 0.0), axis=0, keepdims=True)


def put_stats(ref, first, second, third=None):
    first = to_row(jnp.sum(first, axis=1, keepdims=True))
    second = to_row(jnp.sum(second, axis=1, keepdims=True))
    if third is None:
        third = jnp.zeros((1, 128), F32)
    block = jnp.concatenate([first, second, third, jnp.zeros((5, 128), F32)], axis=0)
    for index in range(ref.shape[0]):
        ref.spot[index] = block
    ref.finish()


def silu(h):
    return h * (1.0 / (1.0 + jnp.exp(-h)))


def silu_slope(h):
    s = 1.0 / (1.0 + jnp.exp(-h))
    return s * (1.0 + h * (1.0 - s))


def masked(value, index, rows, scal):
    if index < 0:
        return value * scal[6]
    if index >= rows:
        return value * scal[7]
    return value


def pick(scal, when_odd, when_even):
    return jnp.where(scal[8] > 0.5, when_odd, when_even)


def spill(ref, value):
    for t in range(4):
        ref[t, : value.shape[0], :] = value[:, 128 * t : 128 * (t + 1)]


def strided(ref, index, size):
    return jnp.concatenate(
        [ref[t, pl.ds(index, size, stride=ROWS), :] for t in range(4)], axis=1
    )


def interleave(transposed):
    left = lax.broadcasted_iota(jnp.int32, (512, 512), 0)
    right = lax.broadcasted_iota(jnp.int32, (512, 512), 1)
    if transposed:
        left, right = right, left
    place = (left & 1) * HALF + (left >> 1)
    return jnp.where(place == right, 1.0, 0.0).astype(BF16)


def fine_grad(blocks, outs, ins):
    parts = []
    for a in range(3):
        even = blocks[(2 * a) * outs : (2 * a + 1) * outs]
        odd = blocks[(2 * a + 1) * outs : (2 * a + 2) * outs]
        parts.append(even[:, : 3 * ins] + odd[:, ins : 4 * ins])
    return parts


def grad_blocks(parts, ins):
    if ins == 128:
        return [part[:, 128 * b : 128 * (b + 1)] for part in parts for b in range(3)]
    if ins == 64:
        blank = jnp.zeros(parts[0][:, :64].shape, F32)
        blocks = [part[:, :128] for part in parts]
        blocks.append(jnp.concatenate([parts[0][:, 128:192], parts[1][:, 128:192]], axis=1))
        blocks.append(jnp.concatenate([parts[2][:, 128:192], blank], axis=1))
        return blocks
    return parts


def put_grad(ref, start, blocks, split=True):
    count = ref.shape[0]
    size = blocks[0].shape[0] // count if split else blocks[0].shape[0]
    for block in blocks:
        for f in range(count):
            piece = block[f * size : (f + 1) * size] if split else block
            ref.spot[f, start : start + size, :] = piece.astype(BF16)
        start += size
    return start


def clear_rest(ref, start):
    count, size, _ = ref.shape
    if start < size:
        for f in range(count):
            ref.spot[f, start:, :] = jnp.zeros((size - start, 128), BF16)


def place(width, target, offset):
    left = lax.broadcasted_iota(jnp.int32, (width, target), 0)
    right = lax.broadcasted_iota(jnp.int32, (width, target), 1)
    return jnp.where(left + offset == right, 1.0, 0.0).astype(BF16)


def flipped(value):
    size = value.shape[1]
    return mm_nt(place(size, size, 0), value).astype(BF16)


def tap_of(pieces, offset, index, size):
    each = size // len(pieces)
    start = offset + index * each
    return jnp.concatenate([piece[start : start + each, :] for piece in pieces], axis=0).astype(
        BF16
    )


def in_order(scal, pieces):
    if len(pieces) == 2:
        mine, other = whole(pieces[0]), whole(pieces[1])
        low = scal[9] > 0.5
        return [jnp.where(low, mine, other), jnp.where(low, other, mine)]
    return [whole(piece) for piece in pieces]


def fine_matrix(taps, slot):
    rows = []
    for a in range(3):
        total = None
        for b in range(3):
            spread_out = jnp.concatenate(
                [place(slot, 4 * slot, b * slot), place(slot, 4 * slot, (b + 1) * slot)], axis=1
            )
            term = mm(taps[3 * a + b][:, :slot], spread_out)
            total = term if total is None else total + term
        rows += [total[:, : 4 * slot], total[:, 4 * slot :]]
    return jnp.concatenate(rows, axis=0).astype(BF16)


def pack(widths, scal, *refs):
    shards, (out, scratch) = refs[: len(widths)], refs[-2:]
    scratch[...] = jnp.zeros(scratch.shape, F32)
    start = 0
    for shard, (taps, rows) in zip(shards, widths):
        if taps == 1:
            scratch[start : start + rows, : shard.shape[1]] = whole(shard)
            start += rows
        else:
            for t in range(taps):
                value = shard.spot[t]
                scratch[start : start + value.shape[0], : value.shape[1]] = value
                start += rows
    give(out, scratch[...].astype(BF16))


def prepare_first(embed_size, scal, vec, *refs):
    pieces, (win, wfirst, wfirst_t, shift) = refs[:-4], refs[-4:]
    count = len(pieces)
    pieces = in_order(scal, pieces)
    each = 9 * (64 // count)
    give(win, fine_matrix([tap_of(pieces, 0, t, 64) for t in range(9)], 32))
    first = fine_matrix([tap_of(pieces, each, t, 64) for t in range(9)], 64)
    give(wfirst, first)
    give(wfirst_t, flipped(first))
    line = mm(whole(vec), tap_of(pieces, 2 * each, 0, embed_size))[0:1, :64]
    both = jnp.concatenate([line, line], axis=1)
    diagonal = place(128, 128, 0).astype(F32)
    column = jnp.sum(diagonal * both, axis=1, keepdims=True)
    give(shift, jnp.broadcast_to(column, (128, 128)))


def prepare_rest(scal, *refs):
    pieces = refs[:-10]
    wsecond, wsecond_t, wdown, wdown_t, wcoarse, wcoarse_t, wup, wup_t, wout, wout_t = refs[-10:]
    count = len(pieces)
    pieces = in_order(scal, pieces)
    start = 0

    def taps_of(size):
        nonlocal start
        taps = [tap_of(pieces, start, t, size) for t in range(9)]
        start += 9 * (size // count)
        return taps

    def both(value, forward, backward):
        give(forward, value)
        give(backward, flipped(value))

    both(fine_matrix(taps_of(64), 64), wsecond, wsecond_t)
    taps = taps_of(128)
    rows = []
    for a in range(3):
        total = None
        for b in range(3):
            term = mm(taps[3 * a + b][:, :64], place(64, 256, 64 * b))
            total = term if total is None else total + term
        rows.append(total)
    both(jnp.concatenate(rows, axis=0)[:, :192].astype(BF16), wdown, wdown_t)
    taps = taps_of(128)
    rows = [jnp.concatenate(taps[3 * a : 3 * a + 3], axis=1) for a in range(3)]
    both(jnp.concatenate(rows, axis=0), wcoarse, wcoarse_t)
    taps = taps_of(64)
    rows = []
    blank = jnp.zeros((64, 128), BF16)
    for a in range(3):
        rows.append(jnp.concatenate(taps[3 * a : 3 * a + 3] + [blank], axis=1))
        rows.append(jnp.concatenate([blank] + taps[3 * a : 3 * a + 3], axis=1))
    both(jnp.concatenate(rows, axis=0), wup, wup_t)
    taps = []
    width = 64 // count
    for t in range(9):
        total = None
        for s in range(count):
            tap = pieces[s][start + 16 * t : start + 16 * (t + 1), :].astype(BF16)
            term = mm(tap[:, :width], place(width, 128, s * width))
            total = term if total is None else total + term
        taps.append(total.astype(BF16))
    both(fine_matrix(taps, 64), wout, wout_t)


def enter(scal, target, condition, noise, own, edge_a, edge_b, line_a, line_b, scratch):
    sigma, skip, in_scale = scal[0], scal[1], scal[3]
    goal = whole(target)
    noisy = goal + sigma * whole(noise)
    q = skip * noisy - goal
    natural = jnp.concatenate([in_scale * noisy, whole(condition)], axis=0).astype(BF16)
    spill(scratch, mm(natural, interleave(False)))
    blank = jnp.zeros((8, 512), F32)
    for i in range(ROWS):
        value = strided(scratch, i, 24)
        own.spot[:, i * 512 : (i + 1) * 512] = jnp.concatenate([value, blank], axis=0).astype(BF16)
    top, low = own.spot[:, : FAR * 512], own.spot[:, (ROWS - FAR) * 512 :]
    give(edge_a, pick(scal, top, low))
    give(edge_b, pick(scal, low, top))
    own.finish()
    spill(scratch, q)
    blank = jnp.zeros((4, 512), F32)
    top = jnp.concatenate([strided(scratch, 0, 12), blank], axis=0)
    low = jnp.concatenate([strided(scratch, ROWS - 1, 12), blank], axis=0)
    give(line_a, pick(scal, top, low))
    give(line_b, pick(scal, low, top))


def stage_a(scal, win, got_a, got_b, own, act, stats, kept, above, below):
    above[...] = pick(scal, whole(got_a), whole(got_b))
    below[...] = pick(scal, whole(got_b), whole(got_a))
    weights = whole(win)
    parts = {}
    total = jnp.zeros((128, HALF), F32)
    square = jnp.zeros((128, HALF), F32)
    for r in range(-FAR, ROWS + FAR):
        if r < 0:
            value = above[:, (r + FAR) * 512 : (r + FAR + 1) * 512]
        elif r < ROWS:
            value = own.spot[:, r * 512 : (r + 1) * 512]
        else:
            value = below[:, (r - ROWS) * 512 : (r - ROWS + 1) * 512]
        value = value.astype(F32)
        z = fine_taps(jnp.concatenate([value[:, :HALF], value[:, HALF:]], axis=0))
        if -1 <= r <= ROWS:
            put(kept, r, z)
        parts[r] = mm(weights, z)
        i = r - 1
        if i > -FAR:
            value = spread(parts, i, i)[i]
            put(act, i, value)
            del parts[i - 1]
            if 0 <= i < ROWS:
                total = total + value
                square = square + value * value
    put_stats(stats, total, square)


def stage_b(members, scal, stats_a, shift, wfirst, act_a, act_b, stats, kept, hats, passed, sem):
    passing = pltpu.make_async_copy(act_a.spot.at[pl.ds(2, 16)], passed.spot, sem)
    passing.start()
    mean, inverse = norm_columns(stats_a, True, members)
    lift = shift.spot[:, 0:1]
    weights = whole(wfirst)
    parts = {}
    total = jnp.zeros((128, HALF), F32)
    square = jnp.zeros((128, HALF), F32)
    for r in range(-6, ROWS + 6):
        hat = (row(act_a, r) - mean) * inverse
        z = fine_taps(masked(silu(hat), r, ROWS, scal))
        if 0 <= r < ROWS:
            put(kept, r, z)
            put(hats, r, hat.astype(BF16))
        parts[r] = mm(weights, z)
        i = r - 1
        if i > -6:
            value = spread(parts, i, i)[i] + lift
            put(act_b, i, value)
            del parts[i - 1]
            if 0 <= i < ROWS:
                total = total + value
                square = square + value * value
    put_stats(stats, total, square)
    passing.wait()


def stage_c(
    members, scal, stats_b, wsecond, act_b, act_a, wdown,
    fine, act_c, edge, stats, kept, kept_pool, hats,
):
    mean, inverse = norm_columns(stats_b, True, members)
    weights = whole(wsecond)
    parts = {}
    pooled = {}
    half = {}
    for r in range(-5, ROWS + 5):
        hat = (row(act_b, r) - mean) * inverse
        z = fine_taps(masked(silu(hat), r, ROWS, scal))
        if 0 <= r < ROWS:
            put(kept, r, z)
        if -1 <= r <= ROWS:
            put(hats, r, hat.astype(BF16))
        parts[r] = mm(weights, z)
        i = r - 1
        if i > -5:
            value = spread(parts, i, i)[i] + row(act_a, i)
            if -3 <= i < ROWS + 3:
                put(fine, i, value)
            del parts[i - 1]
            half[i] = value[:64] + value[64:]
            if i % 2:
                value = 0.25 * (half.pop(i - 1) + half.pop(i))
                value = masked(value, i // 2, CROWS, scal)
                pooled[i // 2] = value.astype(BF16).astype(F32)
    weights = whole(wdown)
    parts = {}
    total = jnp.zeros((128, HALF), F32)
    square = jnp.zeros((128, HALF), F32)
    for r in range(-2, CROWS + 2):
        z = coarse_taps(pooled[r])
        if 0 <= r < CROWS:
            put(kept_pool, r, z)
        parts[r] = mm(weights, z)
        i = r - 1
        if i > -2:
            value = spread(parts, i, i)[i]
            put(act_c, i, value)
            del parts[i - 1]
            if 0 <= i < CROWS:
                total = total + value
                square = square + value * value
            if i in (1, 2):
                put(edge, i, value)
    put_stats(stats, total, square)


def stage_d(
    members, scal, stats_c, wcoarse, got_a, got_b, act_c, wup, fine,
    merged, hats, stats, kept_c, kept_up,
):
    mean, inverse = norm_columns(stats_c, False, members)
    ring = {}
    for j in range(2):
        ring[j - 3] = pick(scal, row(got_a, j), row(got_b, j))
        ring[CROWS + 1 + j] = pick(scal, row(got_b, j), row(got_a, j))
    for j in range(-1, CROWS + 1):
        ring[j] = row(act_c, j)
    weights = whole(wcoarse)
    parts = {}
    lifted = {}
    for r in range(-3, CROWS + 3):
        hat = (ring[r] - mean) * inverse
        z = coarse_taps(masked(silu(hat), r, CROWS, scal))
        if 0 <= r < CROWS:
            put(kept_c, r, z)
        if -2 <= r < CROWS + 2:
            put(hats, r, hat.astype(BF16))
        parts[r] = mm(weights, z)
        i = r - 1
        if i > -3:
            value = spread(parts, i, i)[i] + ring[i]
            del parts[i - 1]
            lifted[i] = masked(value, i, CROWS, scal).astype(BF16).astype(F32)
    weights = whole(wup)
    parts = {}
    total = jnp.zeros((128, HALF), F32)
    square = jnp.zeros((128, HALF), F32)
    for r in range(-2, CROWS + 2):
        z = coarse_taps(lifted[r])
        if 0 <= r < CROWS:
            put(kept_up, r, z)
        four = jnp.concatenate([z[:128], z[128:256], z[128:256], z[256:]], axis=0)
        parts[2 * r] = parts[2 * r + 1] = mm(weights, four)
        for i in (2 * r - 1, 2 * r):
            if i >= -3:
                value = spread(parts, i, i)[i] + row(fine, i)
                put(merged, i, value)
                parts.pop(i - 1)
                if 0 <= i < ROWS:
                    total = total + value
                    square = square + value * value
    put_stats(stats, total, square)


def stage_out(
    members, scal, stats_d, wout, merged, line_a, line_b, target, noise, wout_t,
    denoised, back, edge_a, edge_b, stats, grad, hats, pairs, cells, gs, zs,
    goals, noisies, found,
):
    sigma, skip, out_scale, weight, coef = scal[0], scal[1], scal[2], scal[4], scal[5]
    mean, inverse = norm_columns(stats_d, True, members)
    weights = whole(wout)
    parts = {}
    hat_of = {}
    for r in range(-3, ROWS + 3):
        hat = (row(merged, r) - mean) * inverse
        put(hats, r, hat.astype(BF16))
        if r == -3 or r == ROWS + 2:
            continue
        z = fine_taps(masked(silu(hat), r, ROWS, scal))
        if 0 <= r < ROWS:
            put(zs, r, z)
        parts[r] = mm(weights, z)
        i = r - 1
        if i > -2:
            value = spread(parts, i, i)[i]
            del parts[i - 1]
            pairs[16 * (i + 1) : 16 * (i + 2), :] = jnp.concatenate(
                [value[:16], value[16:]], axis=1
            )
    value = pairs[...]
    high = value.astype(BF16)
    low = (value - high.astype(F32)).astype(BF16)
    back_order = interleave(True)
    pairs[...] = mm(high, back_order) + mm(low, back_order)
    blank = jnp.zeros((4, 512), F32)
    loss_sum = jnp.zeros((12, 512), F32)
    top = pick(scal, whole(line_a), whole(line_b)) + out_scale * pairs[0:16, :]
    cells[0:16, :] = coef * scal[6] * top
    low = pick(scal, whole(line_b), whole(line_a)) + out_scale * pairs[16 * (ROWS + 1) :, :]
    cells[16 * (ROWS + 1) :, :] = coef * scal[7] * low
    spill(goals, whole(target))
    spill(noisies, whole(target) + sigma * whole(noise))
    for i in range(ROWS):
        goal = strided(goals, i, 12)
        noisy = strided(noisies, i, 12)
        estimate = skip * noisy + out_scale * pairs[16 * (i + 1) : 16 * (i + 1) + 12, :]
        for t in range(4):
            found[t, pl.ds(i, 12, stride=ROWS), :] = estimate[:, 128 * t : 128 * (t + 1)]
        mismatch = estimate - goal
        loss_sum = loss_sum + weight * mismatch * mismatch
        cells[16 * (i + 1) : 16 * (i + 2), :] = jnp.concatenate([coef * mismatch, blank], axis=0)
    give(denoised, jnp.concatenate([found[t] for t in range(4)], axis=1))
    loss_sum = jnp.broadcast_to(
        jnp.sum(jnp.sum(loss_sum, axis=1, keepdims=True), axis=0, keepdims=True), (1, 128)
    )
    pairs[...] = mm(cells[...].astype(BF16), interleave(False))
    g = {}
    for i in range(-1, ROWS + 1):
        value = pairs[16 * (i + 1) : 16 * (i + 2), :]
        g[i] = jnp.concatenate([value[:, :HALF], value[:, HALF:]], axis=0).astype(BF16)
    weights = whole(wout_t)
    total = jnp.zeros((128, HALF), F32)
    cross = jnp.zeros((128, HALF), F32)
    for r in range(ROWS):
        rows = stack_rows(g, r)
        put(gs, r, rows)
        value = fine_untap(mm(weights, rows))
        put(back, r, value.astype(BF16))
        hat = row(hats, r).astype(F32)
        e = value * silu_slope(hat)
        total = total + e
        cross = cross + e * hat
    for j in range(3):
        top, low = row(back, j), row(back, ROWS - 3 + j)
        put(edge_a, j, pick(scal, top, low))
        put(edge_b, j, pick(scal, low, top))
    put_stats(stats, total, cross, loss_sum)
    parts = fine_grad(mm_nt(gs[...], zs[...]), 16, 64)
    put_grad(grad, 0, grad_blocks(parts, 64), split=False)


def stage_up(
    members, members_c, scal, stats_d, stats_ed, got_a, got_b, hats, back, wup_t, stats_c, hats_c,
    wcoarse_t, kept_up, kept_c, grad_out,
    grad_merged, back_c, grad_coarse, edge_a, edge_b, stats, loss, grads, gs, zs, gc,
):
    give(loss, jnp.broadcast_to(total_stats(stats_ed)[2:3, :], (8, 128)))
    mean, inverse = norm_columns(stats_d, True, members)
    shift, slope = back_columns(stats_ed, True, members)
    g = {}
    for r in range(-3, ROWS + 3):
        hat = row(hats, r).astype(F32)
        if r < 0:
            u = pick(scal, row(got_a, r + 3), row(got_b, r + 3)).astype(F32)
        elif r < ROWS:
            u = row(back, r).astype(F32)
        else:
            u = pick(scal, row(got_b, r - ROWS), row(got_a, r - ROWS)).astype(F32)
        value = inverse * (u * silu_slope(hat) - shift - hat * slope)
        g[r] = masked(value, r, ROWS, scal).astype(BF16)
        if -2 <= r < ROWS + 2:
            put(grad_merged, r, g[r])
    weights = whole(wup_t)
    gk = {}
    half = {}
    for r in range(-2, ROWS + 2):
        rows = stack_rows(g, r)
        if 0 <= r < ROWS:
            put(gs, r, rows)
        taps = mm(weights, rows)
        half[r] = taps[128:256] + taps[256:384] + from_right(taps[:128]) + from_left(taps[384:])
        if r % 2:
            value = masked(half.pop(r - 1) + half.pop(r), r // 2, CROWS, scal)
            gk[r // 2] = value.astype(BF16)
            put(grad_coarse, r // 2, gk[r // 2])
    weights = whole(wcoarse_t)
    mean, inverse = norm_columns(stats_c, False, members_c)
    total = jnp.zeros((128, HALF), F32)
    cross = jnp.zeros((128, HALF), F32)
    for r in range(CROWS):
        rows = stack_rows(gk, r)
        put(gc, r, rows)
        value = coarse_untap(mm(weights, rows))
        put(back_c, r, value.astype(BF16))
        hat = row(hats_c, r).astype(F32)
        e = value * silu_slope(hat)
        total = total + e
        cross = cross + e * hat
    top = [row(back_c, 0), row(back_c, 1), gk[1]]
    low = [row(back_c, 2), row(back_c, 3), gk[2]]
    for j in range(3):
        put(edge_a, j, pick(scal, top[j], low[j]))
        put(edge_b, j, pick(scal, low[j], top[j]))
    put_stats(stats, total, cross)
    kept_up.wait(1)
    kept_c.wait(1)
    grad_out.wait(1)
    for r in range(ROWS):
        put(zs, r, row(kept_up, r // 2))
    blocks = mm_nt(gs[...], zs[...])
    parts = []
    for a in range(3):
        even = blocks[128 * a : 128 * a + 64]
        odd = blocks[128 * a + 64 : 128 * a + 128]
        parts.append(
            jnp.concatenate(
                [
                    even[:, :128] + odd[:, 128:256],
                    even[:, 128:256] + odd[:, 128:256],
                    even[:, 128:256] + odd[:, 256:],
                ],
                axis=1,
            )
        )
    start = put_grad(grads, 0, grad_blocks(parts, 128))
    blocks = mm_nt(gc[...], whole(kept_c))
    parts = [blocks[128 * a : 128 * (a + 1)] for a in range(3)]
    start = put_grad(grads, start, grad_blocks(parts, 128))
    for f in range(grads.shape[0]):
        grads.spot[f, start : start + 80, :] = grad_out.spot[f]
    clear_rest(grads, start + 80)


def stage_down(
    members, members_c, scal, stats_c, stats_ec, got_a, got_b, hats_c, back_c, grad_coarse,
    wdown_t, grad_merged, stats_b, wsecond_t, hats, kept_pool, kept_b,
    grad_fine, back_b, stats, grads, gs, gc,
):
    mean, inverse = norm_columns(stats_c, False, members_c)
    shift, slope = back_columns(stats_ec, False, members_c)
    g = {}
    for r in range(-2, CROWS + 2):
        hat = row(hats_c, r).astype(F32)
        if r < 0:
            u = pick(scal, row(got_a, r + 2), row(got_b, r + 2)).astype(F32)
        elif r < CROWS:
            u = row(back_c, r).astype(F32)
        else:
            u = pick(scal, row(got_b, r - CROWS), row(got_a, r - CROWS)).astype(F32)
        if r == -2:
            through = pick(scal, row(got_a, 2), row(got_b, 2)).astype(F32)
        elif r == CROWS + 1:
            through = pick(scal, row(got_b, 2), row(got_a, 2)).astype(F32)
        else:
            through = row(grad_coarse, r).astype(F32)
        value = through + inverse * (u * silu_slope(hat) - shift - hat * slope)
        g[r] = masked(value, r, CROWS, scal).astype(BF16)
    weights = whole(wdown_t)
    fine = {}
    for r in range(-1, CROWS + 1):
        rows = stack_rows(g, r)
        if 0 <= r < CROWS:
            put(gc, r, rows)
        value = 0.25 * coarse_untap(mm(weights, rows))
        both = jnp.concatenate([value, value], axis=0)
        for i in (2 * r, 2 * r + 1):
            value = masked(row(grad_merged, i).astype(F32) + both, i, ROWS, scal)
            fine[i] = value.astype(BF16)
            if 0 <= i < ROWS:
                put(grad_fine, i, fine[i])
    weights = whole(wsecond_t)
    mean, inverse = norm_columns(stats_b, True, members)
    total = jnp.zeros((128, HALF), F32)
    cross = jnp.zeros((128, HALF), F32)
    for r in range(-1, ROWS + 1):
        rows = stack_rows(fine, r)
        value = fine_untap(mm(weights, rows))
        put(back_b, r, value.astype(BF16))
        if 0 <= r < ROWS:
            put(gs, r, rows)
            hat = row(hats, r).astype(F32)
            e = value * silu_slope(hat)
            total = total + e
            cross = cross + e * hat
    put_stats(stats, total, cross)
    kept_pool.wait(1)
    kept_b.wait(1)
    blocks = mm_nt(gc[...], whole(kept_pool))
    parts = [blocks[128 * a : 128 * (a + 1)] for a in range(3)]
    start = put_grad(grads, 0, grad_blocks(parts, 64))
    parts = fine_grad(mm_nt(gs[...], whole(kept_b)), 64, 64)
    clear_rest(grads, put_grad(grads, start, grad_blocks(parts, 64)))


def stage_first(
    members, scal, stats_b, stats_eb, hats_b, back_b, wfirst_t, stats_a, hats, vec, kept_a,
    back_a, stats, grads, gs,
):
    mean, inverse = norm_columns(stats_b, True, members)
    shift, slope = back_columns(stats_eb, True, members)
    g = {}
    sums = jnp.zeros((128, HALF), F32)
    for r in range(-1, ROWS + 1):
        hat = row(hats_b, r).astype(F32)
        u = row(back_b, r).astype(F32)
        value = inverse * (u * silu_slope(hat) - shift - hat * slope)
        if 0 <= r < ROWS:
            sums = sums + value
        g[r] = masked(value, r, ROWS, scal).astype(BF16)
    weights = whole(wfirst_t)
    total = jnp.zeros((128, HALF), F32)
    cross = jnp.zeros((128, HALF), F32)
    for r in range(ROWS):
        rows = stack_rows(g, r)
        put(gs, r, rows)
        value = fine_untap(mm(weights, rows))
        put(back_a, r, value.astype(BF16))
        hat = row(hats, r).astype(F32)
        e = value * silu_slope(hat)
        total = total + e
        cross = cross + e * hat
    put_stats(stats, total, cross)
    kept_a.wait(1)
    parts = fine_grad(mm_nt(gs[...], whole(kept_a)), 64, 64)
    start = put_grad(grads, 0, grad_blocks(parts, 64))
    line = to_row(jnp.sum(sums, axis=1, keepdims=True))
    line = line + pltpu.roll(line, 64, 1)
    column = jnp.sum(place(128, 128, 0).astype(F32) * vec.spot[0:1, :].astype(F32), axis=1, keepdims=True)
    outer = (column * line).astype(BF16)
    size = 128 // grads.shape[0]
    for f in range(grads.shape[0]):
        grads.spot[f, start : start + size, :] = outer[f * size : (f + 1) * size]


def stage_last(
    members, scal, stats_a, stats_ea, hats, back_a, grad_fine, kept_in, early, middle, first,
    loss, loss_other, grads, loss_sum, gs, sems,
):
    copies, start = [], 0
    for index, ref in enumerate((early, middle)):
        rows = pl.ds(start, ref.shape[1])
        copies.append(
            pltpu.make_async_copy(ref.spot, grads.spot.at[:, rows, :], sems.at[index])
        )
        copies[index].start()
        start += ref.shape[1]
    give(loss_sum, whole(loss) + whole(loss_other))
    mean, inverse = norm_columns(stats_a, True, members)
    shift, slope = back_columns(stats_ea, True, members)
    for r in range(ROWS):
        hat = row(hats, r).astype(F32)
        u = row(back_a, r).astype(F32)
        value = row(grad_fine, r).astype(F32) + inverse * (
            u * silu_slope(hat) - shift - hat * slope
        )
        put(gs, r, value.astype(BF16))
    parts = []
    for a in range(3):
        blocks = mm_nt(gs[...], kept_in.spot[:, a * HALF : (a + ROWS) * HALF])
        parts.append(
            jnp.concatenate(
                [blocks[:64, :96] + blocks[64:, 32:128], jnp.zeros((64, 32), F32)], axis=1
            )
        )
    size = first.shape[1]
    for f in range(grads.shape[0]):
        grads.spot[f, start : start + size, :] = first.spot[f]
    clear_rest(grads, put_grad(grads, start + size, parts))
    for copy in copies:
        copy.wait()


def add_up(scal, got, out):
    total = got.spot[0].astype(F32)
    for index in range(1, got.shape[0]):
        total = total + got.spot[index].astype(F32)
    total = total.astype(BF16)
    for index in range(out.shape[0]):
        out.spot[index] = total


def unpack(starts, scal, got, *refs):
    first, down, second, coarse, up, out, embed, inputs, flat = refs
    size = got.shape[1]
    for index in range(got.shape[0]):
        flat[index * size : (index + 1) * size, :] = got.spot[index].astype(F32)

    def take(ref, start, out, size, ins):
        for t in range(9):
            a, b = t // 3, t % 3
            if ins == 128:
                at, lanes = t, 0
            elif ins == 64:
                at, lanes = (a, b) if b < 2 else (3 + a // 2, a % 2)
            else:
                at, lanes = a, b
            step = 32 if ins == 24 else ins
            value = ref[start + at * size : start + (at + 1) * size, :]
            rows = out.shape[1]
            out.spot[t] = value[:rows, lanes * step : lanes * step + ins]
        return start + (9 if ins == 128 else 5 if ins == 64 else 3) * size

    start = take(flat, 0, up, up.shape[1], 128)
    start = take(flat, start, coarse, coarse.shape[1], 128)
    take(flat, start, out, 16, 64)
    start = take(flat, starts[0], down, down.shape[1], 64)
    take(flat, start, second, second.shape[1], 64)
    start = take(flat, starts[1], first, first.shape[1], 64)
    size = embed.shape[0]
    give(embed, flat[start : start + size, :64])
    take(flat, start + size, inputs, inputs.shape[1], 24)


class Field:
    def __init__(self, array, first):
        self.array, self.first = array, first


class Saved:
    def __init__(self, item, low=None, high=None, when=0):
        self.item, self.low, self.high, self.when = item, low, high, when


def shape(*dims, dtype=F32):
    return jax.ShapeDtypeStruct(dims, dtype)


def rows_of(first, number, dtype=F32):
    return Field(shape(number, 128, HALF, dtype=dtype), first)


def flat_rows(first, number, channels):
    return Field(shape(channels, number * HALF, dtype=BF16), first)


def opened(item):
    saved = item if isinstance(item, Saved) else None
    item = saved.item if saved else item
    if isinstance(item, Field):
        return saved, item.array, item.first
    return saved, item, 0


def run(name, kernel, outs, scal, *operands, scratch=()):
    vmem, hbm = pl.BlockSpec(memory_space=pltpu.VMEM), pl.BlockSpec(memory_space=pltpu.HBM)
    in_specs, arrays, plans, spots = [pl.BlockSpec(memory_space=pltpu.SMEM)], [scal], [], []
    for item in operands:
        saved, item, first = opened(item)
        if saved is None:
            in_specs.append(vmem)
            arrays.append(item)
            plans.append((first, None, None))
            continue
        part = None
        dims = item.shape
        if saved.low is not None:
            part = pl.ds(saved.low - first, saved.high - saved.low)
            dims = (saved.high - saved.low,) + dims[1:]
            first = saved.low
        in_specs.append(hbm)
        arrays.append(pltpu.with_memory_space_constraint(item, pltpu.HBM))
        if saved.when is None:
            plans.append((first, None, None))
            continue
        plans.append((first, (saved.when, part), len(spots)))
        spots.append(pltpu.VMEM(dims, item.dtype))
    ins = len(operands)
    out_specs, out_shapes = [], []
    for item in outs:
        saved, item, first = opened(item)
        if saved is None:
            out_specs.append(vmem)
            out_shapes.append(item)
            plans.append((first, None, None))
            continue
        out_specs.append(hbm)
        out_shapes.append(pltpu.HBM(item.shape, item.dtype))
        last = None
        if isinstance(saved.item, Field):
            count = item.shape[0] if len(item.shape) == 3 else item.shape[1] // HALF
            last = first + count - 1
        if saved.when is None:
            plans.append((first, None, None))
            continue
        plans.append((first, (last, None), len(spots)))
        spots.append(pltpu.VMEM(item.shape, item.dtype))

    def body(numbers, *refs):
        given, refs = refs[: len(plans)], refs[len(plans) :]
        held, refs = refs[: len(spots)], refs[len(spots) :]
        sems, extra = refs[0], refs[1:]
        wrapped = []
        for index, (ref, (first, plan, place_at)) in enumerate(zip(given, plans)):
            copies = []
            if plan is not None:
                where = held[place_at]
                when, part = plan
                if index < ins:
                    source = ref if part is None else ref.at[part]
                    copies.append((when, pltpu.make_async_copy(source, where, sems.at[place_at])))
                else:
                    copies.append((when, pltpu.make_async_copy(where, ref, sems.at[place_at])))
                ref = where
            wrapped.append((Source if index < ins else Sink)(ref, copies, first))
        for item in wrapped[:ins]:
            item.wait(0)
        kernel(numbers, *wrapped, *extra)
        for item in wrapped[ins:]:
            item.finish()
        for item in wrapped[ins:]:
            for copy in item.started:
                copy.wait()

    made = pl.pallas_call(
        body,
        out_shape=tuple(out_shapes),
        in_specs=in_specs,
        out_specs=tuple(out_specs),
        scratch_shapes=spots
        + [pltpu.SemaphoreType.DMA((max(len(spots), 1),))]
        + [pltpu.VMEM(*item) if isinstance(item, tuple) else item for item in scratch],
        compiler_params=pltpu.CompilerParams(vmem_limit_bytes=LIMIT),
        name=name,
    )(*arrays)
    results = []
    for array, item in zip(made, outs):
        item = item.item if isinstance(item, Saved) else item
        results.append(Field(array, item.first) if isinstance(item, Field) else array)
    return results


def sum_parts(stats):
    return lax.all_to_all(stats, "rows", 0, 0)


def swap(value_a, value_b):
    count = lax.axis_size("rows")
    pairs = [(i, i ^ 1) for i in range(count)]
    across = []
    for i in range(1, count - 1, 2):
        across += [(i, i + 1), (i + 1, i)]
    return lax.ppermute(value_a, "rows", pairs), lax.ppermute(value_b, "rows", across)


def gather_packed(packed):
    if lax.axis_size("fsdp") == 2:
        return [packed, lax.ppermute(packed, "fsdp", [(0, 1), (1, 0)])]
    whole = lax.all_gather(packed, "fsdp").astype(F32)
    return [whole[i] for i in range(whole.shape[0])]


def group_shape(rows, count):
    return shape(count, -(-rows // 16) * 16, 128, dtype=BF16)


def per_device(
    residual_target,
    conditioning,
    noise_sample,
    noise_level,
    input_kernel,
    first_kernel,
    second_kernel,
    down_kernel,
    coarse_kernel,
    upward_kernel,
    output_kernel,
    embed_matrix,
):
    bands, count = lax.axis_size("rows"), lax.axis_size("fsdp")
    members = 2 * ROWS * 2 * HALF * bands
    members_c = 4 * CROWS * HALF * bands
    members_all = count * residual_target.size * bands
    me = lax.axis_index("rows")
    sigma_level, skip_scale, out_scale, in_scale, weight = preconditions(noise_level[0])
    coef = 2.0 * weight * out_scale / members_all
    scal = jnp.stack(
        [
            sigma_level,
            skip_scale,
            out_scale,
            in_scale,
            weight,
            coef,
            (me > 0).astype(F32),
            (me < bands - 1).astype(F32),
            (me % 2).astype(F32),
            (lax.axis_index("fsdp") == 0).astype(F32),
        ]
    )
    embedded = embedding(sigma_level, embed_matrix.shape[0] * count)
    target = residual_target.reshape(12 * ROWS, 512)
    condition = conditioning.reshape(12 * ROWS, 512)
    noise = noise_sample.reshape(12 * ROWS, 512)

    def pack_all(name, shards, rows, *after):
        widths = tuple((9 if item.ndim == 3 else 1, size) for item, size in zip(shards, rows))
        total = sum(taps * size for taps, size in widths)
        (packed,) = run(
            name,
            functools.partial(pack, widths),
            [shape(total, 128, dtype=BF16)],
            scal,
            *[Saved(item) for item in shards],
            *after,
            scratch=[((total, 128), F32)],
        )
        return gather_packed(packed)

    fine_o, coarse_o = input_kernel.shape[1], down_kernel.shape[1]
    early = pack_all(
        "pack_first",
        [input_kernel, first_kernel, embed_matrix],
        [fine_o, fine_o, embed_matrix.shape[0]],
    )
    far = shape(32, FAR * 512, dtype=BF16)
    own, edge_a, edge_b, line_a, line_b = run(
        "enter",
        enter,
        [shape(32, ROWS * 512, dtype=BF16), far, far, shape(16, 512), shape(16, 512)],
        scal,
        Saved(target),
        Saved(condition),
        Saved(noise),
        scratch=[((4, 192, 128), F32)],
    )
    got_a, got_b = swap(edge_a, edge_b)
    line_a, line_b = swap(line_a, line_b)
    vector = jnp.broadcast_to(embedded[None, :], (16, embedded.shape[0]))
    win, wfirst, wfirst_t, shift = run(
        "prepare_first",
        functools.partial(prepare_first, embedded.shape[0]),
        [
            shape(384, 128, dtype=BF16), Saved(shape(384, 256, dtype=BF16)),
            Saved(shape(256, 384, dtype=BF16)), shape(128, 128),
        ],
        scal,
        vector, *early,
    )
    stat = shape(bands, 8, 128)
    act_a, stats_a, kept_in = run(
        "stage_a",
        stage_a,
        [rows_of(-6, 20), stat, Saved(flat_rows(-1, 10, 128))],
        scal,
        win, got_a, got_b, own,
        scratch=[((32, FAR * 512), BF16), ((32, FAR * 512), BF16)],
    )
    rest = pack_all(
        "pack_rest",
        [second_kernel, down_kernel, coarse_kernel, upward_kernel, output_kernel],
        [fine_o, coarse_o, coarse_o, fine_o, 16],
        stats_a,
    )
    (
        wsecond, wsecond_t, wdown, wdown_t, wcoarse, wcoarse_t, wup, wup_t, wout, wout_t
    ) = run(
        "prepare_rest",
        prepare_rest,
        [
            Saved(shape(384, 256, dtype=BF16)), Saved(shape(256, 384, dtype=BF16)),
            Saved(shape(384, 192, dtype=BF16)), Saved(shape(192, 384, dtype=BF16)),
            Saved(shape(384, 384, dtype=BF16)), Saved(shape(384, 384, dtype=BF16)),
            Saved(shape(384, 512, dtype=BF16)), Saved(shape(512, 384, dtype=BF16)),
            Saved(shape(96, 256, dtype=BF16)), Saved(shape(256, 96, dtype=BF16)),
        ],
        scal,
        *rest,
    )

    stats_a = sum_parts(stats_a)
    act_b, stats_b, kept_a, hats_a, act_a = run(
        "stage_b",
        functools.partial(stage_b, members),
        [
            rows_of(-5, 18), stat, Saved(flat_rows(0, 8, 256)), Saved(rows_of(0, 8, BF16)),
            Saved(rows_of(-4, 16), when=None),
        ],
        scal,
        stats_a, shift, Saved(wfirst), act_a,
        scratch=[pltpu.SemaphoreType.DMA(())],
    )
    stats_b = sum_parts(stats_b)
    fine, act_c, edge, stats_c, kept_b, kept_pool, hats_b = run(
        "stage_c",
        functools.partial(stage_c, members),
        [
            rows_of(-3, 14), rows_of(-1, 6), Field(shape(128, 2 * HALF), 1), stat,
            Saved(flat_rows(0, 8, 256)), Saved(flat_rows(0, 4, 192)), Saved(rows_of(-1, 10, BF16)),
        ],
        scal,
        stats_b, Saved(wsecond), act_b, Saved(act_a), Saved(wdown),
    )
    got_a, got_b = swap(edge.array, edge.array)
    stats_c = sum_parts(stats_c)
    merged, hats_c, stats_d, kept_c, kept_up = run(
        "stage_d",
        functools.partial(stage_d, members_c),
        [
            rows_of(-3, 14), Saved(rows_of(-2, 8, BF16)), stat,
            Saved(flat_rows(0, 4, 384)), Saved(flat_rows(0, 4, 384)),
        ],
        scal,
        stats_c, Saved(wcoarse), got_a, got_b, act_c, Saved(wup), fine,
    )
    stats_d = sum_parts(stats_d)
    edge = Field(shape(128, 3 * HALF, dtype=BF16), 0)
    denoised, back_d, edge_a, edge_b, stats_ed, grad_out, hats_d = run(
        "stage_out",
        functools.partial(stage_out, members),
        [
            Saved(shape(96, 512)), rows_of(0, 8, BF16), edge, edge, stat,
            Saved(shape(count, 80, 128, dtype=BF16)), rows_of(-3, 14, BF16),
        ],
        scal,
        stats_d, Saved(wout), merged, Saved(line_a), Saved(line_b), Saved(target), Saved(noise),
        Saved(wout_t),
        scratch=[
            ((160, 512), F32), ((160, 512), F32), ((96, 8 * HALF), BF16), ((256, 8 * HALF), BF16),
            ((4, 96, 128), F32), ((4, 96, 128), F32), ((4, 96, 128), F32),
        ],
    )
    got_a, got_b = swap(edge_a.array, edge_b.array)
    stats_ed = sum_parts(stats_ed)
    grad_merged, back_c, grad_coarse, edge_a, edge_b, stats_ec, loss, early = run(
        "stage_up",
        functools.partial(stage_up, members, members_c),
        [
            rows_of(-2, 12, BF16), rows_of(0, 4, BF16), rows_of(-1, 6, BF16), edge, edge, stat,
            shape(8, 128), Saved(group_shape(9 * (fine_o + coarse_o) + 80, count)),
        ],
        scal,
        stats_d, stats_ed, got_a, got_b, hats_d, back_d, Saved(wup_t), stats_c, Saved(hats_c),
        Saved(wcoarse_t), Saved(kept_up, when=1), Saved(kept_c, when=1), Saved(grad_out, when=1),
        scratch=[
            ((384, 8 * HALF), BF16), ((384, 8 * HALF), BF16), ((384, 4 * HALF), BF16)
        ],
    )
    got_a, got_b = swap(edge_a.array, edge_b.array)
    stats_ec = sum_parts(stats_ec)
    if count == 2:
        loss_other = lax.ppermute(loss, "fsdp", [(0, 1), (1, 0)])
    else:
        loss_other = lax.psum(loss, "fsdp") - loss
    grad_fine, back_b, stats_eb, middle = run(
        "stage_down",
        functools.partial(stage_down, members, members_c),
        [
            Saved(rows_of(0, 8, BF16)), rows_of(-1, 10, BF16), stat,
            Saved(group_shape(5 * (fine_o + coarse_o), count)),
        ],
        scal,
        stats_c, stats_ec, got_a, got_b, Saved(hats_c), back_c, grad_coarse,
        Saved(wdown_t), grad_merged, stats_b, Saved(wsecond_t), Saved(hats_b, 0, 8),
        Saved(kept_pool, when=1), Saved(kept_b, when=1),
        scratch=[((384, 8 * HALF), BF16), ((384, 4 * HALF), BF16)],
    )
    stats_eb = sum_parts(stats_eb)
    back_a, stats_ea, grad_first = run(
        "stage_first",
        functools.partial(stage_first, members),
        [
            rows_of(0, 8, BF16), stat,
            Saved(shape(count, 5 * fine_o + embed_matrix.shape[0], 128, dtype=BF16)),
        ],
        scal,
        stats_b, stats_eb, Saved(hats_b), back_b, Saved(wfirst_t), stats_a, Saved(hats_a), vector,
        Saved(kept_a, when=1),
        scratch=[((384, 8 * HALF), BF16)],
    )
    stats_ea = sum_parts(stats_ea)
    late = group_shape(8 * fine_o + embed_matrix.shape[0], count)
    starts = [early.shape[1], early.shape[1] + middle.shape[1]]
    total = starts[1] + late.shape[1]
    chunk = -(-total // (16 * bands)) * 16
    grads, loss = run(
        "stage_last",
        functools.partial(stage_last, members),
        [shape(count, chunk * bands, 128, dtype=BF16), shape(8, 128)],
        scal,
        stats_a, stats_ea, Saved(hats_a), back_a, Saved(grad_fine), Saved(kept_in),
        Saved(early, when=None), Saved(middle, when=None), Saved(grad_first), loss, loss_other,
        scratch=[((128, 8 * HALF), BF16), pltpu.SemaphoreType.DMA((2,))],
    )
    loss_value = loss[0, 0] / members_all
    got = lax.all_to_all(grads.reshape(count * bands, chunk, 128), ("fsdp", "rows"), 0, 0)
    (mine,) = run("add_up", add_up, [shape(bands, chunk, 128, dtype=BF16)], scal, got)
    got = lax.all_to_all(mine, "rows", 0, 0)
    first_g, down_g, second_g, coarse_g, up_g, out_g, embed_g, in_g = run(
        "unpack",
        functools.partial(unpack, starts),
        [
            shape(*first_kernel.shape),
            shape(*down_kernel.shape),
            shape(*second_kernel.shape),
            shape(*coarse_kernel.shape),
            shape(*upward_kernel.shape),
            shape(9, 12, 64),
            shape(*embed_matrix.shape),
            shape(*input_kernel.shape),
        ],
        scal,
        got,
        scratch=[((chunk * bands, 128), F32)],
    )
    width = output_kernel.shape[2]
    out_g = lax.dynamic_slice_in_dim(out_g, lax.axis_index("fsdp") * width, width, axis=2)
    return (
        denoised.reshape(residual_target.shape),
        loss_value,
        in_g,
        first_g,
        second_g,
        down_g,
        coarse_g,
        up_g,
        out_g,
        embed_g,
    )


def solution(mesh):
    in_specs = (
        P("fsdp", None, "rows", None),
        P("fsdp", None, "rows", None),
        P("fsdp", None, "rows", None),
        P("fsdp"),
        P(None, "fsdp", None),
        P(None, "fsdp", None),
        P(None, "fsdp", None),
        P(None, "fsdp", None),
        P(None, "fsdp", None),
        P(None, "fsdp", None),
        P(None, None, "fsdp"),
        P("fsdp", None),
    )
    out_specs = (
        P("fsdp", None, "rows", None),
        P(),
        P(None, "fsdp", None),
        P(None, "fsdp", None),
        P(None, "fsdp", None),
        P(None, "fsdp", None),
        P(None, "fsdp", None),
        P(None, "fsdp", None),
        P(None, None, "fsdp"),
        P("fsdp", None),
    )
    return jax.shard_map(
        per_device, mesh=mesh, in_specs=in_specs, out_specs=out_specs, check_vma=False
    )
```

profile of v0, /device:TPU:0, one launch (start us, length us, event | category | flops | bytes accessed | tf_op | source)
XLA Modules:
  0.0 209.5 jit_solution(18023407512530396626)
XLA Ops:
  1.6 2.1 enter.1
  4.8 1.7 copy.22.refs_0_
  8.1 2.6 %collective-permute-start = (bf16[640,128]{1,0:T(8,128)(2,1)S(1)}, bf16[640,128]{1,0:T(8,128)(2,1)S(1)}, u32[]{:S(2)}, u32[]{:S(2)}) collective-permute-start(bf16[640,128]{1,0:T(8,128)(2,1)S(1)} %pack_first.1.refs_1_), channel_id=1, source_target_pairs={{0,16},{16,0},{1,17},{17,1},{2,18},{18,2},{3,19},{19,3},{4,20},{20... | collective-permute-start | bytes 491528 | tf_op jit(solution)/shard_map/ppermute | solution.py:1076
  10.9 3.1 %collective-permute-done.refs_2_ = bf16[640,128]{1,0:T(8,128)(2,1)S(1)} collective-permute-done((bf16[640,128]{1,0:T(8,128)(2,1)S(1)}, bf16[640,128]{1,0:T(8,128)(2,1)S(1)}, u32[]{:S(2)}, u32[]{:S(2)}) %collective-permute-start) | collective-permute-done | bytes 163872 | tf_op jit(solution)/shard_map/ppermute | solution.py:1076
  14.0 1.9 prepare_first.1
  15.9 2.5 %stage_a.1 = (f32[20,128,256]{2,1,0:T(8,128)S(1)}, f32[16,8,128]{2,1,0:T(8,128)S(1)}, bf16[128,2560]{1,0:T(8,128)(2,1)}) custom-call(f32[10]{0:T(128)S(1)} %stack.52.numbers, bf16[384,128]{1,0:T(8,128)(2,1)S(1)} %get-tuple-element.81.refs_0_, bf16[32,3584]{1,0:T(8,128)(2,1)S(1)} %collective-permute-done.1.refs_1_, ...), custom_call_target="tpu_custom_call" | custom-call | tf_op jit(solution)/shard_map/stage_a/pallas_call | solution.py:1043
  18.3 1.9 pack_rest.1.refs_0_
  20.2 2.1 collective-permute-start.3
  22.3 15.3 %all_to_all.50.refs_0_.refs_5_ = f32[16,8,128]{2,1,0:T(8,128)S(1)} all-to-all(f32[16,8,128]{2,1,0:T(8,128)S(1)} %get-tuple-element.85.refs_5_), channel_id=1, replica_groups=mesh['fsdp'=2,'rows'=16] {'rows'}, dimensions={0} | all-to-all | bytes 131072 | tf_op jit(solution)/shard_map/all_to_all | solution.py:1062
  37.6 5.1 %stage_b.1 = (f32[18,128,256]{2,1,0:T(8,128)S(1)}, f32[16,8,128]{2,1,0:T(8,128)}, bf16[256,2048]{1,0:T(8,128)(2,1)}, bf16[8,128,256]{2,1,0:T(8,128)(2,1)}, f32[16,128,256]{2,1,0:T(8,128)}) custom-call(f32[10]{0:T(128)S(1)} %stack.52.numbers, f32[16,8,128]{2,1,0:T(8,128)S(1)} %all_to_all.50.refs_0_.refs_5_, f32[128,128]{1,0:T(8,128)S(1)} %get-tuple-element.86.refs_1_, ...), custom_call_target="tpu_custom_call" | custom-call | tf_op jit(solution)/shard_map/stage_b/pallas_call | solution.py:1043
  42.8 3.5 %all-to-all-start.1 = ((f32[16,8,128]{2,1,0:T(8,128)}), f32[16,8,128]{2,1,0:T(8,128)S(1)}, u32[]{:S(2)}, u32[]{:S(2)}) async-start(f32[16,8,128]{2,1,0:T(8,128)} %get-tuple-element.89), calls=%async_computation.1 | async-start | bytes 131072 | tf_op jit(solution)/shard_map/all_to_all | solution.py:1062
  46.3 3.1 %prepare_rest.1 = (bf16[384,256]{1,0:T(8,128)(2,1)}, bf16[256,384]{1,0:T(8,128)(2,1)}, bf16[384,192]{1,0:T(8,128)(2,1)}, bf16[192,384]{1,0:T(8,128)(2,1)}, bf16[...) custom-call(f32[10]{0:T(128)S(1)} %stack.52.numbers, ...), custom_call_target="tpu_custom_call" | custom-call | tf_op jit(solution)/shard_map/prepare_rest/pallas_call | solution.py:1043
  49.4 3.7 %all-to-all-done.1.refs_0_.refs_9_ = f32[16,8,128]{2,1,0:T(8,128)S(1)} async-done(((f32[16,8,128]{2,1,0:T(8,128)}), f32[16,8,128]{2,1,0:T(8,128)S(1)}, u32[]{:S(2)}, u32[]{:S(2)}) %all-to-all-start.1) | async-done | bytes 65568 | tf_op jit(solution)/shard_map/all_to_all | solution.py:1062
  53.1 6.0 %stage_c.1 = (f32[14,128,256]{2,1,0:T(8,128)S(1)}, f32[6,128,256]{2,1,0:T(8,128)S(1)}, f32[128,512]{1,0:T(8,128)S(1)}, f32[16,8,128]{2,1,0:T(8,128)S(1)}, bf16[2...) custom-call(f32[10]{0:T(128)S(1)} %stack.52.numbers, ...), custom_call_target="tpu_custom_call" | custom-call | tf_op jit(solution)/shard_map/stage_c/pallas_call | solution.py:1043
  61.3 9.9 %all_to_all.51.refs_0_.refs_7_ = f32[16,8,128]{2,1,0:T(8,128)S(1)} all-to-all(f32[16,8,128]{2,1,0:T(8,128)S(1)} %get-tuple-element.94), channel_id=1, replica_groups=mesh['fsdp'=2,'rows'=16] {'rows'}, dimensions={0} | all-to-all | bytes 131072 | tf_op jit(solution)/shard_map/all_to_all | solution.py:1062
  71.3 5.4 %stage_d.1 = (f32[14,128,256]{2,1,0:T(8,128)S(1)}, bf16[8,128,256]{2,1,0:T(8,128)(2,1)}, f32[16,8,128]{2,1,0:T(8,128)}, bf16[384,1024]{1,0:T(8,128)(2,1)}, bf16[384,1024]{1,0:T(8,128)(2,1)}) custom-call(f32[10]{0:T(128)S(1)} %stack.52.numbers, f32[16,8,128]{2,1,0:T(8,128)S(1)} %all_to_all.51.refs_0_.refs_7_, bf16[384,384]{1,0:T(8,128)(2,1)} %get-tuple-element.95.refs_1_, ...), custom_call_target="tpu_custom_call" | custom-call | tf_op jit(solution)/shard_map/stage_d/pallas_call | solution.py:1043
  76.7 3.5 %all-to-all-start.3 = ((f32[16,8,128]{2,1,0:T(8,128)}), f32[16,8,128]{2,1,0:T(8,128)S(1)}, u32[]{:S(2)}, u32[]{:S(2)}) async-start(f32[16,8,128]{2,1,0:T(8,128)} %get-tuple-element.100), calls=%async_computation.3 | async-start | bytes 131072 | tf_op jit(solution)/shard_map/all_to_all | solution.py:1062
  81.5 5.6 %all-to-all-done.3.refs_0_ = f32[16,8,128]{2,1,0:T(8,128)S(1)} async-done(((f32[16,8,128]{2,1,0:T(8,128)}), f32[16,8,128]{2,1,0:T(8,128)S(1)}, u32[]{:S(2)}, u32[]{:S(2)}) %all-to-all-start.3) | async-done | bytes 65568 | tf_op jit(solution)/shard_map/all_to_all | solution.py:1062
  87.1 5.1 %stage_out.1 = (f32[96,512]{1,0:T(8,128)}, bf16[8,128,256]{2,1,0:T(8,128)(2,1)S(1)}, bf16[128,768]{1,0:T(8,128)(2,1)S(1)}, bf16[128,768]{1,0:T(8,128)(2,1)S(1)},...) custom-call(f32[10]{0:T(128)S(1)} %stack.52.numbers, ...), custom_call_target="tpu_custom_call" | custom-call | tf_op jit(solution)/shard_map/stage_out/pallas_call | solution.py:1043
  92.9 14.5 %all_to_all.52.refs_1_ = f32[16,8,128]{2,1,0:T(8,128)S(1)} all-to-all(f32[16,8,128]{2,1,0:T(8,128)S(1)} %get-tuple-element.107), channel_id=1, replica_groups=mesh['fsdp'=2,'rows'=16] {'rows'}, dimensions={0} | all-to-all | bytes 131072 | tf_op jit(solution)/shard_map/all_to_all | solution.py:1062
  107.5 7.1 %stage_up.1 = (bf16[12,128,256]{2,1,0:T(8,128)(2,1)S(1)}, bf16[4,128,256]{2,1,0:T(8,128)(2,1)S(1)}, bf16[6,128,256]{2,1,0:T(8,128)(2,1)S(1)}, bf16[128,768]{1,0:...) custom-call(f32[10]{0:T(128)S(1)} %stack.52.numbers, ...), custom_call_target="tpu_custom_call" | custom-call | tf_op jit(solution)/shard_map/stage_up/pallas_call | solution.py:1043
  115.3 11.4 %all_to_all.53.refs_1_ = f32[16,8,128]{2,1,0:T(8,128)S(1)} all-to-all(f32[16,8,128]{2,1,0:T(8,128)S(1)} %get-tuple-element.118), channel_id=1, replica_groups=mesh['fsdp'=2,'rows'=16] {'rows'}, dimensions={0} | all-to-all | bytes 131072 | tf_op jit(solution)/shard_map/all_to_all | solution.py:1062
  126.8 5.6 %stage_down.1 = (bf16[8,128,256]{2,1,0:T(8,128)(2,1)}, bf16[10,128,256]{2,1,0:T(8,128)(2,1)S(1)}, f32[16,8,128]{2,1,0:T(8,128)S(1)}, bf16[2,480,128]{2,1,0:T(8,128)(2,1)}) custom-call(f32[10]{0:T(128)S(1)} %stack.52.numbers, f32[16,8,128]{2,1,0:T(8,128)S(1)} %all_to_all.51.refs_0_.refs_7_, f32[16,8,128]{2,1,0:T(8,128)S(1)} %all_to_all.53.refs_1_, ...), custom_call_target="tpu_custom_call" | custom-call | tf_op jit(solution)/shard_map/stage_down/pallas_call | solution.py:1043
  132.3 9.5 %all_to_all.54.refs_1_ = f32[16,8,128]{2,1,0:T(8,128)S(1)} all-to-all(f32[16,8,128]{2,1,0:T(8,128)S(1)} %get-tuple-element.129), channel_id=1, replica_groups=mesh['fsdp'=2,'rows'=16] {'rows'}, dimensions={0} | all-to-all | bytes 131072 | tf_op jit(solution)/shard_map/all_to_all | solution.py:1062
  141.8 5.5 %stage_first.1 = (bf16[8,128,256]{2,1,0:T(8,128)(2,1)S(1)}, f32[16,8,128]{2,1,0:T(8,128)}, bf16[2,224,128]{2,1,0:T(8,128)(2,1)}) custom-call(f32[10]{0:T(128)S(1)} %stack.52.numbers, f32[16,8,128]{2,1,0:T(8,128)S(1)} %all-to-all-done.1.refs_0_.refs_9_, f32[16,8,128]{2,1,0:T(8,128)S(1)} %all_to_all.54.refs_1_, ...), custom_call_target="tpu_custom_call" | custom-call | tf_op jit(solution)/shard_map/stage_first/pallas_call | solution.py:1043
  147.3 3.5 %all-to-all-start.7 = ((f32[16,8,128]{2,1,0:T(8,128)}), f32[16,8,128]{2,1,0:T(8,128)S(1)}, u32[]{:S(2)}, u32[]{:S(2)}) async-start(f32[16,8,128]{2,1,0:T(8,128)} %get-tuple-element.134), calls=%async_computation.7 | async-start | bytes 131072 | tf_op jit(solution)/shard_map/all_to_all | solution.py:1062
  151.4 3.1 %collective-permute-done.12.refs_10_ = f32[8,128]{1,0:T(8,128)S(1)} collective-permute-done((f32[8,128]{1,0:T(8,128)S(1)}, f32[8,128]{1,0:T(8,128)S(1)}, u32[]{:S(2)}, u32[]{:S(2)}) %collective-permute-start.12) | collective-permute-done | bytes 4128 | tf_op jit(solution)/shard_map/ppermute | solution.py:1271
  154.5 3.2 %all-to-all-done.7.refs_1_ = f32[16,8,128]{2,1,0:T(8,128)S(1)} async-done(((f32[16,8,128]{2,1,0:T(8,128)}), f32[16,8,128]{2,1,0:T(8,128)S(1)}, u32[]{:S(2)}, u32[]{:S(2)}) %all-to-all-start.7) | async-done | bytes 65568 | tf_op jit(solution)/shard_map/all_to_all | solution.py:1062
  157.7 3.2 %stage_last.1 = (bf16[2,1792,128]{2,1,0:T(8,128)(2,1)S(1)}, f32[8,128]{1,0:T(8,128)S(1)}) custom-call(f32[10]{0:T(128)S(1)} %stack.52.numbers, f32[16,8,128]{2,1,0:T(8,128)S(1)} %all_to_all.50.refs_0_.refs_5_, f32[16,8,128]{2,1,0:T(8,128)S(1)} %all-to-all-done.7.refs_1_, bf16[8,128,256]{2,1,0:T(8,128)(2,1)} %get-tuple-element.132.refs_6_.refs_2_, ...), custom_call_target="tpu_custom_call" | custom-call | tf_op jit(solution)/shard_map/stage_last/pallas_call | solution.py:1043
  160.9 26.1 %all_to_all.55.refs_0_ = bf16[32,112,128]{2,1,0:T(8,128)(2,1)S(1)} all-to-all(bf16[32,112,128]{2,1,0:T(8,128)(2,1)S(1)} %bitcast.11), channel_id=1, replica_groups=mesh['fsdp'=2,'rows'=16] {'fsdp','rows'}, dimensions={0} | all-to-all | bytes 1835008 | tf_op jit(solution)/shard_map/all_to_all | solution.py:1315
  188.5 3.6 %all-to-all-start.9 = ((bf16[16,112,128]{2,1,0:T(8,128)(2,1)}), bf16[16,112,128]{2,1,0:T(8,128)(2,1)S(1)}, u32[]{:S(2)}, u32[]{:S(2)}) async-start(bf16[16,112,128]{2,1,0:T(8,128)(2,1)} %add_up.1), calls=%async_computation.9 | async-start | bytes 917504 | tf_op jit(solution)/shard_map/all_to_all | solution.py:1317
  193.2 12.0 %all-to-all-done.9.refs_0_ = bf16[16,112,128]{2,1,0:T(8,128)(2,1)S(1)} async-done(((bf16[16,112,128]{2,1,0:T(8,128)(2,1)}), bf16[16,112,128]{2,1,0:T(8,128)(2,1)S(1)}, u32[]{:S(2)}, u32[]{:S(2)}) %all-to-all-start.9) | async-done | bytes 458784 | tf_op jit(solution)/shard_map/all_to_all | solution.py:1317
  (36 shorter events, 13.6 us)
Async XLA Ops:
  3.6 12.2 %collective-permute-start.1 = (bf16[32,3584]{1,0:T(8,128)(2,1)S(1)}, bf16[32,3584]{1,0:T(8,128)(2,1)S(1)}, u32[]{:S(2)}, u32[]{:S(2)}) collective-permute-start(bf16[32,3584]{1,0:T(8,128)(2,1)S(1)} %get-tuple-element.82), channel_id=1, source_target_pairs={{0,1},{1,0},{2,3},{3,2},{4,5},{5,4},{6,7},{7,6},{8,9},{9,8},{10,11... | collective-permute-start | bytes 688136 | tf_op jit(solution)/shard_map/ppermute | solution.py:1071
  4.1 11.7 %collective-permute-start.2 = (bf16[32,3584]{1,0:T(8,128)(2,1)S(1)}, bf16[32,3584]{1,0:T(8,128)(2,1)S(1)}, u32[]{:S(2)}, u32[]{:S(2)}) collective-permute-start(bf16[32,3584]{1,0:T(8,128)(2,1)S(1)} %get-tuple-element.83), channel_id=1, source_target_pairs={{1,2},{2,1},{3,4},{4,3},{5,6},{6,5},{7,8},{8,7},{9,10},{10,9},{11,... | collective-permute-start | bytes 688136 | tf_op jit(solution)/shard_map/ppermute | solution.py:1071
  8.1 5.9 %collective-permute-start = (bf16[640,128]{1,0:T(8,128)(2,1)S(1)}, bf16[640,128]{1,0:T(8,128)(2,1)S(1)}, u32[]{:S(2)}, u32[]{:S(2)}) collective-permute-start(bf16[640,128]{1,0:T(8,128)(2,1)S(1)} %pack_first.1.refs_1_), channel_id=1, source_target_pairs={{0,16},{16,0},{1,17},{17,1},{2,18},{18,2},{3,19},{19,3},{4,20},{20... | collective-permute-start | bytes 491528 | tf_op jit(solution)/shard_map/ppermute | solution.py:1076
  20.2 26.1 %collective-permute-start.3 = (bf16[1872,128]{1,0:T(8,128)(2,1)S(1)}, bf16[1872,128]{1,0:T(8,128)(2,1)S(1)}, u32[]{:S(2)}, u32[]{:S(2)}) collective-permute-start(bf16[1872,128]{1,0:T(8,128)(2,1)S(1)} %pack_rest.1.refs_0_), channel_id=1, source_target_pairs={{0,16},{16,0},{1,17},{17,1},{2,18},{18,2},{3,19},{19,3},{4,20},{20... | collective-permute-start | bytes 1437704 | tf_op jit(solution)/shard_map/ppermute | solution.py:1076
  42.8 10.4 %all-to-all-start.1 = ((f32[16,8,128]{2,1,0:T(8,128)}), f32[16,8,128]{2,1,0:T(8,128)S(1)}, u32[]{:S(2)}, u32[]{:S(2)}) async-start(f32[16,8,128]{2,1,0:T(8,128)} %get-tuple-element.89), calls=%async_computation.1 | async-start | bytes 131072 | tf_op jit(solution)/shard_map/all_to_all | solution.py:1062
  59.1 12.1 %collective-permute-start.5 = (f32[128,512]{1,0:T(8,128)S(1)}, f32[128,512]{1,0:T(8,128)S(1)}, u32[]{:S(2)}, u32[]{:S(2)}) collective-permute-start(f32[128,512]{1,0:T(8,128)S(1)} %get-tuple-element.96), channel_id=1, source_target_pairs={{1,2},{2,1},{3,4},{4,3},{5,6},{6,5},{7,8},{8,7},{9,10},{10,9},{11,... | collective-permute-start | bytes 786440 | tf_op jit(solution)/shard_map/ppermute | solution.py:1071
  59.8 11.5 %collective-permute-start.4 = (f32[128,512]{1,0:T(8,128)S(1)}, f32[128,512]{1,0:T(8,128)S(1)}, u32[]{:S(2)}, u32[]{:S(2)}) collective-permute-start(f32[128,512]{1,0:T(8,128)S(1)} %get-tuple-element.96), channel_id=1, source_target_pairs={{0,1},{1,0},{2,3},{3,2},{4,5},{5,4},{6,7},{7,6},{8,9},{9,8},{10,11... | collective-permute-start | bytes 786440 | tf_op jit(solution)/shard_map/ppermute | solution.py:1071
  76.7 10.4 %all-to-all-start.3 = ((f32[16,8,128]{2,1,0:T(8,128)}), f32[16,8,128]{2,1,0:T(8,128)S(1)}, u32[]{:S(2)}, u32[]{:S(2)}) async-start(f32[16,8,128]{2,1,0:T(8,128)} %get-tuple-element.100), calls=%async_computation.3 | async-start | bytes 131072 | tf_op jit(solution)/shard_map/all_to_all | solution.py:1062
  80.2 1.3 collective-permute-start.6
  80.5 1.0 collective-permute-start.7
  81.5 5.6 %copy-start = (f32[16,512]{1,0:T(8,128)}, f32[16,512]{1,0:T(8,128)S(1)}, u32[]{:S(2)}) copy-start(f32[16,512]{1,0:T(8,128)S(1)} %collective-permute-done.6.refs_3_) | copy-start | bytes 98308
  81.5 5.6 %copy-start.1 = (f32[16,512]{1,0:T(8,128)}, f32[16,512]{1,0:T(8,128)S(1)}, u32[]{:S(2)}) copy-start(f32[16,512]{1,0:T(8,128)S(1)} %collective-permute-done.7.refs_4_) | copy-start | bytes 98308
  92.1 15.3 %collective-permute-start.8 = (bf16[128,768]{1,0:T(8,128)(2,1)S(1)}, bf16[128,768]{1,0:T(8,128)(2,1)S(1)}, u32[]{:S(2)}, u32[]{:S(2)}) collective-permute-start(bf16[128,768]{1,0:T(8,128)(2,1)S(1)} %get-tuple-element.108), channel_id=1, source_target_pairs={{0,1},{1,0},{2,3},{3,2},{4,5},{5,4},{6,7},{7,6},{8,9},{9,8},{10,11... | collective-permute-start | bytes 589832 | tf_op jit(solution)/shard_map/ppermute | solution.py:1071
  92.2 15.2 %collective-permute-start.9 = (bf16[128,768]{1,0:T(8,128)(2,1)S(1)}, bf16[128,768]{1,0:T(8,128)(2,1)S(1)}, u32[]{:S(2)}, u32[]{:S(2)}) collective-permute-start(bf16[128,768]{1,0:T(8,128)(2,1)S(1)} %get-tuple-element.109), channel_id=1, source_target_pairs={{1,2},{2,1},{3,4},{4,3},{5,6},{6,5},{7,8},{8,7},{9,10},{10,9},{11,... | collective-permute-start | bytes 589832 | tf_op jit(solution)/shard_map/ppermute | solution.py:1071
  114.6 12.2 %collective-permute-start.10 = (bf16[128,768]{1,0:T(8,128)(2,1)S(1)}, bf16[128,768]{1,0:T(8,128)(2,1)S(1)}, u32[]{:S(2)}, u32[]{:S(2)}) collective-permute-start(bf16[128,768]{1,0:T(8,128)(2,1)S(1)} %get-tuple-element.119), channel_id=1, source_target_pairs={{0,1},{1,0},{2,3},{3,2},{4,5},{5,4},{6,7},{7,6},{8,9},{9,8},{10,11... | collective-permute-start | bytes 589832 | tf_op jit(solution)/shard_map/ppermute | solution.py:1071
  114.6 12.1 %collective-permute-start.11 = (bf16[128,768]{1,0:T(8,128)(2,1)S(1)}, bf16[128,768]{1,0:T(8,128)(2,1)S(1)}, u32[]{:S(2)}, u32[]{:S(2)}) collective-permute-start(bf16[128,768]{1,0:T(8,128)(2,1)S(1)} %get-tuple-element.120), channel_id=1, source_target_pairs={{1,2},{2,1},{3,4},{4,3},{5,6},{6,5},{7,8},{8,7},{9,10},{10,9},{11,... | collective-permute-start | bytes 589832 | tf_op jit(solution)/shard_map/ppermute | solution.py:1071
  147.3 10.4 %all-to-all-start.7 = ((f32[16,8,128]{2,1,0:T(8,128)}), f32[16,8,128]{2,1,0:T(8,128)S(1)}, u32[]{:S(2)}, u32[]{:S(2)}) async-start(f32[16,8,128]{2,1,0:T(8,128)} %get-tuple-element.134), calls=%async_computation.7 | async-start | bytes 131072 | tf_op jit(solution)/shard_map/all_to_all | solution.py:1062
  150.8 3.7 %collective-permute-start.12 = (f32[8,128]{1,0:T(8,128)S(1)}, f32[8,128]{1,0:T(8,128)S(1)}, u32[]{:S(2)}, u32[]{:S(2)}) collective-permute-start(f32[8,128]{1,0:T(8,128)S(1)} %get-tuple-element.141.refs_9_), channel_id=1, source_target_pairs={{0,16},{16,0},{1,17},{17,1},{2,18},{18,2},{3,19},{19,3},{4,20},{20... | collective-permute-start | bytes 12296 | tf_op jit(solution)/shard_map/ppermute | solution.py:1271
  188.5 16.8 %all-to-all-start.9 = ((bf16[16,112,128]{2,1,0:T(8,128)(2,1)}), bf16[16,112,128]{2,1,0:T(8,128)(2,1)S(1)}, u32[]{:S(2)}, u32[]{:S(2)}) async-start(bf16[16,112,128]{2,1,0:T(8,128)(2,1)} %add_up.1), calls=%async_computation.9 | async-start | bytes 917504 | tf_op jit(solution)/shard_map/all_to_all | solution.py:1317
where the time goes:
time: 211 us; the launch traced here: 209 us
  blocking collectives  86.8 us (41%)
  Pallas kernels  59 us (28%)
  waiting for transfers between devices  31.1 us (15%)
  starting transfers between devices  25.2 us (12%)
  local copies, waits for them, and re-layouts  3.75 us (2%)
  between operations  3.57 us (2%)
    all_to_all x5, blocking collectives, sum_parts(): return lax.all_to_all(stats, 'rows', 0, 0)  60.7 us
    pallas_call x16, Pallas kernels, run(): pl.pallas_call(body, out_shape=tuple(out_shapes), in_specs=in_specs, out_...  59 us
    all_to_all x1, blocking collectives, per_device(): lax.all_to_all(grads.reshape(count * bands, chunk, 128), ('fsdp', 'rows')...  26.1 us
    all_to_all x3, waiting for transfers between devices, sum_parts(): return lax.all_to_all(stats, 'rows', 0, 0)  12.5 us
    all_to_all x1, waiting for transfers between devices, per_device(): got = lax.all_to_all(mine, 'rows', 0, 0)  12 us
    all_to_all x3, starting transfers between devices, sum_parts(): return lax.all_to_all(stats, 'rows', 0, 0)  10.5 us
    ppermute x2, starting transfers between devices, gather_packed(): return [packed, lax.ppermute(packed, 'fsdp', [(0, 1), (1, 0)])]  4.67 us
  transfers between devices with their start and end apart: 17, of which 7 were waited for; matrix products, arithmetic and copies ran while one was open for 1% of the time, Pallas kernels for 6%

commit v1 on v0

--- a/solution.py
+++ b/solution.py
@@ -220,11 +220,12 @@
 
 
 def silu(h):
-    return h * (1.0 / (1.0 + jnp.exp(-h)))
+    t = 0.5 * h
+    return t + t * jnp.tanh(t)
 
 
 def silu_slope(h):
-    s = 1.0 / (1.0 + jnp.exp(-h))
+    s = 0.5 + 0.5 * jnp.tanh(0.5 * h)
     return s * (1.0 + h * (1.0 - s))
 
 
@@ -344,13 +345,15 @@
     shards, (out, scratch) = refs[: len(widths)], refs[-2:]
     scratch[...] = jnp.zeros(scratch.shape, F32)
     start = 0
-    for shard, (taps, rows) in zip(shards, widths):
+    for shard, (taps, rows, swapped) in zip(shards, widths):
         if taps == 1:
             scratch[start : start + rows, : shard.shape[1]] = whole(shard)
             start += rows
         else:
             for t in range(taps):
                 value = shard.spot[t]
+                if swapped:
+                    value = mm_nt(place(value.shape[1], value.shape[1], 0), value.astype(BF16))
                 scratch[start : start + value.shape[0], : value.shape[1]] = value
                 start += rows
     give(out, scratch[...].astype(BF16))
@@ -421,7 +424,7 @@
     both(fine_matrix(taps, 64), wout, wout_t)
 
 
-def enter(scal, target, condition, noise, own, edge_a, edge_b, line_a, line_b, scratch):
+def enter(scal, target, condition, noise, done, own, edge_a, edge_b, scratch, marks):
     sigma, skip, in_scale = scal[0], scal[1], scal[3]
     goal = whole(target)
     noisy = goal + sigma * whole(noise)
@@ -432,21 +435,47 @@
     for i in range(ROWS):
         value = strided(scratch, i, 24)
         own.spot[:, i * 512 : (i + 1) * 512] = jnp.concatenate([value, blank], axis=0).astype(BF16)
-    top, low = own.spot[:, : FAR * 512], own.spot[:, (ROWS - FAR) * 512 :]
-    give(edge_a, pick(scal, top, low))
-    give(edge_b, pick(scal, low, top))
-    own.finish()
     spill(scratch, q)
     blank = jnp.zeros((4, 512), F32)
-    top = jnp.concatenate([strided(scratch, 0, 12), blank], axis=0)
-    low = jnp.concatenate([strided(scratch, ROWS - 1, 12), blank], axis=0)
-    give(line_a, pick(scal, top, low))
-    give(line_b, pick(scal, low, top))
-
-
-def stage_a(scal, win, got_a, got_b, own, act, stats, kept, above, below):
+    for j, i in enumerate((0, ROWS - 1)):
+        rest = jnp.concatenate([strided(scratch, i, 12), blank], axis=0)
+        marks[j] = jnp.zeros(marks.shape[1:], BF16)
+        for part in range(3):
+            piece = rest.astype(BF16)
+            rest = rest - piece.astype(F32)
+            for k in range(2):
+                lanes = slice((2 * part + k) * 512, (2 * part + k + 1) * 512)
+                marks[j, 8:, lanes] = piece[8 * k : 8 * k + 8]
+    for j, edge in enumerate((edge_a, edge_b)):
+        odd = scal[8] > 0.5 if j == 0 else scal[8] < 0.5
+        low = (ROWS - FAR) * 512
+        edge.spot[:16, :] = jnp.where(odd, own.spot[:16, : FAR * 512], own.spot[:16, low:])
+        edge.spot[16:, :] = jnp.where(odd, own.spot[16:, : FAR * 512], own.spot[16:, low:]) + (
+            jnp.where(odd, marks[0], marks[1])
+        )
+
+
+def marked(scal, got):
+    halves = []
+    for k in range(2):
+        total = None
+        for part in range(3):
+            lanes = slice((2 * part + k) * 512, (2 * part + k + 1) * 512)
+            piece = got.spot[16:32, lanes].astype(F32)[8:]
+            total = piece if total is None else total + piece
+        halves.append(total)
+    return jnp.concatenate(halves, axis=0)
+
+
+def stage_a(scal, win, got_a, got_b, own, done, act, stats, kept, line_a, line_b, above, below):
+    give(line_a, marked(scal, got_a))
+    give(line_b, marked(scal, got_b))
     above[...] = pick(scal, whole(got_a), whole(got_b))
     below[...] = pick(scal, whole(got_b), whole(got_a))
+    clear = jnp.zeros((16, FAR * 512), BF16)
+    keep = lax.broadcasted_iota(jnp.int32, (16, FAR * 512), 0) < 8
+    for ref in (above, below):
+        ref[16:, :] = jnp.where(keep, ref[16:, :], clear)
     weights = whole(win)
     parts = {}
     total = jnp.zeros((128, HALF), F32)
@@ -474,12 +503,12 @@
     put_stats(stats, total, square)
 
 
-def stage_b(members, scal, stats_a, shift, wfirst, act_a, act_b, stats, kept, hats, passed, sem):
+def stage_b(members, scal, stats_a, shift, wfirst, act_a, act_b, stats, kept, hats, passed, totals, sem):
+    give(totals, total_stats(stats_a)[None])
     passing = pltpu.make_async_copy(act_a.spot.at[pl.ds(2, 16)], passed.spot, sem)
     passing.start()
     mean, inverse = norm_columns(stats_a, True, members)
     lift = shift.spot[:, 0:1]
-    weights = whole(wfirst)
     parts = {}
     total = jnp.zeros((128, HALF), F32)
     square = jnp.zeros((128, HALF), F32)
@@ -489,7 +518,9 @@
         if 0 <= r < ROWS:
             put(kept, r, z)
             put(hats, r, hat.astype(BF16))
-        parts[r] = mm(weights, z)
+        if r == -6:
+            wfirst.wait(1)
+        parts[r] = mm(whole(wfirst), z)
         i = r - 1
         if i > -6:
             value = spread(parts, i, i)[i] + lift
@@ -504,10 +535,10 @@
 
 def stage_c(
     members, scal, stats_b, wsecond, act_b, act_a, wdown,
-    fine, act_c, edge, stats, kept, kept_pool, hats,
+    fine, act_c, edge, stats, kept, kept_pool, hats, totals,
 ):
+    give(totals, total_stats(stats_b)[None])
     mean, inverse = norm_columns(stats_b, True, members)
-    weights = whole(wsecond)
     parts = {}
     pooled = {}
     half = {}
@@ -518,7 +549,11 @@
             put(kept, r, z)
         if -1 <= r <= ROWS:
             put(hats, r, hat.astype(BF16))
-        parts[r] = mm(weights, z)
+        if r == -5:
+            wsecond.wait(1)
+        if r == -3:
+            act_a.wait(1)
+        parts[r] = mm(whole(wsecond), z)
         i = r - 1
         if i > -5:
             value = spread(parts, i, i)[i] + row(act_a, i)
@@ -530,6 +565,7 @@
                 value = 0.25 * (half.pop(i - 1) + half.pop(i))
                 value = masked(value, i // 2, CROWS, scal)
                 pooled[i // 2] = value.astype(BF16).astype(F32)
+    wdown.wait(1)
     weights = whole(wdown)
     parts = {}
     total = jnp.zeros((128, HALF), F32)
@@ -554,8 +590,9 @@
 
 def stage_d(
     members, scal, stats_c, wcoarse, got_a, got_b, act_c, wup, fine,
-    merged, hats, stats, kept_c, kept_up,
+    merged, hats, stats, kept_c, kept_up, totals,
 ):
+    give(totals, total_stats(stats_c)[None])
     mean, inverse = norm_columns(stats_c, False, members)
     ring = {}
     for j in range(2):
@@ -563,7 +600,6 @@
         ring[CROWS + 1 + j] = pick(scal, row(got_b, j), row(got_a, j))
     for j in range(-1, CROWS + 1):
         ring[j] = row(act_c, j)
-    weights = whole(wcoarse)
     parts = {}
     lifted = {}
     for r in range(-3, CROWS + 3):
@@ -573,12 +609,15 @@
             put(kept_c, r, z)
         if -2 <= r < CROWS + 2:
             put(hats, r, hat.astype(BF16))
-        parts[r] = mm(weights, z)
+        if r == -3:
+            wcoarse.wait(1)
+        parts[r] = mm(whole(wcoarse), z)
         i = r - 1
         if i > -3:
             value = spread(parts, i, i)[i] + ring[i]
             del parts[i - 1]
             lifted[i] = masked(value, i, CROWS, scal).astype(BF16).astype(F32)
+    wup.wait(1)
     weights = whole(wup)
     parts = {}
     total = jnp.zeros((128, HALF), F32)
@@ -602,14 +641,13 @@
 
 def stage_out(
     members, scal, stats_d, wout, merged, line_a, line_b, target, noise, wout_t,
-    denoised, back, edge_a, edge_b, stats, grad, hats, pairs, cells, gs, zs,
+    denoised, back, edge_a, edge_b, stats, hats, cotangents, zs, totals, pairs, cells,
     goals, noisies, found,
 ):
+    give(totals, total_stats(stats_d)[None])
     sigma, skip, out_scale, weight, coef = scal[0], scal[1], scal[2], scal[4], scal[5]
     mean, inverse = norm_columns(stats_d, True, members)
-    weights = whole(wout)
     parts = {}
-    hat_of = {}
     for r in range(-3, ROWS + 3):
         hat = (row(merged, r) - mean) * inverse
         put(hats, r, hat.astype(BF16))
@@ -618,7 +656,9 @@
         z = fine_taps(masked(silu(hat), r, ROWS, scal))
         if 0 <= r < ROWS:
             put(zs, r, z)
-        parts[r] = mm(weights, z)
+        if r == -2:
+            wout.wait(1)
+        parts[r] = mm(whole(wout), z)
         i = r - 1
         if i > -2:
             value = spread(parts, i, i)[i]
@@ -630,6 +670,8 @@
     high = value.astype(BF16)
     low = (value - high.astype(F32)).astype(BF16)
     back_order = interleave(True)
+    for item in (line_a, line_b, target, noise, wout_t):
+        item.wait(1)
     pairs[...] = mm(high, back_order) + mm(low, back_order)
     blank = jnp.zeros((4, 512), F32)
     loss_sum = jnp.zeros((12, 512), F32)
@@ -657,13 +699,12 @@
     for i in range(-1, ROWS + 1):
         value = pairs[16 * (i + 1) : 16 * (i + 2), :]
         g[i] = jnp.concatenate([value[:, :HALF], value[:, HALF:]], axis=0).astype(BF16)
+        put(cotangents, i, g[i])
     weights = whole(wout_t)
     total = jnp.zeros((128, HALF), F32)
     cross = jnp.zeros((128, HALF), F32)
     for r in range(ROWS):
-        rows = stack_rows(g, r)
-        put(gs, r, rows)
-        value = fine_untap(mm(weights, rows))
+        value = fine_untap(mm(weights, stack_rows(g, r)))
         put(back, r, value.astype(BF16))
         hat = row(hats, r).astype(F32)
         e = value * silu_slope(hat)
@@ -674,68 +715,24 @@
         put(edge_a, j, pick(scal, top, low))
         put(edge_b, j, pick(scal, low, top))
     put_stats(stats, total, cross, loss_sum)
-    parts = fine_grad(mm_nt(gs[...], zs[...]), 16, 64)
+
+
+def grads_out(scal, cotangents, zs, grad, gs):
+    g = {r: row(cotangents, r) for r in range(-1, ROWS + 1)}
+    for r in range(ROWS):
+        put(gs, r, stack_rows(g, r))
+    parts = fine_grad(mm_nt(gs[...], whole(zs)), 16, 64)
     put_grad(grad, 0, grad_blocks(parts, 64), split=False)
 
 
-def stage_up(
-    members, members_c, scal, stats_d, stats_ed, got_a, got_b, hats, back, wup_t, stats_c, hats_c,
-    wcoarse_t, kept_up, kept_c, grad_out,
-    grad_merged, back_c, grad_coarse, edge_a, edge_b, stats, loss, grads, gs, zs, gc,
-):
-    give(loss, jnp.broadcast_to(total_stats(stats_ed)[2:3, :], (8, 128)))
-    mean, inverse = norm_columns(stats_d, True, members)
-    shift, slope = back_columns(stats_ed, True, members)
-    g = {}
-    for r in range(-3, ROWS + 3):
-        hat = row(hats, r).astype(F32)
-        if r < 0:
-            u = pick(scal, row(got_a, r + 3), row(got_b, r + 3)).astype(F32)
-        elif r < ROWS:
-            u = row(back, r).astype(F32)
-        else:
-            u = pick(scal, row(got_b, r - ROWS), row(got_a, r - ROWS)).astype(F32)
-        value = inverse * (u * silu_slope(hat) - shift - hat * slope)
-        g[r] = masked(value, r, ROWS, scal).astype(BF16)
-        if -2 <= r < ROWS + 2:
-            put(grad_merged, r, g[r])
-    weights = whole(wup_t)
-    gk = {}
-    half = {}
-    for r in range(-2, ROWS + 2):
-        rows = stack_rows(g, r)
-        if 0 <= r < ROWS:
-            put(gs, r, rows)
-        taps = mm(weights, rows)
-        half[r] = taps[128:256] + taps[256:384] + from_right(taps[:128]) + from_left(taps[384:])
-        if r % 2:
-            value = masked(half.pop(r - 1) + half.pop(r), r // 2, CROWS, scal)
-            gk[r // 2] = value.astype(BF16)
-            put(grad_coarse, r // 2, gk[r // 2])
-    weights = whole(wcoarse_t)
-    mean, inverse = norm_columns(stats_c, False, members_c)
-    total = jnp.zeros((128, HALF), F32)
-    cross = jnp.zeros((128, HALF), F32)
+def grads_up(scal, grad_merged, grad_coarse, kept_up, kept_c, grad_out, grads, gs, zs, gc):
+    g = {r: row(grad_merged, r) for r in range(-1, ROWS + 1)}
+    for r in range(ROWS):
+        put(gs, r, stack_rows(g, r))
+        put(zs, r, row(kept_up, r // 2))
+    g = {r: row(grad_coarse, r) for r in range(-1, CROWS + 1)}
     for r in range(CROWS):
-        rows = stack_rows(gk, r)
-        put(gc, r, rows)
-        value = coarse_untap(mm(weights, rows))
-        put(back_c, r, value.astype(BF16))
-        hat = row(hats_c, r).astype(F32)
-        e = value * silu_slope(hat)
-        total = total + e
-        cross = cross + e * hat
-    top = [row(back_c, 0), row(back_c, 1), gk[1]]
-    low = [row(back_c, 2), row(back_c, 3), gk[2]]
-    for j in range(3):
-        put(edge_a, j, pick(scal, top[j], low[j]))
-        put(edge_b, j, pick(scal, low[j], top[j]))
-    put_stats(stats, total, cross)
-    kept_up.wait(1)
-    kept_c.wait(1)
-    grad_out.wait(1)
-    for r in range(ROWS):
-        put(zs, r, row(kept_up, r // 2))
+        put(gc, r, stack_rows(g, r))
     blocks = mm_nt(gs[...], zs[...])
     parts = []
     for a in range(3):
@@ -760,10 +757,95 @@
     clear_rest(grads, start + 80)
 
 
+def grads_down(scal, grad_fine, grad_c, kept_pool, kept_b, grads, gs, gc):
+    g = {r: row(grad_fine, r) for r in range(-1, ROWS + 1)}
+    for r in range(ROWS):
+        put(gs, r, stack_rows(g, r))
+    g = {r: row(grad_c, r) for r in range(-1, CROWS + 1)}
+    for r in range(CROWS):
+        put(gc, r, stack_rows(g, r))
+    blocks = mm_nt(gc[...], whole(kept_pool))
+    parts = [blocks[128 * a : 128 * (a + 1)] for a in range(3)]
+    start = put_grad(grads, 0, grad_blocks(parts, 64))
+    parts = fine_grad(mm_nt(gs[...], whole(kept_b)), 64, 64)
+    clear_rest(grads, put_grad(grads, start, grad_blocks(parts, 64)))
+
+
+def grads_first(scal, grad_b, line, vec, kept_a, grads, gs):
+    g = {r: row(grad_b, r) for r in range(-1, ROWS + 1)}
+    for r in range(ROWS):
+        put(gs, r, stack_rows(g, r))
+    parts = fine_grad(mm_nt(gs[...], whole(kept_a)), 64, 64)
+    start = put_grad(grads, 0, grad_blocks(parts, 64))
+    line = line.spot[0:1, :]
+    line = line + pltpu.roll(line, 64, 1)
+    column = jnp.sum(
+        place(128, 128, 0).astype(F32) * vec.spot[0:1, :].astype(F32), axis=1, keepdims=True
+    )
+    outer = (column * line).astype(BF16)
+    size = 128 // grads.shape[0]
+    for f in range(grads.shape[0]):
+        grads.spot[f, start : start + size, :] = outer[f * size : (f + 1) * size]
+
+
+def stage_up(
+    members, members_c, scal, stats_d, stats_ed, got_a, got_b, hats, back, wup_t, stats_c, hats_c,
+    wcoarse_t, done,
+    grad_merged, back_c, grad_coarse, edge_a, edge_b, stats, loss,
+):
+    give(loss, jnp.broadcast_to(total_stats(stats_ed)[2:3, :], (8, 128)))
+    mean, inverse = norm_columns(stats_d, True, members)
+    shift, slope = back_columns(stats_ed, True, members)
+    g = {}
+    for r in range(-3, ROWS + 3):
+        hat = row(hats, r).astype(F32)
+        if r < 0:
+            u = pick(scal, row(got_a, r + 3), row(got_b, r + 3)).astype(F32)
+        elif r < ROWS:
+            u = row(back, r).astype(F32)
+        else:
+            u = pick(scal, row(got_b, r - ROWS), row(got_a, r - ROWS)).astype(F32)
+        value = inverse * (u * silu_slope(hat) - shift - hat * slope)
+        g[r] = masked(value, r, ROWS, scal).astype(BF16)
+        if -2 <= r < ROWS + 2:
+            put(grad_merged, r, g[r])
+    wup_t.wait(1)
+    weights = whole(wup_t)
+    gk = {}
+    half = {}
+    for r in range(-2, ROWS + 2):
+        taps = mm(weights, stack_rows(g, r))
+        half[r] = taps[128:256] + taps[256:384] + from_right(taps[:128]) + from_left(taps[384:])
+        if r % 2:
+            value = masked(half.pop(r - 1) + half.pop(r), r // 2, CROWS, scal)
+            gk[r // 2] = value.astype(BF16)
+            put(grad_coarse, r // 2, gk[r // 2])
+    wcoarse_t.wait(1)
+    hats_c.wait(1)
+    stats_c.wait(1)
+    weights = whole(wcoarse_t)
+    mean, inverse = norm_columns(stats_c, False, members_c)
+    total = jnp.zeros((128, HALF), F32)
+    cross = jnp.zeros((128, HALF), F32)
+    for r in range(CROWS):
+        value = coarse_untap(mm(weights, stack_rows(gk, r)))
+        put(back_c, r, value.astype(BF16))
+        hat = row(hats_c, r).astype(F32)
+        e = value * silu_slope(hat)
+        total = total + e
+        cross = cross + e * hat
+    top = [row(back_c, 0), row(back_c, 1), gk[1]]
+    low = [row(back_c, 2), row(back_c, 3), gk[2]]
+    for j in range(3):
+        put(edge_a, j, pick(scal, top[j], low[j]))
+        put(edge_b, j, pick(scal, low[j], top[j]))
+    put_stats(stats, total, cross)
+
+
 def stage_down(
     members, members_c, scal, stats_c, stats_ec, got_a, got_b, hats_c, back_c, grad_coarse,
-    wdown_t, grad_merged, stats_b, wsecond_t, hats, kept_pool, kept_b,
-    grad_fine, back_b, stats, grads, gs, gc,
+    wdown_t, grad_merged, stats_b, wsecond_t, hats, done,
+    grad_fine, back_b, stats, grad_c,
 ):
     mean, inverse = norm_columns(stats_c, False, members_c)
     shift, slope = back_columns(stats_ec, False, members_c)
@@ -784,46 +866,39 @@
             through = row(grad_coarse, r).astype(F32)
         value = through + inverse * (u * silu_slope(hat) - shift - hat * slope)
         g[r] = masked(value, r, CROWS, scal).astype(BF16)
+        if -1 <= r <= CROWS:
+            put(grad_c, r, g[r])
+    wdown_t.wait(1)
     weights = whole(wdown_t)
     fine = {}
     for r in range(-1, CROWS + 1):
-        rows = stack_rows(g, r)
-        if 0 <= r < CROWS:
-            put(gc, r, rows)
-        value = 0.25 * coarse_untap(mm(weights, rows))
+        value = 0.25 * coarse_untap(mm(weights, stack_rows(g, r)))
         both = jnp.concatenate([value, value], axis=0)
         for i in (2 * r, 2 * r + 1):
             value = masked(row(grad_merged, i).astype(F32) + both, i, ROWS, scal)
             fine[i] = value.astype(BF16)
-            if 0 <= i < ROWS:
+            if -1 <= i <= ROWS:
                 put(grad_fine, i, fine[i])
+    wsecond_t.wait(1)
+    hats.wait(1)
     weights = whole(wsecond_t)
     mean, inverse = norm_columns(stats_b, True, members)
     total = jnp.zeros((128, HALF), F32)
     cross = jnp.zeros((128, HALF), F32)
     for r in range(-1, ROWS + 1):
-        rows = stack_rows(fine, r)
-        value = fine_untap(mm(weights, rows))
+        value = fine_untap(mm(weights, stack_rows(fine, r)))
         put(back_b, r, value.astype(BF16))
         if 0 <= r < ROWS:
-            put(gs, r, rows)
             hat = row(hats, r).astype(F32)
             e = value * silu_slope(hat)
             total = total + e
             cross = cross + e * hat
     put_stats(stats, total, cross)
-    kept_pool.wait(1)
-    kept_b.wait(1)
-    blocks = mm_nt(gc[...], whole(kept_pool))
-    parts = [blocks[128 * a : 128 * (a + 1)] for a in range(3)]
-    start = put_grad(grads, 0, grad_blocks(parts, 64))
-    parts = fine_grad(mm_nt(gs[...], whole(kept_b)), 64, 64)
-    clear_rest(grads, put_grad(grads, start, grad_blocks(parts, 64)))
 
 
 def stage_first(
-    members, scal, stats_b, stats_eb, hats_b, back_b, wfirst_t, stats_a, hats, vec, kept_a,
-    back_a, stats, grads, gs,
+    members, scal, stats_b, stats_eb, hats_b, back_b, wfirst_t, stats_a, hats, done,
+    back_a, stats, grad_b, line,
 ):
     mean, inverse = norm_columns(stats_b, True, members)
     shift, slope = back_columns(stats_eb, True, members)
@@ -836,35 +911,29 @@
         if 0 <= r < ROWS:
             sums = sums + value
         g[r] = masked(value, r, ROWS, scal).astype(BF16)
+        put(grad_b, r, g[r])
+    wfirst_t.wait(1)
+    hats.wait(1)
     weights = whole(wfirst_t)
     total = jnp.zeros((128, HALF), F32)
     cross = jnp.zeros((128, HALF), F32)
     for r in range(ROWS):
-        rows = stack_rows(g, r)
-        put(gs, r, rows)
-        value = fine_untap(mm(weights, rows))
+        value = fine_untap(mm(weights, stack_rows(g, r)))
         put(back_a, r, value.astype(BF16))
         hat = row(hats, r).astype(F32)
         e = value * silu_slope(hat)
         total = total + e
         cross = cross + e * hat
     put_stats(stats, total, cross)
-    kept_a.wait(1)
-    parts = fine_grad(mm_nt(gs[...], whole(kept_a)), 64, 64)
-    start = put_grad(grads, 0, grad_blocks(parts, 64))
-    line = to_row(jnp.sum(sums, axis=1, keepdims=True))
-    line = line + pltpu.roll(line, 64, 1)
-    column = jnp.sum(place(128, 128, 0).astype(F32) * vec.spot[0:1, :].astype(F32), axis=1, keepdims=True)
-    outer = (column * line).astype(BF16)
-    size = 128 // grads.shape[0]
-    for f in range(grads.shape[0]):
-        grads.spot[f, start : start + size, :] = outer[f * size : (f + 1) * size]
+    sums = to_row(jnp.sum(sums, axis=1, keepdims=True))
+    give(line, jnp.broadcast_to(sums, (8, 128)))
 
 
 def stage_last(
     members, scal, stats_a, stats_ea, hats, back_a, grad_fine, kept_in, early, middle, first,
-    loss, loss_other, grads, loss_sum, gs, sems,
+    loss, loss_other, keep, send, loss_sum, gs, held, sems,
 ):
+    grads = Source(held, [], 0)
     copies, start = [], 0
     for index, ref in enumerate((early, middle)):
         rows = pl.ds(start, ref.shape[1])
@@ -883,6 +952,8 @@
             u * silu_slope(hat) - shift - hat * slope
         )
         put(gs, r, value.astype(BF16))
+    kept_in.wait(1)
+    first.wait(1)
     parts = []
     for a in range(3):
         blocks = mm_nt(gs[...], kept_in.spot[:, a * HALF : (a + ROWS) * HALF])
@@ -897,6 +968,16 @@
     clear_rest(grads, put_grad(grads, start + size, parts))
     for copy in copies:
         copy.wait()
+    half = keep.shape[1]
+    odd = scal[8] > 0.5
+    for f in range(keep.shape[0]):
+        low, high = held[f, :half, :], held[f, half:, :]
+        keep.spot[f] = jnp.where(odd, high, low)
+        send.spot[f] = jnp.where(odd, low, high)
+
+
+def join(scal, kept, got, out):
+    give(out, (whole(kept).astype(F32) + whole(got).astype(F32)).astype(BF16))
 
 
 def add_up(scal, got, out):
@@ -908,13 +989,14 @@
         out.spot[index] = total
 
 
-def unpack(starts, scal, got, *refs):
+def unpack(starts, scal, mine, other, *refs):
     first, down, second, coarse, up, out, embed, inputs, flat = refs
-    size = got.shape[1]
-    for index in range(got.shape[0]):
-        flat[index * size : (index + 1) * size, :] = got.spot[index].astype(F32)
-
-    def take(ref, start, out, size, ins):
+    half = mine.shape[0]
+    odd = scal[8] > 0.5
+    flat[:half, :] = jnp.where(odd, whole(other), whole(mine)).astype(F32)
+    flat[half:, :] = jnp.where(odd, whole(mine), whole(other)).astype(F32)
+
+    def take(ref, start, out, size, ins, trim=False):
         for t in range(9):
             a, b = t // 3, t % 3
             if ins == 128:
@@ -923,21 +1005,27 @@
                 at, lanes = (a, b) if b < 2 else (3 + a // 2, a % 2)
             else:
                 at, lanes = a, b
-            step = 32 if ins == 24 else ins
             value = ref[start + at * size : start + (at + 1) * size, :]
-            rows = out.shape[1]
-            out.spot[t] = value[:rows, lanes * step : lanes * step + ins]
+            if ins == 24:
+                out.spot[t] = mm_nt(place(24, 128, 32 * lanes), value.astype(BF16))
+                continue
+            value = value[:, lanes * ins : (lanes + 1) * ins]
+            if trim:
+                value = value[:12]
+                if out.shape[2] == 32:
+                    value = jnp.where(scal[9] > 0.5, value[:, :32], value[:, 32:])
+            out.spot[t] = value
         return start + (9 if ins == 128 else 5 if ins == 64 else 3) * size
 
     start = take(flat, 0, up, up.shape[1], 128)
     start = take(flat, start, coarse, coarse.shape[1], 128)
-    take(flat, start, out, 16, 64)
+    take(flat, start, out, 16, 64, trim=True)
     start = take(flat, starts[0], down, down.shape[1], 64)
     take(flat, start, second, second.shape[1], 64)
     start = take(flat, starts[1], first, first.shape[1], 64)
     size = embed.shape[0]
     give(embed, flat[start : start + size, :64])
-    take(flat, start + size, inputs, inputs.shape[1], 24)
+    take(flat, start + size, inputs, inputs.shape[2], 24)
 
 
 class Field:
@@ -1123,8 +1211,11 @@
     noise = noise_sample.reshape(12 * ROWS, 512)
 
     def pack_all(name, shards, rows, *after):
-        widths = tuple((9 if item.ndim == 3 else 1, size) for item, size in zip(shards, rows))
-        total = sum(taps * size for taps, size in widths)
+        widths = tuple(
+            (9 if item.ndim == 3 else 1, size, item.ndim == 3 and item.shape[1] == 24)
+            for item, size in zip(shards, rows)
+        )
+        total = sum(taps * size for taps, size, _ in widths)
         (packed,) = run(
             name,
             functools.partial(pack, widths),
@@ -1134,27 +1225,35 @@
             *after,
             scratch=[((total, 128), F32)],
         )
-        return gather_packed(packed)
+        return packed
 
     fine_o, coarse_o = input_kernel.shape[1], down_kernel.shape[1]
-    early = pack_all(
+    inputs_t = jnp.swapaxes(input_kernel, 1, 2)
+    early_packed = pack_all(
         "pack_first",
-        [input_kernel, first_kernel, embed_matrix],
+        [inputs_t, first_kernel, embed_matrix],
         [fine_o, fine_o, embed_matrix.shape[0]],
     )
+    early = gather_packed(early_packed)
     far = shape(32, FAR * 512, dtype=BF16)
-    own, edge_a, edge_b, line_a, line_b = run(
+    own, edge_a, edge_b = run(
         "enter",
         enter,
-        [shape(32, ROWS * 512, dtype=BF16), far, far, shape(16, 512), shape(16, 512)],
+        [shape(32, ROWS * 512, dtype=BF16), far, far],
         scal,
         Saved(target),
         Saved(condition),
         Saved(noise),
-        scratch=[((4, 192, 128), F32)],
+        early[0],
+        scratch=[((4, 192, 128), F32), ((2, 16, FAR * 512), BF16)],
     )
     got_a, got_b = swap(edge_a, edge_b)
-    line_a, line_b = swap(line_a, line_b)
+    rest = pack_all(
+        "pack_rest",
+        [second_kernel, down_kernel, coarse_kernel, upward_kernel, output_kernel],
+        [fine_o, coarse_o, coarse_o, fine_o, 16],
+        own,
+    )
     vector = jnp.broadcast_to(embedded[None, :], (16, embedded.shape[0]))
     win, wfirst, wfirst_t, shift = run(
         "prepare_first",
@@ -1167,20 +1266,20 @@
         vector, *early,
     )
     stat = shape(bands, 8, 128)
-    act_a, stats_a, kept_in = run(
+    total = Saved(shape(1, 8, 128))
+    act_a, stats_a, kept_in, line_a, line_b = run(
         "stage_a",
         stage_a,
-        [rows_of(-6, 20), stat, Saved(flat_rows(-1, 10, 128))],
-        scal,
-        win, got_a, got_b, own,
+        [
+            rows_of(-6, 20), stat, Saved(flat_rows(-1, 10, 128)),
+            Saved(shape(16, 512)), Saved(shape(16, 512)),
+        ],
+        scal,
+        win, got_a, got_b, own, rest,
         scratch=[((32, FAR * 512), BF16), ((32, FAR * 512), BF16)],
     )
-    rest = pack_all(
-        "pack_rest",
-        [second_kernel, down_kernel, coarse_kernel, upward_kernel, output_kernel],
-        [fine_o, coarse_o, coarse_o, fine_o, 16],
-        stats_a,
-    )
+    stats_a = sum_parts(stats_a)
+    rest, stats_a = lax.optimization_barrier((rest, stats_a))
     (
         wsecond, wsecond_t, wdown, wdown_t, wcoarse, wcoarse_t, wup, wup_t, wout, wout_t
     ) = run(
@@ -1194,107 +1293,132 @@
             Saved(shape(96, 256, dtype=BF16)), Saved(shape(256, 96, dtype=BF16)),
         ],
         scal,
-        *rest,
-    )
-
-    stats_a = sum_parts(stats_a)
-    act_b, stats_b, kept_a, hats_a, act_a = run(
+        *gather_packed(rest),
+    )
+
+    act_b, stats_b, kept_a, hats_a, act_a, total_a = run(
         "stage_b",
         functools.partial(stage_b, members),
         [
             rows_of(-5, 18), stat, Saved(flat_rows(0, 8, 256)), Saved(rows_of(0, 8, BF16)),
-            Saved(rows_of(-4, 16), when=None),
+            Saved(rows_of(-4, 16), when=None), total,
         ],
         scal,
-        stats_a, shift, Saved(wfirst), act_a,
+        stats_a, shift, Saved(wfirst, when=1), act_a,
         scratch=[pltpu.SemaphoreType.DMA(())],
     )
     stats_b = sum_parts(stats_b)
-    fine, act_c, edge, stats_c, kept_b, kept_pool, hats_b = run(
+    fine, act_c, edge, stats_c, kept_b, kept_pool, hats_b, total_b = run(
         "stage_c",
         functools.partial(stage_c, members),
         [
             rows_of(-3, 14), rows_of(-1, 6), Field(shape(128, 2 * HALF), 1), stat,
             Saved(flat_rows(0, 8, 256)), Saved(flat_rows(0, 4, 192)), Saved(rows_of(-1, 10, BF16)),
+            total,
         ],
         scal,
-        stats_b, Saved(wsecond), act_b, Saved(act_a), Saved(wdown),
+        stats_b, Saved(wsecond, when=1), act_b, Saved(act_a, when=1), Saved(wdown, when=1),
     )
     got_a, got_b = swap(edge.array, edge.array)
     stats_c = sum_parts(stats_c)
-    merged, hats_c, stats_d, kept_c, kept_up = run(
+    merged, hats_c, stats_d, kept_c, kept_up, total_c = run(
         "stage_d",
         functools.partial(stage_d, members_c),
         [
             rows_of(-3, 14), Saved(rows_of(-2, 8, BF16)), stat,
-            Saved(flat_rows(0, 4, 384)), Saved(flat_rows(0, 4, 384)),
+            Saved(flat_rows(0, 4, 384)), Saved(flat_rows(0, 4, 384)), total,
         ],
         scal,
-        stats_c, Saved(wcoarse), got_a, got_b, act_c, Saved(wup), fine,
+        stats_c, Saved(wcoarse), Saved(got_a), Saved(got_b), act_c, Saved(wup), fine,
     )
     stats_d = sum_parts(stats_d)
     edge = Field(shape(128, 3 * HALF, dtype=BF16), 0)
-    denoised, back_d, edge_a, edge_b, stats_ed, grad_out, hats_d = run(
+    denoised, back_d, edge_a, edge_b, stats_ed, hats_d, cotangents, kept_d, total_d = run(
         "stage_out",
         functools.partial(stage_out, members),
         [
             Saved(shape(96, 512)), rows_of(0, 8, BF16), edge, edge, stat,
-            Saved(shape(count, 80, 128, dtype=BF16)), rows_of(-3, 14, BF16),
+            Saved(rows_of(-3, 14, BF16)),
+            Field(shape(10, 32, HALF, dtype=BF16), -1), Saved(flat_rows(0, 8, 256)), total,
         ],
         scal,
-        stats_d, Saved(wout), merged, Saved(line_a), Saved(line_b), Saved(target), Saved(noise),
-        Saved(wout_t),
+        stats_d, Saved(wout, when=1), merged, Saved(line_a, when=1), Saved(line_b, when=1),
+        Saved(target, when=1), Saved(noise, when=1), Saved(wout_t, when=1),
         scratch=[
-            ((160, 512), F32), ((160, 512), F32), ((96, 8 * HALF), BF16), ((256, 8 * HALF), BF16),
+            ((160, 512), F32), ((160, 512), F32),
             ((4, 96, 128), F32), ((4, 96, 128), F32), ((4, 96, 128), F32),
         ],
     )
     got_a, got_b = swap(edge_a.array, edge_b.array)
+    (grad_out,) = run(
+        "grads_out",
+        grads_out,
+        [Saved(shape(count, 80, 128, dtype=BF16))],
+        scal,
+        cotangents, Saved(kept_d),
+        scratch=[((96, 8 * HALF), BF16)],
+    )
     stats_ed = sum_parts(stats_ed)
-    grad_merged, back_c, grad_coarse, edge_a, edge_b, stats_ec, loss, early = run(
+    grad_merged, back_c, grad_coarse, edge_a, edge_b, stats_ec, loss = run(
         "stage_up",
         functools.partial(stage_up, members, members_c),
         [
             rows_of(-2, 12, BF16), rows_of(0, 4, BF16), rows_of(-1, 6, BF16), edge, edge, stat,
-            shape(8, 128), Saved(group_shape(9 * (fine_o + coarse_o) + 80, count)),
+            shape(8, 128),
         ],
         scal,
-        stats_d, stats_ed, got_a, got_b, hats_d, back_d, Saved(wup_t), stats_c, Saved(hats_c),
-        Saved(wcoarse_t), Saved(kept_up, when=1), Saved(kept_c, when=1), Saved(grad_out, when=1),
+        Saved(total_d), stats_ed, Saved(got_a), Saved(got_b), Saved(hats_d), back_d, Saved(wup_t, when=1),
+        Saved(total_c, when=1),
+        Saved(hats_c, when=1), Saved(wcoarse_t, when=1), Saved(grad_out, when=None),
+    )
+    got_a, got_b = swap(edge_a.array, edge_b.array)
+    (early,) = run(
+        "grads_up",
+        grads_up,
+        [Saved(group_shape(9 * (fine_o + coarse_o) + 80, count))],
+        scal,
+        grad_merged, grad_coarse, Saved(kept_up), Saved(kept_c), Saved(grad_out),
         scratch=[
             ((384, 8 * HALF), BF16), ((384, 8 * HALF), BF16), ((384, 4 * HALF), BF16)
         ],
     )
-    got_a, got_b = swap(edge_a.array, edge_b.array)
     stats_ec = sum_parts(stats_ec)
     if count == 2:
         loss_other = lax.ppermute(loss, "fsdp", [(0, 1), (1, 0)])
     else:
         loss_other = lax.psum(loss, "fsdp") - loss
-    grad_fine, back_b, stats_eb, middle = run(
+    grad_fine, back_b, stats_eb, grad_c = run(
         "stage_down",
         functools.partial(stage_down, members, members_c),
-        [
-            Saved(rows_of(0, 8, BF16)), rows_of(-1, 10, BF16), stat,
-            Saved(group_shape(5 * (fine_o + coarse_o), count)),
-        ],
-        scal,
-        stats_c, stats_ec, got_a, got_b, Saved(hats_c), back_c, grad_coarse,
-        Saved(wdown_t), grad_merged, stats_b, Saved(wsecond_t), Saved(hats_b, 0, 8),
-        Saved(kept_pool, when=1), Saved(kept_b, when=1),
+        [rows_of(-1, 10, BF16), rows_of(-1, 10, BF16), stat, rows_of(-1, 6, BF16)],
+        scal,
+        Saved(total_c), stats_ec, Saved(got_a), Saved(got_b), Saved(hats_c), back_c, grad_coarse,
+        Saved(wdown_t, when=1), grad_merged, Saved(total_b), Saved(wsecond_t, when=1),
+        Saved(hats_b, 0, 8, when=1), Saved(early, when=None),
+    )
+    (middle,) = run(
+        "grads_down",
+        grads_down,
+        [Saved(group_shape(5 * (fine_o + coarse_o), count))],
+        scal,
+        grad_fine, grad_c, Saved(kept_pool), Saved(kept_b),
         scratch=[((384, 8 * HALF), BF16), ((384, 4 * HALF), BF16)],
     )
     stats_eb = sum_parts(stats_eb)
-    back_a, stats_ea, grad_first = run(
+    back_a, stats_ea, grad_b, line = run(
         "stage_first",
         functools.partial(stage_first, members),
-        [
-            rows_of(0, 8, BF16), stat,
-            Saved(shape(count, 5 * fine_o + embed_matrix.shape[0], 128, dtype=BF16)),
-        ],
-        scal,
-        stats_b, stats_eb, Saved(hats_b), back_b, Saved(wfirst_t), stats_a, Saved(hats_a), vector,
-        Saved(kept_a, when=1),
+        [rows_of(0, 8, BF16), stat, rows_of(-1, 10, BF16), shape(8, 128)],
+        scal,
+        Saved(total_b), stats_eb, Saved(hats_b), back_b, Saved(wfirst_t, when=1), Saved(total_a),
+        Saved(hats_a, when=1), Saved(middle, when=None),
+    )
+    (grad_first,) = run(
+        "grads_first",
+        grads_first,
+        [Saved(shape(count, 5 * fine_o + embed_matrix.shape[0], 128, dtype=BF16))],
+        scal,
+        grad_b, line, vector, Saved(kept_a),
         scratch=[((384, 8 * HALF), BF16)],
     )
     stats_ea = sum_parts(stats_ea)
@@ -1302,19 +1426,32 @@
     starts = [early.shape[1], early.shape[1] + middle.shape[1]]
     total = starts[1] + late.shape[1]
     chunk = -(-total // (16 * bands)) * 16
-    grads, loss = run(
+    chips = bands // 2
+    half = shape(count, chunk * chips, 128, dtype=BF16)
+    keep, send, loss = run(
         "stage_last",
         functools.partial(stage_last, members),
-        [shape(count, chunk * bands, 128, dtype=BF16), shape(8, 128)],
-        scal,
-        stats_a, stats_ea, Saved(hats_a), back_a, Saved(grad_fine), Saved(kept_in),
-        Saved(early, when=None), Saved(middle, when=None), Saved(grad_first), loss, loss_other,
-        scratch=[((128, 8 * HALF), BF16), pltpu.SemaphoreType.DMA((2,))],
+        [half, half, shape(8, 128)],
+        scal,
+        Saved(total_a), stats_ea, Saved(hats_a), back_a, grad_fine, Saved(kept_in, when=1),
+        Saved(early, when=None), Saved(middle, when=None), Saved(grad_first, when=1), loss, loss_other,
+        scratch=[
+            ((128, 8 * HALF), BF16), ((count, chunk * bands, 128), BF16),
+            pltpu.SemaphoreType.DMA((2,)),
+        ],
     )
     loss_value = loss[0, 0] / members_all
-    got = lax.all_to_all(grads.reshape(count * bands, chunk, 128), ("fsdp", "rows"), 0, 0)
-    (mine,) = run("add_up", add_up, [shape(bands, chunk, 128, dtype=BF16)], scal, got)
-    got = lax.all_to_all(mine, "rows", 0, 0)
+    pairs = [(i, i ^ 1) for i in range(bands)]
+    got = lax.ppermute(send, "rows", pairs)
+    (both,) = run("join", join, [half], scal, keep, got)
+    both = both.reshape(count * chips, chunk, 128)
+    cores = [[f * bands + r for f in range(count) for r in range(c, bands, 2)] for c in range(2)]
+    got = lax.all_to_all(both, ("fsdp", "rows"), 0, 0, axis_index_groups=cores)
+    (mine,) = run("add_up", add_up, [shape(chips, chunk, 128, dtype=BF16)], scal, got)
+    cores = [[r for r in range(c, bands, 2)] for c in range(2)]
+    mine = lax.all_to_all(mine, "rows", 0, 0, axis_index_groups=cores)
+    mine = mine.reshape(chips * chunk, 128)
+    other = lax.ppermute(mine, "rows", pairs)
     first_g, down_g, second_g, coarse_g, up_g, out_g, embed_g, in_g = run(
         "unpack",
         functools.partial(unpack, starts),
@@ -1324,20 +1461,21 @@
             shape(*second_kernel.shape),
             shape(*coarse_kernel.shape),
             shape(*upward_kernel.shape),
-            shape(9, 12, 64),
+            shape(9, 12, output_kernel.shape[2] if count == 2 else 64),
             shape(*embed_matrix.shape),
-            shape(*input_kernel.shape),
+            shape(*inputs_t.shape),
         ],
         scal,
-        got,
+        mine, other,
         scratch=[((chunk * bands, 128), F32)],
     )
     width = output_kernel.shape[2]
-    out_g = lax.dynamic_slice_in_dim(out_g, lax.axis_index("fsdp") * width, width, axis=2)
+    if count != 2:
+        out_g = lax.dynamic_slice_in_dim(out_g, lax.axis_index("fsdp") * width, width, axis=2)
     return (
         denoised.reshape(residual_target.shape),
         loss_value,
-        in_g,
+        jnp.swapaxes(in_g, 1, 2),
         first_g,
         second_g,
         down_g,

time: 211 us -> 193 us (0.915)
  blocking collectives: 86.8 us -> 64.1 us
  Pallas kernels: 59 us -> 71.4 us
  waiting for transfers between devices: 31.1 us -> 19.9 us
  starting transfers between devices: 25.2 us -> 30 us
    all_to_all x5 -> x3, blocking collectives: 60.7 us -> 35.3 us  [sum_parts(): return lax.all_to_all(stats, 'rows', 0, 0)]
    pallas_call x16 -> x21, Pallas kernels: 59 us -> 71.4 us  [run(): pl.pallas_call(body, out_shape=tuple(out_shapes), in_specs=in_specs, out_...]
    all_to_all x1 -> x0, waiting for transfers between devices: 12 us -> none  [per_device(): got = lax.all_to_all(mine, 'rows', 0, 0)]
    all_to_all x3 -> x5, starting transfers between devices: 10.5 us -> 20 us  [sum_parts(): return lax.all_to_all(stats, 'rows', 0, 0)]
    all_to_all x1 -> x0, starting transfers between devices: 3.57 us -> none  [per_device(): got = lax.all_to_all(mine, 'rows', 0, 0)]
    ppermute x1, waiting for transfers between devices: 3.1 us -> 0.01 us  [per_device(): loss_other = lax.ppermute(loss, 'fsdp', [(0, 1), (1, 0)])]
    all_to_all x1 -> x2, blocking collectives: 26.1 us -> 28.9 us  [the longest x1 17.7 us: per_device(): got = lax.all_to_all(both, ('fsdp', 'rows'), 0, 0, axis_index_groups=cores)]
    ppermute x0 -> x2, waiting for transfers between devices: none -> 2.12 us  [the longest x1 1.8 us: per_device(): got = lax.ppermute(send, 'rows', pairs)]
  transfers between devices with their start and end apart: 17 -> 18, of which waited for: 7 -> 9; matrix products, arithmetic and copies ran while one was open for 1% -> 0% of each run, Pallas kernels for 6% -> 13%
where the time goes in v1:
time: 193 us; the launch traced here: 192 us
  Pallas kernels  71.4 us (37%)
  blocking collectives  64.1 us (33%)
  starting transfers between devices  30 us (16%)
  waiting for transfers between devices  19.9 us (10%)
  between operations  3.64 us (2%)
  local copies, waits for them, and re-layouts  2.9 us (2%)
    pallas_call x21, Pallas kernels, run(): pl.pallas_call(body, out_shape=tuple(out_shapes), in_specs=in_specs, out_...  71.4 us
    all_to_all x3, blocking collectives, sum_parts(): return lax.all_to_all(stats, 'rows', 0, 0)  35.3 us
    all_to_all x5, starting transfers between devices, sum_parts(): return lax.all_to_all(stats, 'rows', 0, 0)  20 us
    all_to_all x1, blocking collectives, per_device(): got = lax.all_to_all(both, ('fsdp', 'rows'), 0, 0, axis_index_groups=cores)  17.7 us
    all_to_all x5, waiting for transfers between devices, sum_parts(): return lax.all_to_all(stats, 'rows', 0, 0)  14 us
    all_to_all x1, blocking collectives, per_device(): mine = lax.all_to_all(mine, 'rows', 0, 0, axis_index_groups=cores)  11.1 us
    ppermute x2, starting transfers between devices, gather_packed(): return [packed, lax.ppermute(packed, 'fsdp', [(0, 1), (1, 0)])]  4.06 us
  transfers between devices with their start and end apart: 18, of which 9 were waited for; matrix products, arithmetic and copies ran while one was open for 0% of the time, Pallas kernels for 13%

profile of v1, /device:TPU:0, one launch (start us, length us, event | category | flops | bytes accessed | tf_op | source)
XLA Modules:
  0.0 192.1 jit_solution(12916225200931334159)
XLA Ops:
  3.3 2.1 %enter.1 = (bf16[32,4096]{1,0:T(8,128)(2,1)S(1)}, bf16[32,3584]{1,0:T(8,128)(2,1)S(1)}, bf16[32,3584]{1,0:T(8,128)(2,1)S(1)}) custom-call(f32[10]{0:T(128)S(1)} %stack.52.numbers, f32[96,512]{1,0:T(8,128)} %bitcast.17, f32[96,512]{1,0:T(8,128)} %bitcast.21, f32[96,512]{1,0:T(8,128)} %bitcast.19, bf16[640,128]{1,0:T(8,128)(2,1)S(1)} %pack_first.1.refs_3_.refs_1_), custom_call_target="tpu_custom_call" | custom-call | tf_op jit(solution)/shard_map/enter/pallas_call | solution.py:1131
  6.6 2.6 %collective-permute-start = (bf16[640,128]{1,0:T(8,128)(2,1)S(1)}, bf16[640,128]{1,0:T(8,128)(2,1)S(1)}, u32[]{:S(2)}, u32[]{:S(2)}) collective-permute-start(bf16[640,128]{1,0:T(8,128)(2,1)S(1)} %pack_first.1.refs_3_.refs_1_), channel_id=1, source_target_pairs={{0,16},{16,0},{1,17},{17,1},{2,18},{18,2},{3,19},{19,3},{4,20},{20... | collective-permute-start | bytes 491528 | tf_op jit(solution)/shard_map/ppermute | solution.py:1164
  12.5 1.9 prepare_first.1
  14.3 2.9 %stage_a.1 = (f32[20,128,256]{2,1,0:T(8,128)S(1)}, f32[16,8,128]{2,1,0:T(8,128)S(1)}, bf16[128,2560]{1,0:T(8,128)(2,1)}, f32[16,512]{1,0:T(8,128)}, f32[16,512]{1,0:T(8,128)}) custom-call(f32[10]{0:T(128)S(1)} %stack.52.numbers, bf16[384,128]{1,0:T(8,128)(2,1)S(1)} %get-tuple-element.90.refs_0_, bf16[32,3584]{1,0:T(8,128)(2,1)S(1)} %collective-permute-done.1.refs_1_, ...), custom_call_target="tpu_custom_call" | custom-call | tf_op jit(solution)/shard_map/stage_a/pallas_call | solution.py:1131
  17.2 15.9 %all_to_all.50.refs_0_ = f32[16,8,128]{2,1,0:T(8,128)S(1)} all-to-all(f32[16,8,128]{2,1,0:T(8,128)S(1)} %get-tuple-element.93), channel_id=1, replica_groups=mesh['fsdp'=2,'rows'=16] {'rows'}, dimensions={0} | all-to-all | bytes 131072 | tf_op jit(solution)/shard_map/all_to_all | solution.py:1150
  34.6 4.9 %stage_b.1 = (f32[18,128,256]{2,1,0:T(8,128)S(1)}, f32[16,8,128]{2,1,0:T(8,128)}, bf16[256,2048]{1,0:T(8,128)(2,1)}, bf16[8,128,256]{2,1,0:T(8,128)(2,1)}, f32[1...) custom-call(f32[10]{0:T(128)S(1)} %stack.52.numbers, f32[16,8,128]{2,1,0:T(8,128)S(1)} %all_to_all.50.refs_0_, ...), custom_call_target="tpu_custom_call" | custom-call | tf_op jit(solution)/shard_map/stage_b/pallas_call | solution.py:1131
  39.5 3.5 %all-to-all-start.1 = ((f32[16,8,128]{2,1,0:T(8,128)}), f32[16,8,128]{2,1,0:T(8,128)S(1)}, u32[]{:S(2)}, u32[]{:S(2)}) async-start(f32[16,8,128]{2,1,0:T(8,128)} %get-tuple-element.98), calls=%async_computation.1 | async-start | bytes 131072 | tf_op jit(solution)/shard_map/all_to_all | solution.py:1150
  43.0 2.5 %collective-permute-done.3.refs_1_ = bf16[1872,128]{1,0:T(8,128)(2,1)S(1)} collective-permute-done((bf16[1872,128]{1,0:T(8,128)(2,1)S(1)}, bf16[1872,128]{1,0:T(8,128)(2,1)S(1)}, u32[]{:S(2)}, u32[]{:S(2)}) %collective-permute-start.3) | collective-permute-done | bytes 479264 | tf_op jit(solution)/shard_map/ppermute | solution.py:1164
  45.5 3.1 %prepare_rest.1 = (bf16[384,256]{1,0:T(8,128)(2,1)}, bf16[256,384]{1,0:T(8,128)(2,1)}, bf16[384,192]{1,0:T(8,128)(2,1)}, bf16[192,384]{1,0:T(8,128)(2,1)}, bf16[...) custom-call(f32[10]{0:T(128)S(1)} %stack.52.numbers, ...), custom_call_target="tpu_custom_call" | custom-call | tf_op jit(solution)/shard_map/prepare_rest/pallas_call | solution.py:1131
  49.9 6.1 %stage_c.1 = (f32[14,128,256]{2,1,0:T(8,128)S(1)}, f32[6,128,256]{2,1,0:T(8,128)S(1)}, f32[128,512]{1,0:T(8,128)S(1)}, f32[16,8,128]{2,1,0:T(8,128)S(1)}, bf16[2...) custom-call(f32[10]{0:T(128)S(1)} %stack.52.numbers, ...), custom_call_target="tpu_custom_call" | custom-call | tf_op jit(solution)/shard_map/stage_c/pallas_call | solution.py:1131
  58.2 9.9 %all_to_all.51.refs_0_ = f32[16,8,128]{2,1,0:T(8,128)S(1)} all-to-all(f32[16,8,128]{2,1,0:T(8,128)S(1)} %get-tuple-element.104), channel_id=1, replica_groups=mesh['fsdp'=2,'rows'=16] {'rows'}, dimensions={0} | all-to-all | bytes 131072 | tf_op jit(solution)/shard_map/all_to_all | solution.py:1150
  69.0 6.2 %stage_d.1 = (f32[14,128,256]{2,1,0:T(8,128)S(1)}, bf16[8,128,256]{2,1,0:T(8,128)(2,1)}, f32[16,8,128]{2,1,0:T(8,128)S(1)}, bf16[384,1024]{1,0:T(8,128)(2,1)}, b...) custom-call(f32[10]{0:T(128)S(1)} %stack.52.numbers, f32[16,8,128]{2,1,0:T(8,128)S(1)} %all_to_all.51.refs_0_, ...), custom_call_target="tpu_custom_call" | custom-call | tf_op jit(solution)/shard_map/stage_d/pallas_call | solution.py:1131
  75.2 9.5 %all_to_all.52.refs_0_ = f32[16,8,128]{2,1,0:T(8,128)S(1)} all-to-all(f32[16,8,128]{2,1,0:T(8,128)S(1)} %get-tuple-element.110), channel_id=1, replica_groups=mesh['fsdp'=2,'rows'=16] {'rows'}, dimensions={0} | all-to-all | bytes 131072 | tf_op jit(solution)/shard_map/all_to_all | solution.py:1150
  84.6 5.2 %stage_out.1 = (f32[96,512]{1,0:T(8,128)}, bf16[8,128,256]{2,1,0:T(8,128)(2,1)S(1)}, bf16[128,768]{1,0:T(8,128)(2,1)S(1)}, bf16[128,768]{1,0:T(8,128)(2,1)S(1)},...) custom-call(f32[10]{0:T(128)S(1)} %stack.52.numbers, ...), custom_call_target="tpu_custom_call" | custom-call | tf_op jit(solution)/shard_map/stage_out/pallas_call | solution.py:1131
  90.6 4.7 %all-to-all-start.4 = ((f32[16,8,128]{2,1,0:T(8,128)}), f32[16,8,128]{2,1,0:T(8,128)S(1)}, u32[]{:S(2)}, u32[]{:S(2)}) async-start(f32[16,8,128]{2,1,0:T(8,128)} %get-tuple-element.121), calls=%async_computation.4 | async-start | bytes 131072 | tf_op jit(solution)/shard_map/all_to_all | solution.py:1150
  95.3 3.0 %grads_out.1.refs_10_.refs_4_ = bf16[2,80,128]{2,1,0:T(8,128)(2,1)} custom-call(f32[10]{0:T(128)S(1)} %stack.52.numbers, bf16[10,32,256]{2,1,0:T(8,128)(2,1)S(1)} %get-tuple-element.129.refs_0_, bf16[256,2048]{1,0:T(8,128)(2,1)} %get-tuple-element.130.refs_1_), custom_call_target="tpu_custom_call" | custom-call | tf_op jit(solution)/shard_map/grads_out/pallas_call | solution.py:1131
  98.3 3.9 %all-to-all-done.4.refs_1_ = f32[16,8,128]{2,1,0:T(8,128)S(1)} async-done(((f32[16,8,128]{2,1,0:T(8,128)}), f32[16,8,128]{2,1,0:T(8,128)S(1)}, u32[]{:S(2)}, u32[]{:S(2)}) %all-to-all-start.4) | async-done | bytes 65568 | tf_op jit(solution)/shard_map/all_to_all | solution.py:1150
  103.0 6.7 %stage_up.1 = (bf16[12,128,256]{2,1,0:T(8,128)(2,1)S(1)}, bf16[4,128,256]{2,1,0:T(8,128)(2,1)S(1)}, bf16[6,128,256]{2,1,0:T(8,128)(2,1)S(1)}, bf16[128,768]{1,0:...) custom-call(f32[10]{0:T(128)S(1)} %stack.52.numbers, ...), custom_call_target="tpu_custom_call" | custom-call | tf_op jit(solution)/shard_map/stage_up/pallas_call | solution.py:1131
  110.4 4.8 %all-to-all-start.5 = ((f32[16,8,128]{2,1,0:T(8,128)}), f32[16,8,128]{2,1,0:T(8,128)S(1)}, u32[]{:S(2)}, u32[]{:S(2)}) async-start(f32[16,8,128]{2,1,0:T(8,128)} %get-tuple-element.131), calls=%async_computation.5 | async-start | bytes 131072 | tf_op jit(solution)/shard_map/all_to_all | solution.py:1150
  115.2 4.2 %grads_up.1.refs_12_.refs_6_ = bf16[2,944,128]{2,1,0:T(8,128)(2,1)} custom-call(f32[10]{0:T(128)S(1)} %stack.52.numbers, bf16[12,128,256]{2,1,0:T(8,128)(2,1)S(1)} %get-tuple-element.137.refs_0_.refs_8_, bf16[6,128,256]{2,1,0:T(8,128)(2,1)S(1)} %get-tuple-element.135.refs_1_.refs_6_, bf16[384,1024]{1,0:T(8,128)(2,1)} %get-tuple-element.140.refs_2_, ...), custom_call_target="tpu_custom_call" | custom-call | tf_op jit(solution)/shard_map/grads_up/pallas_call | solution.py:1131
  119.3 2.7 %all-to-all-done.5.refs_1_ = f32[16,8,128]{2,1,0:T(8,128)S(1)} async-done(((f32[16,8,128]{2,1,0:T(8,128)}), f32[16,8,128]{2,1,0:T(8,128)S(1)}, u32[]{:S(2)}, u32[]{:S(2)}) %all-to-all-start.5) | async-done | bytes 65568 | tf_op jit(solution)/shard_map/all_to_all | solution.py:1150
  122.8 4.9 %stage_down.1 = (bf16[10,128,256]{2,1,0:T(8,128)(2,1)S(1)}, bf16[10,128,256]{2,1,0:T(8,128)(2,1)S(1)}, f32[16,8,128]{2,1,0:T(8,128)}, bf16[6,128,256]{2,1,0:T(8,128)(2,1)S(1)}) custom-call(f32[10]{0:T(128)S(1)} %stack.52.numbers, f32[1,8,128]{2,1,0:T(8,128)} %get-tuple-element.119.refs_7_.refs_0_, f32[16,8,128]{2,1,0:T(8,128)S(1)} %all-to-all-done.5.refs_1_, ...), custom_call_target="tpu_custom_call" | custom-call | tf_op jit(solution)/shard_map/stage_down/pallas_call | solution.py:1131
  127.7 3.5 %all-to-all-start.6 = ((f32[16,8,128]{2,1,0:T(8,128)}), f32[16,8,128]{2,1,0:T(8,128)S(1)}, u32[]{:S(2)}, u32[]{:S(2)}) async-start(f32[16,8,128]{2,1,0:T(8,128)} %get-tuple-element.142), calls=%async_computation.6 | async-start | bytes 131072 | tf_op jit(solution)/shard_map/all_to_all | solution.py:1150
  131.2 3.5 %grads_down.1.refs_7_ = bf16[2,480,128]{2,1,0:T(8,128)(2,1)} custom-call(f32[10]{0:T(128)S(1)} %stack.52.numbers, bf16[10,128,256]{2,1,0:T(8,128)(2,1)S(1)} %get-tuple-element.146.refs_0_.refs_4_, bf16[6,128,256]{2,1,0:T(8,128)(2,1)S(1)} %get-tuple-element.147.refs_1_, bf16[192,1024]{1,0:T(8,128)(2,1)} %get-tuple-element.148.refs_2_, ...), custom_call_target="tpu_custom_call" | custom-call | tf_op jit(solution)/shard_map/grads_down/pallas_call | solution.py:1131
  134.7 3.3 %all-to-all-done.6.refs_1_ = f32[16,8,128]{2,1,0:T(8,128)S(1)} async-done(((f32[16,8,128]{2,1,0:T(8,128)}), f32[16,8,128]{2,1,0:T(8,128)S(1)}, u32[]{:S(2)}, u32[]{:S(2)}) %all-to-all-start.6) | async-done | bytes 65568 | tf_op jit(solution)/shard_map/all_to_all | solution.py:1150
  138.1 4.1 %stage_first.1 = (bf16[8,128,256]{2,1,0:T(8,128)(2,1)S(1)}, f32[16,8,128]{2,1,0:T(8,128)}, bf16[10,128,256]{2,1,0:T(8,128)(2,1)S(1)}, f32[8,128]{1,0:T(8,128)S(1)}) custom-call(f32[10]{0:T(128)S(1)} %stack.52.numbers, f32[1,8,128]{2,1,0:T(8,128)} %get-tuple-element.118.refs_9_.refs_0_, f32[16,8,128]{2,1,0:T(8,128)S(1)} %all-to-all-done.6.refs_1_, ...), custom_call_target="tpu_custom_call" | custom-call | tf_op jit(solution)/shard_map/stage_first/pallas_call | solution.py:1131
  142.2 3.5 %all-to-all-start.7 = ((f32[16,8,128]{2,1,0:T(8,128)}), f32[16,8,128]{2,1,0:T(8,128)S(1)}, u32[]{:S(2)}, u32[]{:S(2)}) async-start(f32[16,8,128]{2,1,0:T(8,128)} %get-tuple-element.150), calls=%async_computation.7 | async-start | bytes 131072 | tf_op jit(solution)/shard_map/all_to_all | solution.py:1150
  146.6 3.1 %grads_first.1.refs_8_ = bf16[2,224,128]{2,1,0:T(8,128)(2,1)} custom-call(f32[10]{0:T(128)S(1)} %stack.52.numbers, bf16[10,128,256]{2,1,0:T(8,128)(2,1)S(1)} %get-tuple-element.153.refs_0_, f32[8,128]{1,0:T(8,128)S(1)} %get-tuple-element.154.refs_1_, bf16[16,128]{1,0:T(8,128)(2,1)S(1)} %broadcast_in_dim.2.refs_0_.refs_2_, ...), custom_call_target="tpu_custom_call" | custom-call | tf_op jit(solution)/shard_map/grads_first/pallas_call | solution.py:1131
  149.8 2.8 %all-to-all-done.7.refs_1_ = f32[16,8,128]{2,1,0:T(8,128)S(1)} async-done(((f32[16,8,128]{2,1,0:T(8,128)}), f32[16,8,128]{2,1,0:T(8,128)S(1)}, u32[]{:S(2)}, u32[]{:S(2)}) %all-to-all-start.7) | async-done | bytes 65568 | tf_op jit(solution)/shard_map/all_to_all | solution.py:1150
  152.5 3.1 %stage_last.1 = (bf16[2,896,128]{2,1,0:T(8,128)(2,1)S(1)}, bf16[2,896,128]{2,1,0:T(8,128)(2,1)S(1)}, f32[8,128]{1,0:T(8,128)S(1)}) custom-call(f32[10]{0:T(128)S(1)} %stack.52.numbers, f32[1,8,128]{2,1,0:T(8,128)} %get-tuple-element.117.refs_5_.refs_0_, f32[16,8,128]{2,1,0:T(8,128)S(1)} %all-to-all-done.7.refs_1_, ...), custom_call_target="tpu_custom_call" | custom-call | tf_op jit(solution)/shard_map/stage_last/pallas_call | solution.py:1131
  158.3 17.7 %all_to_all.53.refs_0_ = bf16[16,112,128]{2,1,0:T(8,128)(2,1)S(1)} all-to-all(bf16[16,112,128]{2,1,0:T(8,128)(2,1)S(1)} %bitcast.14), channel_id=1, replica_groups={{0,2,4,6,8,10,12,14,16,18,20,22,24,26,28,30},{1,3,5,7,9,11,13,15,17,19,..., dimensions={0} | all-to-all | bytes 917504 | tf_op jit(solution)/shard_map/all_to_all | solution.py:1449
  176.6 11.1 %all_to_all.54 = bf16[8,112,128]{2,1,0:T(8,128)(2,1)S(1)} all-to-all(bf16[8,112,128]{2,1,0:T(8,128)(2,1)S(1)} %add_up.1), channel_id=1, replica_groups={{0,2,4,6,8,10,12,14},{1,3,5,7,9,11,13,15},{16,18,20,22,24,26,28,30},{17..., dimensions={0} | all-to-all | bytes 458752 | tf_op jit(solution)/shard_map/all_to_all | solution.py:1452
  (47 shorter events, 21.6 us)
Async XLA Ops:
  5.4 8.9 %collective-permute-start.1 = (bf16[32,3584]{1,0:T(8,128)(2,1)S(1)}, bf16[32,3584]{1,0:T(8,128)(2,1)S(1)}, u32[]{:S(2)}, u32[]{:S(2)}) collective-permute-start(bf16[32,3584]{1,0:T(8,128)(2,1)S(1)} %get-tuple-element.91), channel_id=1, source_target_pairs={{0,1},{1,0},{2,3},{3,2},{4,5},{5,4},{6,7},{7,6},{8,9},{9,8},{10,11... | collective-permute-start | bytes 688136 | tf_op jit(solution)/shard_map/ppermute | solution.py:1159
  5.9 8.4 %collective-permute-start.2 = (bf16[32,3584]{1,0:T(8,128)(2,1)S(1)}, bf16[32,3584]{1,0:T(8,128)(2,1)S(1)}, u32[]{:S(2)}, u32[]{:S(2)}) collective-permute-start(bf16[32,3584]{1,0:T(8,128)(2,1)S(1)} %get-tuple-element.92), channel_id=1, source_target_pairs={{1,2},{2,1},{3,4},{4,3},{5,6},{6,5},{7,8},{8,7},{9,10},{10,9},{11,... | collective-permute-start | bytes 688136 | tf_op jit(solution)/shard_map/ppermute | solution.py:1159
  6.6 5.9 %collective-permute-start = (bf16[640,128]{1,0:T(8,128)(2,1)S(1)}, bf16[640,128]{1,0:T(8,128)(2,1)S(1)}, u32[]{:S(2)}, u32[]{:S(2)}) collective-permute-start(bf16[640,128]{1,0:T(8,128)(2,1)S(1)} %pack_first.1.refs_3_.refs_1_), channel_id=1, source_target_pairs={{0,16},{16,0},{1,17},{17,1},{2,18},{18,2},{3,19},{19,3},{4,20},{20... | collective-permute-start | bytes 491528 | tf_op jit(solution)/shard_map/ppermute | solution.py:1164
  33.1 12.4 %collective-permute-start.3 = (bf16[1872,128]{1,0:T(8,128)(2,1)S(1)}, bf16[1872,128]{1,0:T(8,128)(2,1)S(1)}, u32[]{:S(2)}, u32[]{:S(2)}) collective-permute-start(bf16[1872,128]{1,0:T(8,128)(2,1)S(1)} %pack_rest.1.refs_4_.refs_0_), channel_id=1, source_target_pairs={{0,16},{16,0},{1,17},{17,1},{2,18},{18,2},{3,19},{19,3},{4,20},{20... | collective-permute-start | bytes 1437704 | tf_op jit(solution)/shard_map/ppermute | solution.py:1164
  39.5 10.4 %all-to-all-start.1 = ((f32[16,8,128]{2,1,0:T(8,128)}), f32[16,8,128]{2,1,0:T(8,128)S(1)}, u32[]{:S(2)}, u32[]{:S(2)}) async-start(f32[16,8,128]{2,1,0:T(8,128)} %get-tuple-element.98), calls=%async_computation.1 | async-start | bytes 131072 | tf_op jit(solution)/shard_map/all_to_all | solution.py:1150
  56.0 12.1 %collective-permute-start.5 = (f32[128,512]{1,0:T(8,128)S(1)}, f32[128,512]{1,0:T(8,128)S(1)}, u32[]{:S(2)}, u32[]{:S(2)}) collective-permute-start(f32[128,512]{1,0:T(8,128)S(1)} %get-tuple-element.106), channel_id=1, source_target_pairs={{1,2},{2,1},{3,4},{4,3},{5,6},{6,5},{7,8},{8,7},{9,10},{10,9},{11,... | collective-permute-start | bytes 786440 | tf_op jit(solution)/shard_map/ppermute | solution.py:1159
  56.7 11.5 %collective-permute-start.4 = (f32[128,512]{1,0:T(8,128)S(1)}, f32[128,512]{1,0:T(8,128)S(1)}, u32[]{:S(2)}, u32[]{:S(2)}) collective-permute-start(f32[128,512]{1,0:T(8,128)S(1)} %get-tuple-element.106), channel_id=1, source_target_pairs={{0,1},{1,0},{2,3},{3,2},{4,5},{5,4},{6,7},{7,6},{8,9},{9,8},{10,11... | collective-permute-start | bytes 786440 | tf_op jit(solution)/shard_map/ppermute | solution.py:1159
  68.1 0.7 copy-start
  68.1 0.8 copy-start.1
  89.8 12.4 %collective-permute-start.6 = (bf16[128,768]{1,0:T(8,128)(2,1)S(1)}, bf16[128,768]{1,0:T(8,128)(2,1)S(1)}, u32[]{:S(2)}, u32[]{:S(2)}) collective-permute-start(bf16[128,768]{1,0:T(8,128)(2,1)S(1)} %get-tuple-element.122), channel_id=1, source_target_pairs={{0,1},{1,0},{2,3},{3,2},{4,5},{5,4},{6,7},{7,6},{8,9},{9,8},{10,11... | collective-permute-start | bytes 589832 | tf_op jit(solution)/shard_map/ppermute | solution.py:1159
  89.9 12.3 %collective-permute-start.7 = (bf16[128,768]{1,0:T(8,128)(2,1)S(1)}, bf16[128,768]{1,0:T(8,128)(2,1)S(1)}, u32[]{:S(2)}, u32[]{:S(2)}) collective-permute-start(bf16[128,768]{1,0:T(8,128)(2,1)S(1)} %get-tuple-element.123), channel_id=1, source_target_pairs={{1,2},{2,1},{3,4},{4,3},{5,6},{6,5},{7,8},{8,7},{9,10},{10,9},{11,... | collective-permute-start | bytes 589832 | tf_op jit(solution)/shard_map/ppermute | solution.py:1159
  90.6 11.6 %all-to-all-start.4 = ((f32[16,8,128]{2,1,0:T(8,128)}), f32[16,8,128]{2,1,0:T(8,128)S(1)}, u32[]{:S(2)}, u32[]{:S(2)}) async-start(f32[16,8,128]{2,1,0:T(8,128)} %get-tuple-element.121), calls=%async_computation.4 | async-start | bytes 131072 | tf_op jit(solution)/shard_map/all_to_all | solution.py:1150
  102.2 0.7 copy-start.4
  102.2 0.7 copy-start.5
  109.7 12.4 %collective-permute-start.8 = (bf16[128,768]{1,0:T(8,128)(2,1)S(1)}, bf16[128,768]{1,0:T(8,128)(2,1)S(1)}, u32[]{:S(2)}, u32[]{:S(2)}) collective-permute-start(bf16[128,768]{1,0:T(8,128)(2,1)S(1)} %get-tuple-element.132), channel_id=1, source_target_pairs={{0,1},{1,0},{2,3},{3,2},{4,5},{5,4},{6,7},{7,6},{8,9},{9,8},{10,11... | collective-permute-start | bytes 589832 | tf_op jit(solution)/shard_map/ppermute | solution.py:1159
  109.7 12.3 %collective-permute-start.9 = (bf16[128,768]{1,0:T(8,128)(2,1)S(1)}, bf16[128,768]{1,0:T(8,128)(2,1)S(1)}, u32[]{:S(2)}, u32[]{:S(2)}) collective-permute-start(bf16[128,768]{1,0:T(8,128)(2,1)S(1)} %get-tuple-element.133), channel_id=1, source_target_pairs={{1,2},{2,1},{3,4},{4,3},{5,6},{6,5},{7,8},{8,7},{9,10},{10,9},{11,... | collective-permute-start | bytes 589832 | tf_op jit(solution)/shard_map/ppermute | solution.py:1159
  110.4 11.6 %all-to-all-start.5 = ((f32[16,8,128]{2,1,0:T(8,128)}), f32[16,8,128]{2,1,0:T(8,128)S(1)}, u32[]{:S(2)}, u32[]{:S(2)}) async-start(f32[16,8,128]{2,1,0:T(8,128)} %get-tuple-element.131), calls=%async_computation.5 | async-start | bytes 131072 | tf_op jit(solution)/shard_map/all_to_all | solution.py:1150
  122.1 0.7 copy-start.2
  122.1 0.7 copy-start.3
  127.7 10.4 %all-to-all-start.6 = ((f32[16,8,128]{2,1,0:T(8,128)}), f32[16,8,128]{2,1,0:T(8,128)S(1)}, u32[]{:S(2)}, u32[]{:S(2)}) async-start(f32[16,8,128]{2,1,0:T(8,128)} %get-tuple-element.142), calls=%async_computation.6 | async-start | bytes 131072 | tf_op jit(solution)/shard_map/all_to_all | solution.py:1150
  142.2 10.4 %all-to-all-start.7 = ((f32[16,8,128]{2,1,0:T(8,128)}), f32[16,8,128]{2,1,0:T(8,128)S(1)}, u32[]{:S(2)}, u32[]{:S(2)}) async-start(f32[16,8,128]{2,1,0:T(8,128)} %get-tuple-element.150), calls=%async_computation.7 | async-start | bytes 131072 | tf_op jit(solution)/shard_map/all_to_all | solution.py:1150
  145.7 4.1 %collective-permute-start.10 = (f32[8,128]{1,0:T(8,128)S(1)}, f32[8,128]{1,0:T(8,128)S(1)}, u32[]{:S(2)}, u32[]{:S(2)}) collective-permute-start(f32[8,128]{1,0:T(8,128)S(1)} %get-tuple-element.156.refs_9_), channel_id=1, source_target_pairs={{0,16},{16,0},{1,17},{17,1},{2,18},{18,2},{3,19},{19,3},{4,20},{20... | collective-permute-start | bytes 12296 | tf_op jit(solution)/shard_map/ppermute | solution.py:1387
  155.7 1.9 collective-permute-start.11
  187.7 1.5 collective-permute-start.12

commit v2 on v1

--- a/solution.py
+++ b/solution.py
@@ -72,6 +72,11 @@
                 copy.start()
                 self.started.append(copy)
 
+    def send(self, source, sem):
+        copy = pltpu.make_async_copy(source, self.spot, sem)
+        copy.start()
+        self.started.append(copy)
+
     def finish(self):
         for _, copy in self.copies:
             if not any(copy is other for other in self.started):
@@ -213,7 +218,7 @@
     second = to_row(jnp.sum(second, axis=1, keepdims=True))
     if third is None:
         third = jnp.zeros((1, 128), F32)
-    block = jnp.concatenate([first, second, third, jnp.zeros((5, 128), F32)], axis=0)
+    block = jnp.concatenate([first, second, third, jnp.zeros((1, 128), F32)], axis=0)
     for index in range(ref.shape[0]):
         ref.spot[index] = block
     ref.finish()
@@ -424,7 +429,9 @@
     both(fine_matrix(taps, 64), wout, wout_t)
 
 
-def enter(scal, target, condition, noise, done, own, edge_a, edge_b, scratch, marks):
+def enter(scal, target, condition, noise, done, own, edge_a, edge_b, figures, scratch, marks):
+    values = [jnp.full((1, 128), scal[k], F32) for k in range(6)]
+    give(figures, jnp.concatenate(values + [jnp.zeros((2, 128), F32)], axis=0))
     sigma, skip, in_scale = scal[0], scal[1], scal[3]
     goal = whole(target)
     noisy = goal + sigma * whole(noise)
@@ -503,24 +510,35 @@
     put_stats(stats, total, square)
 
 
-def stage_b(members, scal, stats_a, shift, wfirst, act_a, act_b, stats, kept, hats, passed, totals, sem):
+def slot(ref, index):
+    return ref[:, index * HALF : (index + 1) * HALF]
+
+
+def fill(ref, index, value):
+    ref[:, index * HALF : (index + 1) * HALF] = value
+
+
+def stage_b(
+    members, scal, stats_a, shift, wfirst, act_a,
+    act_b, stats, kept, hats, passed, totals, zs, sems,
+):
+    passed.send(act_a.spot.at[pl.ds(2, 16)], sems.at[0])
     give(totals, total_stats(stats_a)[None])
-    passing = pltpu.make_async_copy(act_a.spot.at[pl.ds(2, 16)], passed.spot, sem)
-    passing.start()
     mean, inverse = norm_columns(stats_a, True, members)
     lift = shift.spot[:, 0:1]
+    for r in range(-6, ROWS + 6):
+        hat = (row(act_a, r) - mean) * inverse
+        fill(zs, r + 6, fine_taps(masked(silu(hat), r, ROWS, scal)))
+        if 0 <= r < ROWS:
+            hats.spot[r] = hat.astype(BF16)
+    hats.finish()
+    kept.send(zs.at[:, pl.ds(6 * HALF, 8 * HALF)], sems.at[1])
+    wfirst.wait(1)
     parts = {}
     total = jnp.zeros((128, HALF), F32)
     square = jnp.zeros((128, HALF), F32)
     for r in range(-6, ROWS + 6):
-        hat = (row(act_a, r) - mean) * inverse
-        z = fine_taps(masked(silu(hat), r, ROWS, scal))
-        if 0 <= r < ROWS:
-            put(kept, r, z)
-            put(hats, r, hat.astype(BF16))
-        if r == -6:
-            wfirst.wait(1)
-        parts[r] = mm(whole(wfirst), z)
+        parts[r] = mm(whole(wfirst), slot(zs, r + 6))
         i = r - 1
         if i > -6:
             value = spread(parts, i, i)[i] + lift
@@ -530,30 +548,28 @@
                 total = total + value
                 square = square + value * value
     put_stats(stats, total, square)
-    passing.wait()
 
 
 def stage_c(
     members, scal, stats_b, wsecond, act_b, act_a, wdown,
-    fine, act_c, edge, stats, kept, kept_pool, hats, totals,
+    fine, act_c, edge, stats, kept, kept_pool, hats, totals, zs, sems,
 ):
     give(totals, total_stats(stats_b)[None])
     mean, inverse = norm_columns(stats_b, True, members)
+    for r in range(-5, ROWS + 5):
+        hat = (row(act_b, r) - mean) * inverse
+        fill(zs, r + 5, fine_taps(masked(silu(hat), r, ROWS, scal)))
+        if -1 <= r <= ROWS:
+            hats.spot[r + 1] = hat.astype(BF16)
+    hats.finish()
+    kept.send(zs.at[:, pl.ds(5 * HALF, 8 * HALF)], sems.at[0])
+    for item in (wsecond, act_a, wdown):
+        item.wait(1)
     parts = {}
     pooled = {}
     half = {}
     for r in range(-5, ROWS + 5):
-        hat = (row(act_b, r) - mean) * inverse
-        z = fine_taps(masked(silu(hat), r, ROWS, scal))
-        if 0 <= r < ROWS:
-            put(kept, r, z)
-        if -1 <= r <= ROWS:
-            put(hats, r, hat.astype(BF16))
-        if r == -5:
-            wsecond.wait(1)
-        if r == -3:
-            act_a.wait(1)
-        parts[r] = mm(whole(wsecond), z)
+        parts[r] = mm(whole(wsecond), slot(zs, r + 5))
         i = r - 1
         if i > -5:
             value = spread(parts, i, i)[i] + row(act_a, i)
@@ -565,7 +581,6 @@
                 value = 0.25 * (half.pop(i - 1) + half.pop(i))
                 value = masked(value, i // 2, CROWS, scal)
                 pooled[i // 2] = value.astype(BF16).astype(F32)
-    wdown.wait(1)
     weights = whole(wdown)
     parts = {}
     total = jnp.zeros((128, HALF), F32)
@@ -590,7 +605,7 @@
 
 def stage_d(
     members, scal, stats_c, wcoarse, got_a, got_b, act_c, wup, fine,
-    merged, hats, stats, kept_c, kept_up, totals,
+    merged, hats, stats, kept_c, kept_up, totals, zs, sems,
 ):
     give(totals, total_stats(stats_c)[None])
     mean, inverse = norm_columns(stats_c, False, members)
@@ -600,24 +615,24 @@
         ring[CROWS + 1 + j] = pick(scal, row(got_b, j), row(got_a, j))
     for j in range(-1, CROWS + 1):
         ring[j] = row(act_c, j)
+    for r in range(-3, CROWS + 3):
+        hat = (ring[r] - mean) * inverse
+        fill(zs, r + 3, coarse_taps(masked(silu(hat), r, CROWS, scal)))
+        if -2 <= r < CROWS + 2:
+            hats.spot[r + 2] = hat.astype(BF16)
+    hats.finish()
+    kept_c.send(zs.at[:, pl.ds(3 * HALF, 4 * HALF)], sems.at[0])
+    wcoarse.wait(1)
+    wup.wait(1)
     parts = {}
     lifted = {}
     for r in range(-3, CROWS + 3):
-        hat = (ring[r] - mean) * inverse
-        z = coarse_taps(masked(silu(hat), r, CROWS, scal))
-        if 0 <= r < CROWS:
-            put(kept_c, r, z)
-        if -2 <= r < CROWS + 2:
-            put(hats, r, hat.astype(BF16))
-        if r == -3:
-            wcoarse.wait(1)
-        parts[r] = mm(whole(wcoarse), z)
+        parts[r] = mm(whole(wcoarse), slot(zs, r + 3))
         i = r - 1
         if i > -3:
             value = spread(parts, i, i)[i] + ring[i]
             del parts[i - 1]
             lifted[i] = masked(value, i, CROWS, scal).astype(BF16).astype(F32)
-    wup.wait(1)
     weights = whole(wup)
     parts = {}
     total = jnp.zeros((128, HALF), F32)
@@ -640,25 +655,24 @@
 
 
 def stage_out(
-    members, scal, stats_d, wout, merged, line_a, line_b, target, noise, wout_t,
-    denoised, back, edge_a, edge_b, stats, hats, cotangents, zs, totals, pairs, cells,
-    goals, noisies, found,
+    members, scal, stats_d, wout, merged, line_a, line_b, target, noise, wout_t, figures,
+    denoised, back, edge_a, edge_b, stats, hats, cotangents, kept, totals, pairs, cells,
+    goals, noisies, found, zs, sems,
 ):
     give(totals, total_stats(stats_d)[None])
-    sigma, skip, out_scale, weight, coef = scal[0], scal[1], scal[2], scal[4], scal[5]
     mean, inverse = norm_columns(stats_d, True, members)
-    parts = {}
     for r in range(-3, ROWS + 3):
         hat = (row(merged, r) - mean) * inverse
-        put(hats, r, hat.astype(BF16))
-        if r == -3 or r == ROWS + 2:
-            continue
-        z = fine_taps(masked(silu(hat), r, ROWS, scal))
-        if 0 <= r < ROWS:
-            put(zs, r, z)
-        if r == -2:
-            wout.wait(1)
-        parts[r] = mm(whole(wout), z)
+        hats.spot[r + 3] = hat.astype(BF16)
+        if -3 < r < ROWS + 2:
+            fill(zs, r + 2, fine_taps(masked(silu(hat), r, ROWS, scal)))
+    hats.finish()
+    kept.send(zs.at[:, pl.ds(2 * HALF, 8 * HALF)], sems.at[0])
+    for item in (wout, line_a, line_b, target, noise, wout_t, figures):
+        item.wait(1)
+    parts = {}
+    for r in range(-2, ROWS + 2):
+        parts[r] = mm(whole(wout), slot(zs, r + 2))
         i = r - 1
         if i > -2:
             value = spread(parts, i, i)[i]
@@ -670,8 +684,9 @@
     high = value.astype(BF16)
     low = (value - high.astype(F32)).astype(BF16)
     back_order = interleave(True)
-    for item in (line_a, line_b, target, noise, wout_t):
-        item.wait(1)
+    sigma, skip, out_scale, weight, coef = [
+        figures.spot[k : k + 1, 0:1] for k in (0, 1, 2, 4, 5)
+    ]
     pairs[...] = mm(high, back_order) + mm(low, back_order)
     blank = jnp.zeros((4, 512), F32)
     loss_sum = jnp.zeros((12, 512), F32)
@@ -791,7 +806,7 @@
 def stage_up(
     members, members_c, scal, stats_d, stats_ed, got_a, got_b, hats, back, wup_t, stats_c, hats_c,
     wcoarse_t, done,
-    grad_merged, back_c, grad_coarse, edge_a, edge_b, stats, loss,
+    grad_merged, back_c, grad_coarse, edge_a, edge_b, stats, loss, total_next,
 ):
     give(loss, jnp.broadcast_to(total_stats(stats_ed)[2:3, :], (8, 128)))
     mean, inverse = norm_columns(stats_d, True, members)
@@ -840,12 +855,13 @@
         put(edge_a, j, pick(scal, top[j], low[j]))
         put(edge_b, j, pick(scal, low[j], top[j]))
     put_stats(stats, total, cross)
+    give(total_next, whole(stats_c))
 
 
 def stage_down(
     members, members_c, scal, stats_c, stats_ec, got_a, got_b, hats_c, back_c, grad_coarse,
     wdown_t, grad_merged, stats_b, wsecond_t, hats, done,
-    grad_fine, back_b, stats, grad_c,
+    grad_fine, back_b, stats, grad_c, total_next,
 ):
     mean, inverse = norm_columns(stats_c, False, members_c)
     shift, slope = back_columns(stats_ec, False, members_c)
@@ -881,6 +897,7 @@
                 put(grad_fine, i, fine[i])
     wsecond_t.wait(1)
     hats.wait(1)
+    stats_b.wait(1)
     weights = whole(wsecond_t)
     mean, inverse = norm_columns(stats_b, True, members)
     total = jnp.zeros((128, HALF), F32)
@@ -894,11 +911,12 @@
             total = total + e
             cross = cross + e * hat
     put_stats(stats, total, cross)
+    give(total_next, whole(stats_b))
 
 
 def stage_first(
     members, scal, stats_b, stats_eb, hats_b, back_b, wfirst_t, stats_a, hats, done,
-    back_a, stats, grad_b, line,
+    back_a, stats, grad_b, line, total_next,
 ):
     mean, inverse = norm_columns(stats_b, True, members)
     shift, slope = back_columns(stats_eb, True, members)
@@ -914,6 +932,7 @@
         put(grad_b, r, g[r])
     wfirst_t.wait(1)
     hats.wait(1)
+    stats_a.wait(1)
     weights = whole(wfirst_t)
     total = jnp.zeros((128, HALF), F32)
     cross = jnp.zeros((128, HALF), F32)
@@ -927,6 +946,7 @@
     put_stats(stats, total, cross)
     sums = to_row(jnp.sum(sums, axis=1, keepdims=True))
     give(line, jnp.broadcast_to(sums, (8, 128)))
+    give(total_next, whole(stats_a))
 
 
 def stage_last(
@@ -1058,9 +1078,21 @@
     return saved, item, 0
 
 
+def position():
+    me, bands = lax.axis_index("rows"), lax.axis_size("rows")
+    return {
+        6: jnp.where(me > 0, 1.0, 0.0),
+        7: jnp.where(me < bands - 1, 1.0, 0.0),
+        8: jnp.where(me % 2 == 1, 1.0, 0.0),
+        9: jnp.where(lax.axis_index("fsdp") == 0, 1.0, 0.0),
+    }
+
+
 def run(name, kernel, outs, scal, *operands, scratch=()):
     vmem, hbm = pl.BlockSpec(memory_space=pltpu.VMEM), pl.BlockSpec(memory_space=pltpu.HBM)
-    in_specs, arrays, plans, spots = [pl.BlockSpec(memory_space=pltpu.SMEM)], [scal], [], []
+    in_specs, arrays, plans, spots = [], [], [], []
+    if scal is not None:
+        in_specs, arrays = [pl.BlockSpec(memory_space=pltpu.SMEM)], [scal]
     for item in operands:
         saved, item, first = opened(item)
         if saved is None:
@@ -1102,7 +1134,11 @@
         plans.append((first, (last, None), len(spots)))
         spots.append(pltpu.VMEM(item.shape, item.dtype))
 
-    def body(numbers, *refs):
+    def body(*refs):
+        numbers = position()
+        if scal is not None:
+            numbers.update({index: refs[0][index] for index in range(6)})
+            refs = refs[1:]
         given, refs = refs[: len(plans)], refs[len(plans) :]
         held, refs = refs[: len(spots)], refs[len(spots) :]
         sems, extra = refs[0], refs[1:]
@@ -1188,23 +1224,9 @@
     members = 2 * ROWS * 2 * HALF * bands
     members_c = 4 * CROWS * HALF * bands
     members_all = count * residual_target.size * bands
-    me = lax.axis_index("rows")
     sigma_level, skip_scale, out_scale, in_scale, weight = preconditions(noise_level[0])
     coef = 2.0 * weight * out_scale / members_all
-    scal = jnp.stack(
-        [
-            sigma_level,
-            skip_scale,
-            out_scale,
-            in_scale,
-            weight,
-            coef,
-            (me > 0).astype(F32),
-            (me < bands - 1).astype(F32),
-            (me % 2).astype(F32),
-            (lax.axis_index("fsdp") == 0).astype(F32),
-        ]
-    )
+    scal = jnp.stack([sigma_level, skip_scale, out_scale, in_scale, weight, coef])
     embedded = embedding(sigma_level, embed_matrix.shape[0] * count)
     target = residual_target.reshape(12 * ROWS, 512)
     condition = conditioning.reshape(12 * ROWS, 512)
@@ -1220,7 +1242,7 @@
             name,
             functools.partial(pack, widths),
             [shape(total, 128, dtype=BF16)],
-            scal,
+            None,
             *[Saved(item) for item in shards],
             *after,
             scratch=[((total, 128), F32)],
@@ -1236,10 +1258,10 @@
     )
     early = gather_packed(early_packed)
     far = shape(32, FAR * 512, dtype=BF16)
-    own, edge_a, edge_b = run(
+    own, edge_a, edge_b, figures = run(
         "enter",
         enter,
-        [shape(32, ROWS * 512, dtype=BF16), far, far],
+        [shape(32, ROWS * 512, dtype=BF16), far, far, Saved(shape(8, 128))],
         scal,
         Saved(target),
         Saved(condition),
@@ -1262,11 +1284,11 @@
             shape(384, 128, dtype=BF16), Saved(shape(384, 256, dtype=BF16)),
             Saved(shape(256, 384, dtype=BF16)), shape(128, 128),
         ],
-        scal,
+        None,
         vector, *early,
     )
-    stat = shape(bands, 8, 128)
-    total = Saved(shape(1, 8, 128))
+    stat = shape(bands, 4, 128)
+    total = Saved(shape(1, 4, 128))
     act_a, stats_a, kept_in, line_a, line_b = run(
         "stage_a",
         stage_a,
@@ -1274,7 +1296,7 @@
             rows_of(-6, 20), stat, Saved(flat_rows(-1, 10, 128)),
             Saved(shape(16, 512)), Saved(shape(16, 512)),
         ],
-        scal,
+        None,
         win, got_a, got_b, own, rest,
         scratch=[((32, FAR * 512), BF16), ((32, FAR * 512), BF16)],
     )
@@ -1292,7 +1314,7 @@
             Saved(shape(384, 512, dtype=BF16)), Saved(shape(512, 384, dtype=BF16)),
             Saved(shape(96, 256, dtype=BF16)), Saved(shape(256, 96, dtype=BF16)),
         ],
-        scal,
+        None,
         *gather_packed(rest),
     )
 
@@ -1300,12 +1322,13 @@
         "stage_b",
         functools.partial(stage_b, members),
         [
-            rows_of(-5, 18), stat, Saved(flat_rows(0, 8, 256)), Saved(rows_of(0, 8, BF16)),
+            rows_of(-5, 18), stat, Saved(flat_rows(0, 8, 256), when=None),
+            Saved(rows_of(0, 8, BF16)),
             Saved(rows_of(-4, 16), when=None), total,
         ],
-        scal,
+        None,
         stats_a, shift, Saved(wfirst, when=1), act_a,
-        scratch=[pltpu.SemaphoreType.DMA(())],
+        scratch=[((256, 20 * HALF), BF16), pltpu.SemaphoreType.DMA((2,))],
     )
     stats_b = sum_parts(stats_b)
     fine, act_c, edge, stats_c, kept_b, kept_pool, hats_b, total_b = run(
@@ -1313,11 +1336,12 @@
         functools.partial(stage_c, members),
         [
             rows_of(-3, 14), rows_of(-1, 6), Field(shape(128, 2 * HALF), 1), stat,
-            Saved(flat_rows(0, 8, 256)), Saved(flat_rows(0, 4, 192)), Saved(rows_of(-1, 10, BF16)),
-            total,
+            Saved(flat_rows(0, 8, 256), when=None), Saved(flat_rows(0, 4, 192)),
+            Saved(rows_of(-1, 10, BF16)), total,
         ],
-        scal,
+        None,
         stats_b, Saved(wsecond, when=1), act_b, Saved(act_a, when=1), Saved(wdown, when=1),
+        scratch=[((256, 18 * HALF), BF16), pltpu.SemaphoreType.DMA((1,))],
     )
     got_a, got_b = swap(edge.array, edge.array)
     stats_c = sum_parts(stats_c)
@@ -1326,10 +1350,11 @@
         functools.partial(stage_d, members_c),
         [
             rows_of(-3, 14), Saved(rows_of(-2, 8, BF16)), stat,
-            Saved(flat_rows(0, 4, 384)), Saved(flat_rows(0, 4, 384)), total,
+            Saved(flat_rows(0, 4, 384), when=None), Saved(flat_rows(0, 4, 384)), total,
         ],
-        scal,
-        stats_c, Saved(wcoarse), Saved(got_a), Saved(got_b), act_c, Saved(wup), fine,
+        None,
+        stats_c, Saved(wcoarse, when=1), got_a, got_b, act_c, Saved(wup, when=1), fine,
+        scratch=[((384, 10 * HALF), BF16), pltpu.SemaphoreType.DMA((1,))],
     )
     stats_d = sum_parts(stats_d)
     edge = Field(shape(128, 3 * HALF, dtype=BF16), 0)
@@ -1339,14 +1364,17 @@
         [
             Saved(shape(96, 512)), rows_of(0, 8, BF16), edge, edge, stat,
             Saved(rows_of(-3, 14, BF16)),
-            Field(shape(10, 32, HALF, dtype=BF16), -1), Saved(flat_rows(0, 8, 256)), total,
+            Field(shape(10, 32, HALF, dtype=BF16), -1),
+            Saved(flat_rows(0, 8, 256), when=None), shape(1, 4, 128),
         ],
-        scal,
+        None,
         stats_d, Saved(wout, when=1), merged, Saved(line_a, when=1), Saved(line_b, when=1),
         Saved(target, when=1), Saved(noise, when=1), Saved(wout_t, when=1),
+        Saved(figures, when=1),
         scratch=[
             ((160, 512), F32), ((160, 512), F32),
             ((4, 96, 128), F32), ((4, 96, 128), F32), ((4, 96, 128), F32),
+            ((256, 12 * HALF), BF16), pltpu.SemaphoreType.DMA((1,)),
         ],
     )
     got_a, got_b = swap(edge_a.array, edge_b.array)
@@ -1354,20 +1382,20 @@
         "grads_out",
         grads_out,
         [Saved(shape(count, 80, 128, dtype=BF16))],
-        scal,
+        None,
         cotangents, Saved(kept_d),
         scratch=[((96, 8 * HALF), BF16)],
     )
     stats_ed = sum_parts(stats_ed)
-    grad_merged, back_c, grad_coarse, edge_a, edge_b, stats_ec, loss = run(
+    grad_merged, back_c, grad_coarse, edge_a, edge_b, stats_ec, loss, total_c = run(
         "stage_up",
         functools.partial(stage_up, members, members_c),
         [
             rows_of(-2, 12, BF16), rows_of(0, 4, BF16), rows_of(-1, 6, BF16), edge, edge, stat,
-            shape(8, 128),
+            shape(8, 128), shape(1, 4, 128),
         ],
-        scal,
-        Saved(total_d), stats_ed, Saved(got_a), Saved(got_b), Saved(hats_d), back_d, Saved(wup_t, when=1),
+        None,
+        total_d, stats_ed, got_a, got_b, Saved(hats_d), back_d, Saved(wup_t, when=1),
         Saved(total_c, when=1),
         Saved(hats_c, when=1), Saved(wcoarse_t, when=1), Saved(grad_out, when=None),
     )
@@ -1376,7 +1404,7 @@
         "grads_up",
         grads_up,
         [Saved(group_shape(9 * (fine_o + coarse_o) + 80, count))],
-        scal,
+        None,
         grad_merged, grad_coarse, Saved(kept_up), Saved(kept_c), Saved(grad_out),
         scratch=[
             ((384, 8 * HALF), BF16), ((384, 8 * HALF), BF16), ((384, 4 * HALF), BF16)
@@ -1387,37 +1415,43 @@
         loss_other = lax.ppermute(loss, "fsdp", [(0, 1), (1, 0)])
     else:
         loss_other = lax.psum(loss, "fsdp") - loss
-    grad_fine, back_b, stats_eb, grad_c = run(
+    grad_fine, back_b, stats_eb, grad_c, total_b = run(
         "stage_down",
         functools.partial(stage_down, members, members_c),
-        [rows_of(-1, 10, BF16), rows_of(-1, 10, BF16), stat, rows_of(-1, 6, BF16)],
-        scal,
-        Saved(total_c), stats_ec, Saved(got_a), Saved(got_b), Saved(hats_c), back_c, grad_coarse,
-        Saved(wdown_t, when=1), grad_merged, Saved(total_b), Saved(wsecond_t, when=1),
+        [
+            rows_of(-1, 10, BF16), rows_of(-1, 10, BF16), stat, rows_of(-1, 6, BF16),
+            shape(1, 4, 128),
+        ],
+        None,
+        total_c, stats_ec, got_a, got_b, Saved(hats_c), back_c, grad_coarse,
+        Saved(wdown_t, when=1), grad_merged, Saved(total_b, when=1), Saved(wsecond_t, when=1),
         Saved(hats_b, 0, 8, when=1), Saved(early, when=None),
     )
     (middle,) = run(
         "grads_down",
         grads_down,
         [Saved(group_shape(5 * (fine_o + coarse_o), count))],
-        scal,
+        None,
         grad_fine, grad_c, Saved(kept_pool), Saved(kept_b),
         scratch=[((384, 8 * HALF), BF16), ((384, 4 * HALF), BF16)],
     )
     stats_eb = sum_parts(stats_eb)
-    back_a, stats_ea, grad_b, line = run(
+    back_a, stats_ea, grad_b, line, total_a = run(
         "stage_first",
         functools.partial(stage_first, members),
-        [rows_of(0, 8, BF16), stat, rows_of(-1, 10, BF16), shape(8, 128)],
-        scal,
-        Saved(total_b), stats_eb, Saved(hats_b), back_b, Saved(wfirst_t, when=1), Saved(total_a),
+        [
+            rows_of(0, 8, BF16), stat, rows_of(-1, 10, BF16), shape(8, 128),
+            shape(1, 4, 128),
+        ],
+        None,
+        total_b, stats_eb, Saved(hats_b), back_b, Saved(wfirst_t, when=1), Saved(total_a, when=1),
         Saved(hats_a, when=1), Saved(middle, when=None),
     )
     (grad_first,) = run(
         "grads_first",
         grads_first,
         [Saved(shape(count, 5 * fine_o + embed_matrix.shape[0], 128, dtype=BF16))],
-        scal,
+        None,
         grad_b, line, vector, Saved(kept_a),
         scratch=[((384, 8 * HALF), BF16)],
     )
@@ -1432,8 +1466,8 @@
         "stage_last",
         functools.partial(stage_last, members),
         [half, half, shape(8, 128)],
-        scal,
-        Saved(total_a), stats_ea, Saved(hats_a), back_a, grad_fine, Saved(kept_in, when=1),
+        None,
+        total_a, stats_ea, Saved(hats_a), back_a, grad_fine, Saved(kept_in, when=1),
         Saved(early, when=None), Saved(middle, when=None), Saved(grad_first, when=1), loss, loss_other,
         scratch=[
             ((128, 8 * HALF), BF16), ((count, chunk * bands, 128), BF16),
@@ -1443,11 +1477,11 @@
     loss_value = loss[0, 0] / members_all
     pairs = [(i, i ^ 1) for i in range(bands)]
     got = lax.ppermute(send, "rows", pairs)
-    (both,) = run("join", join, [half], scal, keep, got)
+    (both,) = run("join", join, [half], None, keep, got)
     both = both.reshape(count * chips, chunk, 128)
     cores = [[f * bands + r for f in range(count) for r in range(c, bands, 2)] for c in range(2)]
     got = lax.all_to_all(both, ("fsdp", "rows"), 0, 0, axis_index_groups=cores)
-    (mine,) = run("add_up", add_up, [shape(chips, chunk, 128, dtype=BF16)], scal, got)
+    (mine,) = run("add_up", add_up, [shape(chips, chunk, 128, dtype=BF16)], None, got)
     cores = [[r for r in range(c, bands, 2)] for c in range(2)]
     mine = lax.all_to_all(mine, "rows", 0, 0, axis_index_groups=cores)
     mine = mine.reshape(chips * chunk, 128)
@@ -1465,7 +1499,7 @@
             shape(*embed_matrix.shape),
             shape(*inputs_t.shape),
         ],
-        scal,
+        None,
         mine, other,
         scratch=[((chunk * bands, 128), F32)],
     )

time: 193 us -> 184 us (0.953)
  Pallas kernels: 71.4 us -> 60.6 us
    pallas_call x21, Pallas kernels: 71.4 us -> 60.6 us  [run(): pl.pallas_call(body, out_shape=tuple(out_shapes), in_specs=in_specs, out_...]
    ppermute x2, waiting for transfers between devices: 3.74 us -> 5.95 us  [gather_packed(): return [packed, lax.ppermute(packed, 'fsdp', [(0, 1), (1, 0)])]]
  transfers between devices with their start and end apart: 18 -> 18, of which waited for: 9 -> 8; matrix products, arithmetic and copies ran while one was open for 0% -> 0% of each run, Pallas kernels for 13% -> 11%
where the time goes in v2:
time: 184 us; the launch traced here: 183 us
  blocking collectives  63.2 us (34%)
  Pallas kernels  60.6 us (33%)
  starting transfers between devices  31.2 us (17%)
  waiting for transfers between devices  21.3 us (12%)
  between operations  3.61 us (2%)
  local copies, waits for them, and re-layouts  2.58 us (1%)
    pallas_call x21, Pallas kernels, run(): pl.pallas_call(body, out_shape=tuple(out_shapes), in_specs=in_specs, out_...  60.6 us
    all_to_all x3, blocking collectives, sum_parts(): return lax.all_to_all(stats, 'rows', 0, 0)  34.2 us
    all_to_all x5, starting transfers between devices, sum_parts(): return lax.all_to_all(stats, 'rows', 0, 0)  20 us
    all_to_all x1, blocking collectives, per_device(): got = lax.all_to_all(both, ('fsdp', 'rows'), 0, 0, axis_index_groups=cores)  17.9 us
    all_to_all x5, waiting for transfers between devices, sum_parts(): return lax.all_to_all(stats, 'rows', 0, 0)  13.2 us
    all_to_all x1, blocking collectives, per_device(): mine = lax.all_to_all(mine, 'rows', 0, 0, axis_index_groups=cores)  11.1 us
    ppermute x2, waiting for transfers between devices, gather_packed(): return [packed, lax.ppermute(packed, 'fsdp', [(0, 1), (1, 0)])]  5.95 us
    ppermute x2, starting transfers between devices, gather_packed(): return [packed, lax.ppermute(packed, 'fsdp', [(0, 1), (1, 0)])]  4.06 us
  transfers between devices with their start and end apart: 18, of which 8 were waited for; matrix products, arithmetic and copies ran while one was open for 0% of the time, Pallas kernels for 11%

profile of v2, /device:TPU:0, one launch (start us, length us, event | category | flops | bytes accessed | tf_op | source)
XLA Modules:
  0.0 182.7 jit_solution(11094648881329610715)
XLA Ops:
  2.8 2.6 %enter.1 = (bf16[32,4096]{1,0:T(8,128)(2,1)S(1)}, bf16[32,3584]{1,0:T(8,128)(2,1)S(1)}, bf16[32,3584]{1,0:T(8,128)(2,1)S(1)}, f32[8,128]{1,0:T(8,128)}) custom-call(f32[6]{0:T(128)S(1)} %stack.24.refs_0_, f32[96,512]{1,0:T(8,128)} %bitcast.13, f32[96,512]{1,0:T(8,128)} %bitcast.17, f32[96,512]{1,0:T(8,128)} %bitcast.15, ...), custom_call_target="tpu_custom_call" | custom-call | tf_op jit(solution)/shard_map/enter/pallas_call | solution.py:1167
  6.5 2.6 %collective-permute-start = (bf16[640,128]{1,0:T(8,128)(2,1)S(1)}, bf16[640,128]{1,0:T(8,128)(2,1)S(1)}, u32[]{:S(2)}, u32[]{:S(2)}) collective-permute-start(bf16[640,128]{1,0:T(8,128)(2,1)S(1)} %pack_first.1.refs_4_.refs_1_), channel_id=1, source_target_pairs={{0,16},{16,0},{1,17},{17,1},{2,18},{18,2},{3,19},{19,3},{4,20},{20... | collective-permute-start | bytes 491528 | tf_op jit(solution)/shard_map/ppermute | solution.py:1200
  13.7 2.3 %stage_a.1 = (f32[20,128,256]{2,1,0:T(8,128)S(1)}, f32[16,4,128]{2,1,0:T(4,128)S(1)}, bf16[128,2560]{1,0:T(8,128)(2,1)}, f32[16,512]{1,0:T(8,128)}, f32[16,512]{1,0:T(8,128)}) custom-call(bf16[384,128]{1,0:T(8,128)(2,1)S(1)} %get-tuple-element.94.refs_0_, bf16[32,3584]{1,0:T(8,128)(2,1)S(1)} %collective-permute-done.1.refs_1_, ...), custom_call_target="tpu_custom_call" | custom-call | tf_op jit(solution)/shard_map/stage_a/pallas_call | solution.py:1167
  16.1 15.6 %all_to_all.50.refs_0_ = f32[16,4,128]{2,1,0:T(4,128)S(1)} all-to-all(f32[16,4,128]{2,1,0:T(4,128)S(1)} %get-tuple-element.97), channel_id=1, replica_groups=mesh['fsdp'=2,'rows'=16] {'rows'}, dimensions={0} | all-to-all | bytes 65536 | tf_op jit(solution)/shard_map/all_to_all | solution.py:1186
  33.2 3.4 %stage_b.1 = (f32[18,128,256]{2,1,0:T(8,128)S(1)}, f32[16,4,128]{2,1,0:T(4,128)}, bf16[256,2048]{1,0:T(8,128)(2,1)}, bf16[8,128,256]{2,1,0:T(8,128)(2,1)}, f32[1...) custom-call(f32[16,4,128]{2,1,0:T(4,128)S(1)} %all_to_all.50.refs_0_, f32[128,128]{1,0:T(8,128)S(1)} %get-tuple-element.99.refs_1_, ...), custom_call_target="tpu_custom_call" | custom-call | tf_op jit(solution)/shard_map/stage_b/pallas_call | solution.py:1167
  36.6 3.5 %all-to-all-start.1 = ((f32[16,4,128]{2,1,0:T(4,128)}), f32[16,4,128]{2,1,0:T(4,128)S(1)}, u32[]{:S(2)}, u32[]{:S(2)}) async-start(f32[16,4,128]{2,1,0:T(4,128)} %get-tuple-element.102), calls=%async_computation.1 | async-start | bytes 65536 | tf_op jit(solution)/shard_map/all_to_all | solution.py:1186
  40.1 4.2 %collective-permute-done.3.refs_1_ = bf16[1872,128]{1,0:T(8,128)(2,1)S(1)} collective-permute-done((bf16[1872,128]{1,0:T(8,128)(2,1)S(1)}, bf16[1872,128]{1,0:T(8,128)(2,1)S(1)}, u32[]{:S(2)}, u32[]{:S(2)}) %collective-permute-start.3) | collective-permute-done | bytes 479264 | tf_op jit(solution)/shard_map/ppermute | solution.py:1200
  44.3 2.6 %prepare_rest.1 = (bf16[384,256]{1,0:T(8,128)(2,1)}, bf16[256,384]{1,0:T(8,128)(2,1)}, bf16[384,192]{1,0:T(8,128)(2,1)}, bf16[192,384]{1,0:T(8,128)(2,1)}, bf16[...) custom-call(bf16[1872,128]{1,0:T(8,128)(2,1)S(1)} %pack_rest.1.refs_, ...), custom_call_target="tpu_custom_call" | custom-call | tf_op jit(solution)/shard_map/prepare_rest/pallas_call | solution.py:1167
  46.9 6.0 %stage_c.1 = (f32[14,128,256]{2,1,0:T(8,128)S(1)}, f32[6,128,256]{2,1,0:T(8,128)S(1)}, f32[128,512]{1,0:T(8,128)S(1)}, f32[16,4,128]{2,1,0:T(4,128)S(1)}, bf16[2...) custom-call(f32[16,4,128]{2,1,0:T(4,128)S(1)} %all-to-all-done.1.refs_0_,, ...), custom_call_target="tpu_custom_call" | custom-call | tf_op jit(solution)/shard_map/stage_c/pallas_call | solution.py:1167
  53.6 2.2 %collective-permute-start.4 = (f32[128,512]{1,0:T(8,128)S(1)}, f32[128,512]{1,0:T(8,128)S(1)}, u32[]{:S(2)}, u32[]{:S(2)}) collective-permute-start(f32[128,512]{1,0:T(8,128)S(1)} %get-tuple-element.110), channel_id=1, source_target_pairs={{0,1},{1,0},{2,3},{3,2},{4,5},{5,4},{6,7},{7,6},{8,9},{9,8},{10,11... | collective-permute-start | bytes 786440 | tf_op jit(solution)/shard_map/ppermute | solution.py:1195
  55.8 9.4 %all_to_all.51.refs_0_ = f32[16,4,128]{2,1,0:T(4,128)S(1)} all-to-all(f32[16,4,128]{2,1,0:T(4,128)S(1)} %get-tuple-element.108), channel_id=1, replica_groups=mesh['fsdp'=2,'rows'=16] {'rows'}, dimensions={0} | all-to-all | bytes 65536 | tf_op jit(solution)/shard_map/all_to_all | solution.py:1186
  65.1 5.6 %stage_d.1 = (f32[14,128,256]{2,1,0:T(8,128)S(1)}, bf16[8,128,256]{2,1,0:T(8,128)(2,1)}, f32[16,4,128]{2,1,0:T(4,128)S(1)}, bf16[384,1024]{1,0:T(8,128)(2,1)}, b...) custom-call(f32[16,4,128]{2,1,0:T(4,128)S(1)} %all_to_all.51.refs_0_, bf16[384,384]{1,0:T(8,128)(2,1)} %get-tuple-element.109.refs_1_, ...), custom_call_target="tpu_custom_call" | custom-call | tf_op jit(solution)/shard_map/stage_d/pallas_call | solution.py:1167
  70.8 9.2 %all_to_all.52.refs_0_ = f32[16,4,128]{2,1,0:T(4,128)S(1)} all-to-all(f32[16,4,128]{2,1,0:T(4,128)S(1)} %get-tuple-element.114), channel_id=1, replica_groups=mesh['fsdp'=2,'rows'=16] {'rows'}, dimensions={0} | all-to-all | bytes 65536 | tf_op jit(solution)/shard_map/all_to_all | solution.py:1186
  80.0 5.7 %stage_out.1 = (f32[96,512]{1,0:T(8,128)}, bf16[8,128,256]{2,1,0:T(8,128)(2,1)S(1)}, bf16[128,768]{1,0:T(8,128)(2,1)S(1)}, bf16[128,768]{1,0:T(8,128)(2,1)S(1)},...) custom-call(f32[16,4,128]{2,1,0:T(4,128)S(1)} %all_to_all.52.refs_0_, ...), custom_call_target="tpu_custom_call" | custom-call | tf_op jit(solution)/shard_map/stage_out/pallas_call | solution.py:1167
  86.5 4.7 %all-to-all-start.4 = ((f32[16,4,128]{2,1,0:T(4,128)}), f32[16,4,128]{2,1,0:T(4,128)S(1)}, u32[]{:S(2)}, u32[]{:S(2)}) async-start(f32[16,4,128]{2,1,0:T(4,128)} %get-tuple-element.123), calls=%async_computation.4 | async-start | bytes 65536 | tf_op jit(solution)/shard_map/all_to_all | solution.py:1186
  91.2 2.4 %grads_out.1.refs_10_.refs_4_ = bf16[2,80,128]{2,1,0:T(8,128)(2,1)} custom-call(bf16[10,32,256]{2,1,0:T(8,128)(2,1)S(1)} %get-tuple-element.132.refs_0_, bf16[256,2048]{1,0:T(8,128)(2,1)} %get-tuple-element.133.refs_1_), custom_call_target="tpu_custom_call" | custom-call | tf_op jit(solution)/shard_map/grads_out/pallas_call | solution.py:1167
  93.7 4.2 %all-to-all-done.4.refs_1_ = f32[16,4,128]{2,1,0:T(4,128)S(1)} async-done(((f32[16,4,128]{2,1,0:T(4,128)}), f32[16,4,128]{2,1,0:T(4,128)S(1)}, u32[]{:S(2)}, u32[]{:S(2)}) %all-to-all-start.4) | async-done | bytes 32800 | tf_op jit(solution)/shard_map/all_to_all | solution.py:1186
  97.8 5.9 %stage_up.1 = (bf16[12,128,256]{2,1,0:T(8,128)(2,1)S(1)}, bf16[4,128,256]{2,1,0:T(8,128)(2,1)S(1)}, bf16[6,128,256]{2,1,0:T(8,128)(2,1)S(1)}, bf16[128,768]{1,0:...) custom-call(f32[1,4,128]{2,1,0:T(4,128)S(1)} %get-tuple-element.122., ...), custom_call_target="tpu_custom_call" | custom-call | tf_op jit(solution)/shard_map/stage_up/pallas_call | solution.py:1167
  104.5 4.8 %all-to-all-start.5 = ((f32[16,4,128]{2,1,0:T(4,128)}), f32[16,4,128]{2,1,0:T(4,128)S(1)}, u32[]{:S(2)}, u32[]{:S(2)}) async-start(f32[16,4,128]{2,1,0:T(4,128)} %get-tuple-element.135), calls=%async_computation.5 | async-start | bytes 65536 | tf_op jit(solution)/shard_map/all_to_all | solution.py:1186
  109.3 3.6 %grads_up.1.refs_12_.refs_6_ = bf16[2,944,128]{2,1,0:T(8,128)(2,1)} custom-call(bf16[12,128,256]{2,1,0:T(8,128)(2,1)S(1)} %get-tuple-element.141.refs_0_.refs_8_, bf16[6,128,256]{2,1,0:T(8,128)(2,1)S(1)} %get-tuple-element.139.refs_1_.refs_6_, bf16[384,1024]{1,0:T(8,128)(2,1)} %get-tuple-element.145.refs_2_, bf16[384,1024]{1,0:T(8,128)(2,1)} %get-tuple-element.146.refs_3_, ...), custom_call_target="tpu_custom_call" | custom-call | tf_op jit(solution)/shard_map/grads_up/pallas_call | solution.py:1167
  112.9 3.0 %all-to-all-done.5.refs_1_ = f32[16,4,128]{2,1,0:T(4,128)S(1)} async-done(((f32[16,4,128]{2,1,0:T(4,128)}), f32[16,4,128]{2,1,0:T(4,128)S(1)}, u32[]{:S(2)}, u32[]{:S(2)}) %all-to-all-start.5) | async-done | bytes 32800 | tf_op jit(solution)/shard_map/all_to_all | solution.py:1186
  117.3 3.5 %stage_down.1 = (bf16[10,128,256]{2,1,0:T(8,128)(2,1)S(1)}, bf16[10,128,256]{2,1,0:T(8,128)(2,1)S(1)}, f32[16,4,128]{2,1,0:T(4,128)S(1)}, bf16[6,128,256]{2,1,0:T(8,128)(2,1)S(1)}, f32[1,4,128]{2,1,0:T(4,128)S(1)}) custom-call(f32[1,4,128]{2,1,0:T(4,128)S(1)} %get-tuple-element.134.refs_0_, f32[16,4,128]{2,1,0:T(4,128)S(1)} %copy-done.1, ...), custom_call_target="tpu_custom_call" | custom-call | tf_op jit(solution)/shard_map/stage_down/pallas_call | solution.py:1167
  121.4 3.5 %all-to-all-start.6 = ((f32[16,4,128]{2,1,0:T(4,128)}), f32[16,4,128]{2,1,0:T(4,128)S(1)}, u32[]{:S(2)}, u32[]{:S(2)}) async-start(f32[16,4,128]{2,1,0:T(4,128)} %copy-done.2), calls=%async_computation.6 | async-start | bytes 65536 | tf_op jit(solution)/shard_map/all_to_all | solution.py:1186
  124.9 3.0 %grads_down.1.refs_7_ = bf16[2,480,128]{2,1,0:T(8,128)(2,1)} custom-call(bf16[10,128,256]{2,1,0:T(8,128)(2,1)S(1)} %get-tuple-element.153.refs_0_.refs_4_, bf16[6,128,256]{2,1,0:T(8,128)(2,1)S(1)} %get-tuple-element.154.refs_1_, bf16[192,1024]{1,0:T(8,128)(2,1)} %get-tuple-element.155.refs_2_, bf16[256,2048]{1,0:T(8,128)(2,1)} %get-tuple-element.156.refs_3_), custom_call_target="tpu_custom_call" | custom-call | tf_op jit(solution)/shard_map/grads_down/pallas_call | solution.py:1167
  127.9 3.6 %all-to-all-done.6.refs_1_ = f32[16,4,128]{2,1,0:T(4,128)S(1)} async-done(((f32[16,4,128]{2,1,0:T(4,128)}), f32[16,4,128]{2,1,0:T(4,128)S(1)}, u32[]{:S(2)}, u32[]{:S(2)}) %all-to-all-start.6) | async-done | bytes 32800 | tf_op jit(solution)/shard_map/all_to_all | solution.py:1186
  131.5 3.5 %stage_first.1 = (bf16[8,128,256]{2,1,0:T(8,128)(2,1)S(1)}, f32[16,4,128]{2,1,0:T(4,128)}, bf16[10,128,256]{2,1,0:T(8,128)(2,1)S(1)}, f32[8,128]{1,0:T(8,128)S(1)}, f32[1,4,128]{2,1,0:T(4,128)S(1)}) custom-call(f32[1,4,128]{2,1,0:T(4,128)S(1)} %get-tuple-element.147.refs_0_, f32[16,4,128]{2,1,0:T(4,128)S(1)} %all-to-all-done.6.refs_1_, ...), custom_call_target="tpu_custom_call" | custom-call | tf_op jit(solution)/shard_map/stage_first/pallas_call | solution.py:1167
  135.0 3.5 %all-to-all-start.7 = ((f32[16,4,128]{2,1,0:T(4,128)}), f32[16,4,128]{2,1,0:T(4,128)S(1)}, u32[]{:S(2)}, u32[]{:S(2)}) async-start(f32[16,4,128]{2,1,0:T(4,128)} %get-tuple-element.158), calls=%async_computation.7 | async-start | bytes 65536 | tf_op jit(solution)/shard_map/all_to_all | solution.py:1186
  140.1 2.6 %grads_first.1.refs_8_ = bf16[2,224,128]{2,1,0:T(8,128)(2,1)} custom-call(bf16[10,128,256]{2,1,0:T(8,128)(2,1)S(1)} %get-tuple-element.161.refs_0_, f32[8,128]{1,0:T(8,128)S(1)} %get-tuple-element.162.refs_1_, bf16[16,128]{1,0:T(8,128)(2,1)S(1)} %broadcast_in_dim.2.refs_0_.refs_2_, bf16[256,2048]{1,0:T(8,128)(2,1)} %get-tuple-element.163.refs_3_), custom_call_target="tpu_custom_call" | custom-call | tf_op jit(solution)/shard_map/grads_first/pallas_call | solution.py:1167
  142.7 2.4 %all-to-all-done.7.refs_1_ = f32[16,4,128]{2,1,0:T(4,128)S(1)} async-done(((f32[16,4,128]{2,1,0:T(4,128)}), f32[16,4,128]{2,1,0:T(4,128)S(1)}, u32[]{:S(2)}, u32[]{:S(2)}) %all-to-all-start.7) | async-done | bytes 32800 | tf_op jit(solution)/shard_map/all_to_all | solution.py:1186
  145.1 2.6 %stage_last.1 = (bf16[2,896,128]{2,1,0:T(8,128)(2,1)S(1)}, bf16[2,896,128]{2,1,0:T(8,128)(2,1)S(1)}, f32[8,128]{1,0:T(8,128)S(1)}) custom-call(f32[1,4,128]{2,1,0:T(4,128)S(1)} %get-tuple-element.157.refs_0_, f32[16,4,128]{2,1,0:T(4,128)S(1)} %all-to-all-done.7.refs_1_, bf16[8,128,256]{2,1,0:T(8,128)(2,1)} %get-tuple-element.152.refs_6_.refs_2_, ...), custom_call_target="tpu_custom_call" | custom-call | tf_op jit(solution)/shard_map/stage_last/pallas_call | solution.py:1167
  149.8 17.9 %all_to_all.53.refs_0_ = bf16[16,112,128]{2,1,0:T(8,128)(2,1)S(1)} all-to-all(bf16[16,112,128]{2,1,0:T(8,128)(2,1)S(1)} %bitcast.10), channel_id=1, replica_groups={{0,2,4,6,8,10,12,14,16,18,20,22,24,26,28,30},{1,3,5,7,9,11,13,15,17,19,..., dimensions={0} | all-to-all | bytes 917504 | tf_op jit(solution)/shard_map/all_to_all | solution.py:1483
  167.8 11.1 %all_to_all.54 = bf16[8,112,128]{2,1,0:T(8,128)(2,1)S(1)} all-to-all(bf16[8,112,128]{2,1,0:T(8,128)(2,1)S(1)} %add_up.1), channel_id=1, replica_groups={{0,2,4,6,8,10,12,14},{1,3,5,7,9,11,13,15},{16,18,20,22,24,26,28,30},{17..., dimensions={0} | all-to-all | bytes 458752 | tf_op jit(solution)/shard_map/all_to_all | solution.py:1486
  (41 shorter events, 18.3 us)
Async XLA Ops:
  5.3 8.4 %collective-permute-start.1 = (bf16[32,3584]{1,0:T(8,128)(2,1)S(1)}, bf16[32,3584]{1,0:T(8,128)(2,1)S(1)}, u32[]{:S(2)}, u32[]{:S(2)}) collective-permute-start(bf16[32,3584]{1,0:T(8,128)(2,1)S(1)} %get-tuple-element.95), channel_id=1, source_target_pairs={{0,1},{1,0},{2,3},{3,2},{4,5},{5,4},{6,7},{7,6},{8,9},{9,8},{10,11... | collective-permute-start | bytes 688136 | tf_op jit(solution)/shard_map/ppermute | solution.py:1195
  5.9 7.9 %collective-permute-start.2 = (bf16[32,3584]{1,0:T(8,128)(2,1)S(1)}, bf16[32,3584]{1,0:T(8,128)(2,1)S(1)}, u32[]{:S(2)}, u32[]{:S(2)}) collective-permute-start(bf16[32,3584]{1,0:T(8,128)(2,1)S(1)} %get-tuple-element.96), channel_id=1, source_target_pairs={{1,2},{2,1},{3,4},{4,3},{5,6},{6,5},{7,8},{8,7},{9,10},{10,9},{11,... | collective-permute-start | bytes 688136 | tf_op jit(solution)/shard_map/ppermute | solution.py:1195
  6.5 5.9 %collective-permute-start = (bf16[640,128]{1,0:T(8,128)(2,1)S(1)}, bf16[640,128]{1,0:T(8,128)(2,1)S(1)}, u32[]{:S(2)}, u32[]{:S(2)}) collective-permute-start(bf16[640,128]{1,0:T(8,128)(2,1)S(1)} %pack_first.1.refs_4_.refs_1_), channel_id=1, source_target_pairs={{0,16},{16,0},{1,17},{17,1},{2,18},{18,2},{3,19},{19,3},{4,20},{20... | collective-permute-start | bytes 491528 | tf_op jit(solution)/shard_map/ppermute | solution.py:1200
  31.7 12.6 %collective-permute-start.3 = (bf16[1872,128]{1,0:T(8,128)(2,1)S(1)}, bf16[1872,128]{1,0:T(8,128)(2,1)S(1)}, u32[]{:S(2)}, u32[]{:S(2)}) collective-permute-start(bf16[1872,128]{1,0:T(8,128)(2,1)S(1)} %pack_rest.1.refs_4_.refs_0_), channel_id=1, source_target_pairs={{0,16},{16,0},{1,17},{17,1},{2,18},{18,2},{3,19},{19,3},{4,20},{20... | collective-permute-start | bytes 1437704 | tf_op jit(solution)/shard_map/ppermute | solution.py:1200
  36.6 10.3 %all-to-all-start.1 = ((f32[16,4,128]{2,1,0:T(4,128)}), f32[16,4,128]{2,1,0:T(4,128)S(1)}, u32[]{:S(2)}, u32[]{:S(2)}) async-start(f32[16,4,128]{2,1,0:T(4,128)} %get-tuple-element.102), calls=%async_computation.1 | async-start | bytes 65536 | tf_op jit(solution)/shard_map/all_to_all | solution.py:1186
  52.9 12.2 %collective-permute-start.5 = (f32[128,512]{1,0:T(8,128)S(1)}, f32[128,512]{1,0:T(8,128)S(1)}, u32[]{:S(2)}, u32[]{:S(2)}) collective-permute-start(f32[128,512]{1,0:T(8,128)S(1)} %get-tuple-element.110), channel_id=1, source_target_pairs={{1,2},{2,1},{3,4},{4,3},{5,6},{6,5},{7,8},{8,7},{9,10},{10,9},{11,... | collective-permute-start | bytes 786440 | tf_op jit(solution)/shard_map/ppermute | solution.py:1195
  53.6 11.5 %collective-permute-start.4 = (f32[128,512]{1,0:T(8,128)S(1)}, f32[128,512]{1,0:T(8,128)S(1)}, u32[]{:S(2)}, u32[]{:S(2)}) collective-permute-start(f32[128,512]{1,0:T(8,128)S(1)} %get-tuple-element.110), channel_id=1, source_target_pairs={{0,1},{1,0},{2,3},{3,2},{4,5},{5,4},{6,7},{7,6},{8,9},{9,8},{10,11... | collective-permute-start | bytes 786440 | tf_op jit(solution)/shard_map/ppermute | solution.py:1195
  85.7 12.1 %collective-permute-start.6 = (bf16[128,768]{1,0:T(8,128)(2,1)S(1)}, bf16[128,768]{1,0:T(8,128)(2,1)S(1)}, u32[]{:S(2)}, u32[]{:S(2)}) collective-permute-start(bf16[128,768]{1,0:T(8,128)(2,1)S(1)} %get-tuple-element.124), channel_id=1, source_target_pairs={{0,1},{1,0},{2,3},{3,2},{4,5},{5,4},{6,7},{7,6},{8,9},{9,8},{10,11... | collective-permute-start | bytes 589832 | tf_op jit(solution)/shard_map/ppermute | solution.py:1195
  85.8 12.1 %collective-permute-start.7 = (bf16[128,768]{1,0:T(8,128)(2,1)S(1)}, bf16[128,768]{1,0:T(8,128)(2,1)S(1)}, u32[]{:S(2)}, u32[]{:S(2)}) collective-permute-start(bf16[128,768]{1,0:T(8,128)(2,1)S(1)} %get-tuple-element.125), channel_id=1, source_target_pairs={{1,2},{2,1},{3,4},{4,3},{5,6},{6,5},{7,8},{8,7},{9,10},{10,9},{11,... | collective-permute-start | bytes 589832 | tf_op jit(solution)/shard_map/ppermute | solution.py:1195
  86.5 11.4 %all-to-all-start.4 = ((f32[16,4,128]{2,1,0:T(4,128)}), f32[16,4,128]{2,1,0:T(4,128)S(1)}, u32[]{:S(2)}, u32[]{:S(2)}) async-start(f32[16,4,128]{2,1,0:T(4,128)} %get-tuple-element.123), calls=%async_computation.4 | async-start | bytes 65536 | tf_op jit(solution)/shard_map/all_to_all | solution.py:1186
  103.8 12.8 %collective-permute-start.8 = (bf16[128,768]{1,0:T(8,128)(2,1)S(1)}, bf16[128,768]{1,0:T(8,128)(2,1)S(1)}, u32[]{:S(2)}, u32[]{:S(2)}) collective-permute-start(bf16[128,768]{1,0:T(8,128)(2,1)S(1)} %get-tuple-element.136), channel_id=1, source_target_pairs={{0,1},{1,0},{2,3},{3,2},{4,5},{5,4},{6,7},{7,6},{8,9},{9,8},{10,11... | collective-permute-start | bytes 589832 | tf_op jit(solution)/shard_map/ppermute | solution.py:1195
  103.8 12.7 %collective-permute-start.9 = (bf16[128,768]{1,0:T(8,128)(2,1)S(1)}, bf16[128,768]{1,0:T(8,128)(2,1)S(1)}, u32[]{:S(2)}, u32[]{:S(2)}) collective-permute-start(bf16[128,768]{1,0:T(8,128)(2,1)S(1)} %get-tuple-element.137), channel_id=1, source_target_pairs={{1,2},{2,1},{3,4},{4,3},{5,6},{6,5},{7,8},{8,7},{9,10},{10,9},{11,... | collective-permute-start | bytes 589832 | tf_op jit(solution)/shard_map/ppermute | solution.py:1195
  104.5 11.4 %all-to-all-start.5 = ((f32[16,4,128]{2,1,0:T(4,128)}), f32[16,4,128]{2,1,0:T(4,128)S(1)}, u32[]{:S(2)}, u32[]{:S(2)}) async-start(f32[16,4,128]{2,1,0:T(4,128)} %get-tuple-element.135), calls=%async_computation.5 | async-start | bytes 65536 | tf_op jit(solution)/shard_map/all_to_all | solution.py:1186
  115.9 0.6 copy-start
  116.5 0.8 copy-start.1
  120.8 0.6 copy-start.2
  121.4 10.1 %all-to-all-start.6 = ((f32[16,4,128]{2,1,0:T(4,128)}), f32[16,4,128]{2,1,0:T(4,128)S(1)}, u32[]{:S(2)}, u32[]{:S(2)}) async-start(f32[16,4,128]{2,1,0:T(4,128)} %copy-done.2), calls=%async_computation.6 | async-start | bytes 65536 | tf_op jit(solution)/shard_map/all_to_all | solution.py:1186
  135.0 10.1 %all-to-all-start.7 = ((f32[16,4,128]{2,1,0:T(4,128)}), f32[16,4,128]{2,1,0:T(4,128)S(1)}, u32[]{:S(2)}, u32[]{:S(2)}) async-start(f32[16,4,128]{2,1,0:T(4,128)} %get-tuple-element.158), calls=%async_computation.7 | async-start | bytes 65536 | tf_op jit(solution)/shard_map/all_to_all | solution.py:1186
  138.5 4.2 %collective-permute-start.10 = (f32[8,128]{1,0:T(8,128)S(1)}, f32[8,128]{1,0:T(8,128)S(1)}, u32[]{:S(2)}, u32[]{:S(2)}) collective-permute-start(f32[8,128]{1,0:T(8,128)S(1)} %get-tuple-element.164.refs_9_), channel_id=1, source_target_pairs={{0,16},{16,0},{1,17},{17,1},{2,18},{18,2},{3,19},{19,3},{4,20},{20... | collective-permute-start | bytes 12296 | tf_op jit(solution)/shard_map/ppermute | solution.py:1415
  147.8 1.9 %collective-permute-start.11 = (bf16[2,896,128]{2,1,0:T(8,128)(2,1)S(1)}, bf16[2,896,128]{2,1,0:T(8,128)(2,1)S(1)}, u32[]{:S(2)}, u32[]{:S(2)}) collective-permute-start(bf16[2,896,128]{2,1,0:T(8,128)(2,1)S(1)} %get-tuple-element.167), channel_id=1, source_target_pairs={{0,1},{1,0},{2,3},{3,2},{4,5},{5,4},{6,7},{7,6},{8,9},{9,8},{10,11... | collective-permute-start | bytes 1376264 | tf_op jit(solution)/shard_map/ppermute | solution.py:1479
  178.9 1.5 collective-permute-start.12

commit v3 on v2

--- a/solution.py
+++ b/solution.py
@@ -316,12 +316,13 @@
     return mm_nt(place(size, size, 0), value).astype(BF16)
 
 
-def tap_of(pieces, offset, index, size):
+def tap_of(pieces, offset, index, size, paired=False):
     each = size // len(pieces)
-    start = offset + index * each
-    return jnp.concatenate([piece[start : start + each, :] for piece in pieces], axis=0).astype(
-        BF16
-    )
+    start = offset + (index // 2 if paired else index) * each
+    tap = jnp.concatenate([piece[start : start + each, :] for piece in pieces], axis=0)
+    if paired:
+        tap = tap[:, 64 * (index % 2) : 64 * (index % 2) + 64]
+    return tap.astype(BF16)
 
 
 def in_order(scal, pieces):
@@ -359,25 +360,14 @@
                 value = shard.spot[t]
                 if swapped:
                     value = mm_nt(place(value.shape[1], value.shape[1], 0), value.astype(BF16))
-                scratch[start : start + value.shape[0], : value.shape[1]] = value
-                start += rows
+                if value.shape[1] == 64:
+                    lanes = slice(64 * (t % 2), 64 * (t % 2) + 64)
+                    scratch[start : start + value.shape[0], lanes] = value
+                    start += rows if t % 2 or t == taps - 1 else 0
+                else:
+                    scratch[start : start + value.shape[0], : value.shape[1]] = value
+                    start += rows
     give(out, scratch[...].astype(BF16))
-
-
-def prepare_first(embed_size, scal, vec, *refs):
-    pieces, (win, wfirst, wfirst_t, shift) = refs[:-4], refs[-4:]
-    count = len(pieces)
-    pieces = in_order(scal, pieces)
-    each = 9 * (64 // count)
-    give(win, fine_matrix([tap_of(pieces, 0, t, 64) for t in range(9)], 32))
-    first = fine_matrix([tap_of(pieces, each, t, 64) for t in range(9)], 64)
-    give(wfirst, first)
-    give(wfirst_t, flipped(first))
-    line = mm(whole(vec), tap_of(pieces, 2 * each, 0, embed_size))[0:1, :64]
-    both = jnp.concatenate([line, line], axis=1)
-    diagonal = place(128, 128, 0).astype(F32)
-    column = jnp.sum(diagonal * both, axis=1, keepdims=True)
-    give(shift, jnp.broadcast_to(column, (128, 128)))
 
 
 def prepare_rest(scal, *refs):
@@ -387,18 +377,18 @@
     pieces = in_order(scal, pieces)
     start = 0
 
-    def taps_of(size):
+    def taps_of(size, paired=False):
         nonlocal start
-        taps = [tap_of(pieces, start, t, size) for t in range(9)]
-        start += 9 * (size // count)
+        taps = [tap_of(pieces, start, t, size, paired) for t in range(9)]
+        start += (5 if paired else 9) * (size // count)
         return taps
 
     def both(value, forward, backward):
         give(forward, value)
         give(backward, flipped(value))
 
-    both(fine_matrix(taps_of(64), 64), wsecond, wsecond_t)
-    taps = taps_of(128)
+    both(fine_matrix(taps_of(64, True), 64), wsecond, wsecond_t)
+    taps = taps_of(128, True)
     rows = []
     for a in range(3):
         total = None
@@ -429,7 +419,15 @@
     both(fine_matrix(taps, 64), wout, wout_t)
 
 
-def enter(scal, target, condition, noise, done, own, edge_a, edge_b, figures, scratch, marks):
+def enter(
+    widths, scal, target, condition, noise, *refs
+):
+    *shards, packed, own, edge_a, edge_b, figures, taps, scratch, marks = refs
+    for item in shards:
+        item.wait(1)
+    pack(widths, scal, *shards, packed, taps)
+    for item in (target, condition, noise):
+        item.wait(2)
     values = [jnp.full((1, 128), scal[k], F32) for k in range(6)]
     give(figures, jnp.concatenate(values + [jnp.zeros((2, 128), F32)], axis=0))
     sigma, skip, in_scale = scal[0], scal[1], scal[3]
@@ -474,7 +472,10 @@
     return jnp.concatenate(halves, axis=0)
 
 
-def stage_a(scal, win, got_a, got_b, own, done, act, stats, kept, line_a, line_b, above, below):
+def stage_a(scal, got_a, got_b, own, done, *refs):
+    *pieces, act, stats, kept, line_a, line_b, above, below = refs
+    pieces = in_order(scal, pieces)
+    weights = fine_matrix([tap_of(pieces, 0, t, 64) for t in range(9)], 32)
     give(line_a, marked(scal, got_a))
     give(line_b, marked(scal, got_b))
     above[...] = pick(scal, whole(got_a), whole(got_b))
@@ -483,7 +484,6 @@
     keep = lax.broadcasted_iota(jnp.int32, (16, FAR * 512), 0) < 8
     for ref in (above, below):
         ref[16:, :] = jnp.where(keep, ref[16:, :], clear)
-    weights = whole(win)
     parts = {}
     total = jnp.zeros((128, HALF), F32)
     square = jnp.zeros((128, HALF), F32)
@@ -518,14 +518,21 @@
     ref[:, index * HALF : (index + 1) * HALF] = value
 
 
-def stage_b(
-    members, scal, stats_a, shift, wfirst, act_a,
-    act_b, stats, kept, hats, passed, totals, zs, sems,
-):
+def stage_b(members, embed_size, scal, stats_a, act_a, vec, *refs):
+    *pieces, act_b, stats, kept, hats, passed, totals, wfirst_t, wfirst, zs, sems = refs
     passed.send(act_a.spot.at[pl.ds(2, 16)], sems.at[0])
     give(totals, total_stats(stats_a)[None])
+    count = len(pieces)
+    pieces = in_order(scal, pieces)
+    start = 9 * (64 // count)
+    first = fine_matrix([tap_of(pieces, start, t, 64, True) for t in range(9)], 64)
+    start += 5 * (64 // count)
+    wfirst[...] = first
+    give(wfirst_t, flipped(first))
+    line = mm(whole(vec), tap_of(pieces, start, 0, embed_size))[0:1, :64]
+    both = jnp.concatenate([line, line], axis=1)
+    lift = jnp.sum(place(128, 128, 0).astype(F32) * both, axis=1, keepdims=True)
     mean, inverse = norm_columns(stats_a, True, members)
-    lift = shift.spot[:, 0:1]
     for r in range(-6, ROWS + 6):
         hat = (row(act_a, r) - mean) * inverse
         fill(zs, r + 6, fine_taps(masked(silu(hat), r, ROWS, scal)))
@@ -533,12 +540,11 @@
             hats.spot[r] = hat.astype(BF16)
     hats.finish()
     kept.send(zs.at[:, pl.ds(6 * HALF, 8 * HALF)], sems.at[1])
-    wfirst.wait(1)
     parts = {}
     total = jnp.zeros((128, HALF), F32)
     square = jnp.zeros((128, HALF), F32)
     for r in range(-6, ROWS + 6):
-        parts[r] = mm(whole(wfirst), slot(zs, r + 6))
+        parts[r] = mm(wfirst[...], slot(zs, r + 6))
         i = r - 1
         if i > -6:
             value = spread(parts, i, i)[i] + lift
@@ -552,7 +558,7 @@
 
 def stage_c(
     members, scal, stats_b, wsecond, act_b, act_a, wdown,
-    fine, act_c, edge, stats, kept, kept_pool, hats, totals, zs, sems,
+    fine, act_c, edge, stats, kept, kept_pool, hats, totals, zs, convolved, sems,
 ):
     give(totals, total_stats(stats_b)[None])
     mean, inverse = norm_columns(stats_b, True, members)
@@ -563,24 +569,27 @@
             hats.spot[r + 1] = hat.astype(BF16)
     hats.finish()
     kept.send(zs.at[:, pl.ds(5 * HALF, 8 * HALF)], sems.at[0])
-    for item in (wsecond, act_a, wdown):
-        item.wait(1)
+    wsecond.wait(1)
     parts = {}
-    pooled = {}
-    half = {}
     for r in range(-5, ROWS + 5):
         parts[r] = mm(whole(wsecond), slot(zs, r + 5))
         i = r - 1
         if i > -5:
-            value = spread(parts, i, i)[i] + row(act_a, i)
-            if -3 <= i < ROWS + 3:
-                put(fine, i, value)
+            convolved[i + 4] = spread(parts, i, i)[i]
             del parts[i - 1]
-            half[i] = value[:64] + value[64:]
-            if i % 2:
-                value = 0.25 * (half.pop(i - 1) + half.pop(i))
-                value = masked(value, i // 2, CROWS, scal)
-                pooled[i // 2] = value.astype(BF16).astype(F32)
+    act_a.wait(1)
+    wdown.wait(1)
+    pooled = {}
+    half = {}
+    for i in range(-4, ROWS + 4):
+        value = convolved[i + 4] + row(act_a, i)
+        if -3 <= i < ROWS + 3:
+            put(fine, i, value)
+        half[i] = value[:64] + value[64:]
+        if i % 2:
+            value = 0.25 * (half.pop(i - 1) + half.pop(i))
+            value = masked(value, i // 2, CROWS, scal)
+            pooled[i // 2] = value.astype(BF16).astype(F32)
     weights = whole(wdown)
     parts = {}
     total = jnp.zeros((128, HALF), F32)
@@ -811,6 +820,7 @@
     give(loss, jnp.broadcast_to(total_stats(stats_ed)[2:3, :], (8, 128)))
     mean, inverse = norm_columns(stats_d, True, members)
     shift, slope = back_columns(stats_ed, True, members)
+    hats.wait(1)
     g = {}
     for r in range(-3, ROWS + 3):
         hat = row(hats, r).astype(F32)
@@ -865,6 +875,7 @@
 ):
     mean, inverse = norm_columns(stats_c, False, members_c)
     shift, slope = back_columns(stats_ec, False, members_c)
+    hats_c.wait(1)
     g = {}
     for r in range(-2, CROWS + 2):
         hat = row(hats_c, r).astype(F32)
@@ -920,6 +931,7 @@
 ):
     mean, inverse = norm_columns(stats_b, True, members)
     shift, slope = back_columns(stats_eb, True, members)
+    hats_b.wait(1)
     g = {}
     sums = jnp.zeros((128, HALF), F32)
     for r in range(-1, ROWS + 1):
@@ -950,7 +962,7 @@
 
 
 def stage_last(
-    members, scal, stats_a, stats_ea, hats, back_a, grad_fine, kept_in, early, middle, first,
+    members, members_all, scal, stats_a, stats_ea, hats, back_a, grad_fine, kept_in, early, middle, first,
     loss, loss_other, keep, send, loss_sum, gs, held, sems,
 ):
     grads = Source(held, [], 0)
@@ -962,7 +974,7 @@
         )
         copies[index].start()
         start += ref.shape[1]
-    give(loss_sum, whole(loss) + whole(loss_other))
+    give(loss_sum, (loss.spot[0:1, 0:1] + loss_other.spot[0:1, 0:1]) * (1.0 / members_all))
     mean, inverse = norm_columns(stats_a, True, members)
     shift, slope = back_columns(stats_ea, True, members)
     for r in range(ROWS):
@@ -1232,61 +1244,52 @@
     condition = conditioning.reshape(12 * ROWS, 512)
     noise = noise_sample.reshape(12 * ROWS, 512)
 
-    def pack_all(name, shards, rows, *after):
+    def widths_of(shards, rows):
         widths = tuple(
             (9 if item.ndim == 3 else 1, size, item.ndim == 3 and item.shape[1] == 24)
             for item, size in zip(shards, rows)
         )
-        total = sum(taps * size for taps, size, _ in widths)
-        (packed,) = run(
-            name,
-            functools.partial(pack, widths),
-            [shape(total, 128, dtype=BF16)],
-            None,
-            *[Saved(item) for item in shards],
-            *after,
-            scratch=[((total, 128), F32)],
-        )
-        return packed
+        total = 0
+        for item, (taps, size, swapped) in zip(shards, widths):
+            paired = taps == 9 and item.shape[2] == 64
+            total += (5 if paired else taps) * size
+        return widths, total
 
     fine_o, coarse_o = input_kernel.shape[1], down_kernel.shape[1]
     inputs_t = jnp.swapaxes(input_kernel, 1, 2)
-    early_packed = pack_all(
-        "pack_first",
-        [inputs_t, first_kernel, embed_matrix],
-        [fine_o, fine_o, embed_matrix.shape[0]],
-    )
-    early = gather_packed(early_packed)
+    shards = [inputs_t, first_kernel, embed_matrix]
+    widths, packed_rows = widths_of(shards, [fine_o, fine_o, embed_matrix.shape[0]])
     far = shape(32, FAR * 512, dtype=BF16)
-    own, edge_a, edge_b, figures = run(
+    early, own, edge_a, edge_b, figures = run(
         "enter",
-        enter,
-        [shape(32, ROWS * 512, dtype=BF16), far, far, Saved(shape(8, 128))],
+        functools.partial(enter, widths),
+        [
+            shape(packed_rows, 128, dtype=BF16), shape(32, ROWS * 512, dtype=BF16), far, far,
+            Saved(shape(8, 128)),
+        ],
         scal,
-        Saved(target),
-        Saved(condition),
-        Saved(noise),
-        early[0],
-        scratch=[((4, 192, 128), F32), ((2, 16, FAR * 512), BF16)],
+        Saved(target, when=2),
+        Saved(condition, when=2),
+        Saved(noise, when=2),
+        *[Saved(item, when=1) for item in shards],
+        scratch=[
+            ((packed_rows, 128), F32), ((4, 192, 128), F32), ((2, 16, FAR * 512), BF16)
+        ],
     )
     got_a, got_b = swap(edge_a, edge_b)
-    rest = pack_all(
+    early = gather_packed(early)
+    shards = [second_kernel, down_kernel, coarse_kernel, upward_kernel, output_kernel]
+    widths, packed_rows = widths_of(shards, [fine_o, coarse_o, coarse_o, fine_o, 16])
+    (rest,) = run(
         "pack_rest",
-        [second_kernel, down_kernel, coarse_kernel, upward_kernel, output_kernel],
-        [fine_o, coarse_o, coarse_o, fine_o, 16],
+        functools.partial(pack, widths),
+        [shape(packed_rows, 128, dtype=BF16)],
+        None,
+        *[Saved(item) for item in shards],
         own,
+        scratch=[((packed_rows, 128), F32)],
     )
     vector = jnp.broadcast_to(embedded[None, :], (16, embedded.shape[0]))
-    win, wfirst, wfirst_t, shift = run(
-        "prepare_first",
-        functools.partial(prepare_first, embedded.shape[0]),
-        [
-            shape(384, 128, dtype=BF16), Saved(shape(384, 256, dtype=BF16)),
-            Saved(shape(256, 384, dtype=BF16)), shape(128, 128),
-        ],
-        None,
-        vector, *early,
-    )
     stat = shape(bands, 4, 128)
     total = Saved(shape(1, 4, 128))
     act_a, stats_a, kept_in, line_a, line_b = run(
@@ -1297,7 +1300,7 @@
             Saved(shape(16, 512)), Saved(shape(16, 512)),
         ],
         None,
-        win, got_a, got_b, own, rest,
+        got_a, got_b, own, rest, *early,
         scratch=[((32, FAR * 512), BF16), ((32, FAR * 512), BF16)],
     )
     stats_a = sum_parts(stats_a)
@@ -1318,17 +1321,17 @@
         *gather_packed(rest),
     )
 
-    act_b, stats_b, kept_a, hats_a, act_a, total_a = run(
+    act_b, stats_b, kept_a, hats_a, act_a, total_a, wfirst_t = run(
         "stage_b",
-        functools.partial(stage_b, members),
+        functools.partial(stage_b, members, embedded.shape[0]),
         [
             rows_of(-5, 18), stat, Saved(flat_rows(0, 8, 256), when=None),
             Saved(rows_of(0, 8, BF16)),
-            Saved(rows_of(-4, 16), when=None), total,
+            Saved(rows_of(-4, 16), when=None), total, Saved(shape(256, 384, dtype=BF16)),
         ],
         None,
-        stats_a, shift, Saved(wfirst, when=1), act_a,
-        scratch=[((256, 20 * HALF), BF16), pltpu.SemaphoreType.DMA((2,))],
+        stats_a, act_a, vector, *early,
+        scratch=[((384, 256), BF16), ((256, 20 * HALF), BF16), pltpu.SemaphoreType.DMA((2,))],
     )
     stats_b = sum_parts(stats_b)
     fine, act_c, edge, stats_c, kept_b, kept_pool, hats_b, total_b = run(
@@ -1341,7 +1344,9 @@
         ],
         None,
         stats_b, Saved(wsecond, when=1), act_b, Saved(act_a, when=1), Saved(wdown, when=1),
-        scratch=[((256, 18 * HALF), BF16), pltpu.SemaphoreType.DMA((1,))],
+        scratch=[
+            ((256, 18 * HALF), BF16), ((16, 128, HALF), F32), pltpu.SemaphoreType.DMA((1,)),
+        ],
     )
     got_a, got_b = swap(edge.array, edge.array)
     stats_c = sum_parts(stats_c)
@@ -1395,7 +1400,7 @@
             shape(8, 128), shape(1, 4, 128),
         ],
         None,
-        total_d, stats_ed, got_a, got_b, Saved(hats_d), back_d, Saved(wup_t, when=1),
+        total_d, stats_ed, got_a, got_b, Saved(hats_d, when=1), back_d, Saved(wup_t, when=1),
         Saved(total_c, when=1),
         Saved(hats_c, when=1), Saved(wcoarse_t, when=1), Saved(grad_out, when=None),
     )
@@ -1419,11 +1424,11 @@
         "stage_down",
         functools.partial(stage_down, members, members_c),
         [
-            rows_of(-1, 10, BF16), rows_of(-1, 10, BF16), stat, rows_of(-1, 6, BF16),
+            rows_of(-1, 10, BF16), rows_of(-1, 10, BF16), stat, Saved(rows_of(-1, 6, BF16)),
             shape(1, 4, 128),
         ],
         None,
-        total_c, stats_ec, got_a, got_b, Saved(hats_c), back_c, grad_coarse,
+        total_c, stats_ec, got_a, got_b, Saved(hats_c, when=1), back_c, grad_coarse,
         Saved(wdown_t, when=1), grad_merged, Saved(total_b, when=1), Saved(wsecond_t, when=1),
         Saved(hats_b, 0, 8, when=1), Saved(early, when=None),
     )
@@ -1432,7 +1437,7 @@
         grads_down,
         [Saved(group_shape(5 * (fine_o + coarse_o), count))],
         None,
-        grad_fine, grad_c, Saved(kept_pool), Saved(kept_b),
+        grad_fine, Saved(grad_c), Saved(kept_pool), Saved(kept_b),
         scratch=[((384, 8 * HALF), BF16), ((384, 4 * HALF), BF16)],
     )
     stats_eb = sum_parts(stats_eb)
@@ -1444,7 +1449,7 @@
             shape(1, 4, 128),
         ],
         None,
-        total_b, stats_eb, Saved(hats_b), back_b, Saved(wfirst_t, when=1), Saved(total_a, when=1),
+        total_b, stats_eb, Saved(hats_b, when=1), back_b, Saved(wfirst_t, when=1), Saved(total_a, when=1),
         Saved(hats_a, when=1), Saved(middle, when=None),
     )
     (grad_first,) = run(
@@ -1464,8 +1469,8 @@
     half = shape(count, chunk * chips, 128, dtype=BF16)
     keep, send, loss = run(
         "stage_last",
-        functools.partial(stage_last, members),
-        [half, half, shape(8, 128)],
+        functools.partial(stage_last, members, members_all),
+        [half, half, shape(1, 1)],
         None,
         total_a, stats_ea, Saved(hats_a), back_a, grad_fine, Saved(kept_in, when=1),
         Saved(early, when=None), Saved(middle, when=None), Saved(grad_first, when=1), loss, loss_other,
@@ -1474,7 +1479,7 @@
             pltpu.SemaphoreType.DMA((2,)),
         ],
     )
-    loss_value = loss[0, 0] / members_all
+    loss_value = loss.reshape(())
     pairs = [(i, i ^ 1) for i in range(bands)]
     got = lax.ppermute(send, "rows", pairs)
     (both,) = run("join", join, [half], None, keep, got)

time: 184 us -> 178 us (0.967)
  local copies, waits for them, and re-layouts: 2.58 us -> 0.09 us
    ppermute x2, waiting for transfers between devices: 5.95 us -> 2.86 us  [gather_packed(): return [packed, lax.ppermute(packed, 'fsdp', [(0, 1), (1, 0)])]]
    all_to_all x5, waiting for transfers between devices: 13.2 us -> 16.2 us  [sum_parts(): return lax.all_to_all(stats, 'rows', 0, 0)]
    unnamed x6 -> x0, local copies, waits for them, and re-layouts: 1.98 us -> none
    pallas_call x21 -> x19, Pallas kernels: 60.6 us -> 59.2 us  [run(): pl.pallas_call(body, out_shape=tuple(out_shapes), in_specs=in_specs, out_...]
  transfers between devices with their start and end apart: 18 -> 18, of which waited for: 8 -> 10; matrix products, arithmetic and copies ran while one was open for 0% -> 0% of each run, Pallas kernels for 11% -> 11%
where the time goes in v3:
time: 178 us; the launch traced here: 177 us
  blocking collectives  63.3 us (36%)
  Pallas kernels  59.2 us (33%)
  starting transfers between devices  29.9 us (17%)
  waiting for transfers between devices  22.8 us (13%)
  between operations  1.94 us (1%)
    pallas_call x19, Pallas kernels, run(): pl.pallas_call(body, out_shape=tuple(out_shapes), in_specs=in_specs, out_...  59.2 us
    all_to_all x3, blocking collectives, sum_parts(): return lax.all_to_all(stats, 'rows', 0, 0)  34.7 us
    all_to_all x5, starting transfers between devices, sum_parts(): return lax.all_to_all(stats, 'rows', 0, 0)  20 us
    all_to_all x1, blocking collectives, per_device(): got = lax.all_to_all(both, ('fsdp', 'rows'), 0, 0, axis_index_groups=cores)  17.5 us
    all_to_all x5, waiting for transfers between devices, sum_parts(): return lax.all_to_all(stats, 'rows', 0, 0)  16.2 us
    all_to_all x1, blocking collectives, per_device(): mine = lax.all_to_all(mine, 'rows', 0, 0, axis_index_groups=cores)  11.1 us
    ppermute x2, starting transfers between devices, gather_packed(): return [packed, lax.ppermute(packed, 'fsdp', [(0, 1), (1, 0)])]  4.07 us
  transfers between devices with their start and end apart: 18, of which 10 were waited for; matrix products, arithmetic and copies ran while one was open for 0% of the time, Pallas kernels for 11%

profile of v3, /device:TPU:0, one launch (start us, length us, event | category | flops | bytes accessed | tf_op | source)
XLA Modules:
  0.0 177.4 jit_solution(12080988189420398957)
XLA Ops:
  1.5 2.9 %enter.1 = (bf16[512,128]{1,0:T(8,128)(2,1)S(1)}, bf16[32,4096]{1,0:T(8,128)(2,1)S(1)}, bf16[32,3584]{1,0:T(8,128)(2,1)S(1)}, bf16[32,3584]{1,0:T(8,128)(2,1)S(1)}, f32[8,128]{1,0:T(8,128)}) custom-call(f32[6]{0:T(128)S(1)} %stack.24.refs_0_, f32[96,512]{1,0:T(8,128)} %bitcast.13, f32[96,512]{1,0:T(8,128)} %bitcast.17, f32[96,512]{1,0:T(8,128)} %bitcast.15, ...), custom_call_target="tpu_custom_call" | custom-call | tf_op jit(solution)/shard_map/enter/pallas_call | solution.py:1179
  5.7 2.6 %collective-permute-start.2 = (bf16[512,128]{1,0:T(8,128)(2,1)S(1)}, bf16[512,128]{1,0:T(8,128)(2,1)S(1)}, u32[]{:S(2)}, u32[]{:S(2)}) collective-permute-start(bf16[512,128]{1,0:T(8,128)(2,1)S(1)} %get-tuple-element.94.refs_4_.refs_3_), channel_id=1, source_target_pairs={{0,16},{16,0},{1,17},{17,1},{2,18},{18,2},{3,19},{19,3},{4,20},{20... | collective-permute-start | bytes 393224 | tf_op jit(solution)/shard_map/ppermute | solution.py:1212
  11.2 2.4 %stage_a.1 = (f32[20,128,256]{2,1,0:T(8,128)S(1)}, f32[16,4,128]{2,1,0:T(4,128)S(1)}, bf16[128,2560]{1,0:T(8,128)(2,1)}, f32[16,512]{1,0:T(8,128)}, f32[16,512]{1,0:T(8,128)}) custom-call(bf16[32,3584]{1,0:T(8,128)(2,1)S(1)} %collective-permute-done.refs_0_, bf16[32,3584]{1,0:T(8,128)(2,1)S(1)} %collective-permute-done.1.refs_1_, ...), custom_call_target="tpu_custom_call" | custom-call | tf_op jit(solution)/shard_map/stage_a/pallas_call | solution.py:1179
  13.6 16.1 %all_to_all.50.refs_0_ = f32[16,4,128]{2,1,0:T(4,128)S(1)} all-to-all(f32[16,4,128]{2,1,0:T(4,128)S(1)} %get-tuple-element.95), channel_id=1, replica_groups=mesh['fsdp'=2,'rows'=16] {'rows'}, dimensions={0} | all-to-all | bytes 65536 | tf_op jit(solution)/shard_map/all_to_all | solution.py:1198
  31.4 3.9 %stage_b.1 = (f32[18,128,256]{2,1,0:T(8,128)S(1)}, f32[16,4,128]{2,1,0:T(4,128)}, bf16[256,2048]{1,0:T(8,128)(2,1)}, bf16[8,128,256]{2,1,0:T(8,128)(2,1)}, f32[1...) custom-call(f32[16,4,128]{2,1,0:T(4,128)S(1)} %all_to_all.50.refs_0_, ...), custom_call_target="tpu_custom_call" | custom-call | tf_op jit(solution)/shard_map/stage_b/pallas_call | solution.py:1179
  35.3 3.5 %all-to-all-start.1 = ((f32[16,4,128]{2,1,0:T(4,128)}), f32[16,4,128]{2,1,0:T(4,128)S(1)}, u32[]{:S(2)}, u32[]{:S(2)}) async-start(f32[16,4,128]{2,1,0:T(4,128)} %get-tuple-element.98), calls=%async_computation.1 | async-start | bytes 65536 | tf_op jit(solution)/shard_map/all_to_all | solution.py:1198
  40.1 2.7 %prepare_rest.1 = (bf16[384,256]{1,0:T(8,128)(2,1)}, bf16[256,384]{1,0:T(8,128)(2,1)}, bf16[384,192]{1,0:T(8,128)(2,1)}, bf16[192,384]{1,0:T(8,128)(2,1)}, bf16[...) custom-call(bf16[1488,128]{1,0:T(8,128)(2,1)S(1)} %pack_rest.1.refs_, ...), custom_call_target="tpu_custom_call" | custom-call | tf_op jit(solution)/shard_map/prepare_rest/pallas_call | solution.py:1179
  42.8 2.6 %all-to-all-done.1.refs_0_ = f32[16,4,128]{2,1,0:T(4,128)S(1)} async-done(((f32[16,4,128]{2,1,0:T(4,128)}), f32[16,4,128]{2,1,0:T(4,128)S(1)}, u32[]{:S(2)}, u32[]{:S(2)}) %all-to-all-start.1) | async-done | bytes 32800 | tf_op jit(solution)/shard_map/all_to_all | solution.py:1198
  45.4 5.0 %stage_c.1 = (f32[14,128,256]{2,1,0:T(8,128)S(1)}, f32[6,128,256]{2,1,0:T(8,128)S(1)}, f32[128,512]{1,0:T(8,128)S(1)}, f32[16,4,128]{2,1,0:T(4,128)S(1)}, bf16[2...) custom-call(f32[16,4,128]{2,1,0:T(4,128)S(1)} %all-to-all-done.1.refs_0_,, ...), custom_call_target="tpu_custom_call" | custom-call | tf_op jit(solution)/shard_map/stage_c/pallas_call | solution.py:1179
  52.9 9.4 %all_to_all.51.refs_0_ = f32[16,4,128]{2,1,0:T(4,128)S(1)} all-to-all(f32[16,4,128]{2,1,0:T(4,128)S(1)} %get-tuple-element.104), channel_id=1, replica_groups=mesh['fsdp'=2,'rows'=16] {'rows'}, dimensions={0} | all-to-all | bytes 65536 | tf_op jit(solution)/shard_map/all_to_all | solution.py:1198
  62.3 5.7 %stage_d.1 = (f32[14,128,256]{2,1,0:T(8,128)S(1)}, bf16[8,128,256]{2,1,0:T(8,128)(2,1)}, f32[16,4,128]{2,1,0:T(4,128)S(1)}, bf16[384,1024]{1,0:T(8,128)(2,1)}, b...) custom-call(f32[16,4,128]{2,1,0:T(4,128)S(1)} %all_to_all.51.refs_0_, bf16[384,384]{1,0:T(8,128)(2,1)} %get-tuple-element.105.refs_1_, ...), custom_call_target="tpu_custom_call" | custom-call | tf_op jit(solution)/shard_map/stage_d/pallas_call | solution.py:1179
  68.0 9.2 %all_to_all.52.refs_0_ = f32[16,4,128]{2,1,0:T(4,128)S(1)} all-to-all(f32[16,4,128]{2,1,0:T(4,128)S(1)} %get-tuple-element.110), channel_id=1, replica_groups=mesh['fsdp'=2,'rows'=16] {'rows'}, dimensions={0} | all-to-all | bytes 65536 | tf_op jit(solution)/shard_map/all_to_all | solution.py:1198
  77.2 5.7 %stage_out.1 = (f32[96,512]{1,0:T(8,128)}, bf16[8,128,256]{2,1,0:T(8,128)(2,1)S(1)}, bf16[128,768]{1,0:T(8,128)(2,1)S(1)}, bf16[128,768]{1,0:T(8,128)(2,1)S(1)},...) custom-call(f32[16,4,128]{2,1,0:T(4,128)S(1)} %all_to_all.52.refs_0_, ...), custom_call_target="tpu_custom_call" | custom-call | tf_op jit(solution)/shard_map/stage_out/pallas_call | solution.py:1179
  83.7 4.7 %all-to-all-start.4 = ((f32[16,4,128]{2,1,0:T(4,128)}), f32[16,4,128]{2,1,0:T(4,128)S(1)}, u32[]{:S(2)}, u32[]{:S(2)}) async-start(f32[16,4,128]{2,1,0:T(4,128)} %get-tuple-element.119), calls=%async_computation.4 | async-start | bytes 65536 | tf_op jit(solution)/shard_map/all_to_all | solution.py:1198
  88.4 2.4 %grads_out.1.refs_10_.refs_4_ = bf16[2,80,128]{2,1,0:T(8,128)(2,1)} custom-call(bf16[10,32,256]{2,1,0:T(8,128)(2,1)S(1)} %get-tuple-element.128.refs_0_, bf16[256,2048]{1,0:T(8,128)(2,1)} %get-tuple-element.129.refs_1_), custom_call_target="tpu_custom_call" | custom-call | tf_op jit(solution)/shard_map/grads_out/pallas_call | solution.py:1179
  90.9 4.2 %all-to-all-done.4.refs_1_ = f32[16,4,128]{2,1,0:T(4,128)S(1)} async-done(((f32[16,4,128]{2,1,0:T(4,128)}), f32[16,4,128]{2,1,0:T(4,128)S(1)}, u32[]{:S(2)}, u32[]{:S(2)}) %all-to-all-start.4) | async-done | bytes 32800 | tf_op jit(solution)/shard_map/all_to_all | solution.py:1198
  95.1 5.7 %stage_up.1 = (bf16[12,128,256]{2,1,0:T(8,128)(2,1)S(1)}, bf16[4,128,256]{2,1,0:T(8,128)(2,1)S(1)}, bf16[6,128,256]{2,1,0:T(8,128)(2,1)S(1)}, bf16[128,768]{1,0:...) custom-call(f32[1,4,128]{2,1,0:T(4,128)S(1)} %get-tuple-element.118., ...), custom_call_target="tpu_custom_call" | custom-call | tf_op jit(solution)/shard_map/stage_up/pallas_call | solution.py:1179
  101.6 4.8 %all-to-all-start.5 = ((f32[16,4,128]{2,1,0:T(4,128)}), f32[16,4,128]{2,1,0:T(4,128)S(1)}, u32[]{:S(2)}, u32[]{:S(2)}) async-start(f32[16,4,128]{2,1,0:T(4,128)} %get-tuple-element.131), calls=%async_computation.5 | async-start | bytes 65536 | tf_op jit(solution)/shard_map/all_to_all | solution.py:1198
  106.3 3.6 %grads_up.1.refs_12_.refs_6_ = bf16[2,944,128]{2,1,0:T(8,128)(2,1)} custom-call(bf16[12,128,256]{2,1,0:T(8,128)(2,1)S(1)} %get-tuple-element.137.refs_0_.refs_8_, bf16[6,128,256]{2,1,0:T(8,128)(2,1)S(1)} %get-tuple-element.135.refs_1_.refs_6_, bf16[384,1024]{1,0:T(8,128)(2,1)} %get-tuple-element.141.refs_2_, bf16[384,1024]{1,0:T(8,128)(2,1)} %get-tuple-element.142.refs_3_, ...), custom_call_target="tpu_custom_call" | custom-call | tf_op jit(solution)/shard_map/grads_up/pallas_call | solution.py:1179
  109.9 3.0 %all-to-all-done.5.refs_1_ = f32[16,4,128]{2,1,0:T(4,128)S(1)} async-done(((f32[16,4,128]{2,1,0:T(4,128)}), f32[16,4,128]{2,1,0:T(4,128)S(1)}, u32[]{:S(2)}, u32[]{:S(2)}) %all-to-all-start.5) | async-done | bytes 32800 | tf_op jit(solution)/shard_map/all_to_all | solution.py:1198
  113.0 4.1 %stage_down.1 = (bf16[10,128,256]{2,1,0:T(8,128)(2,1)S(1)}, bf16[10,128,256]{2,1,0:T(8,128)(2,1)S(1)}, f32[16,4,128]{2,1,0:T(4,128)}, bf16[6,128,256]{2,1,0:T(8,128)(2,1)}, f32[1,4,128]{2,1,0:T(4,128)S(1)}) custom-call(f32[1,4,128]{2,1,0:T(4,128)S(1)} %get-tuple-element.130.refs_0_, f32[16,4,128]{2,1,0:T(4,128)S(1)} %all-to-all-done.5.refs_1_, ...), custom_call_target="tpu_custom_call" | custom-call | tf_op jit(solution)/shard_map/stage_down/pallas_call | solution.py:1179
  117.1 3.5 %all-to-all-start.6 = ((f32[16,4,128]{2,1,0:T(4,128)}), f32[16,4,128]{2,1,0:T(4,128)S(1)}, u32[]{:S(2)}, u32[]{:S(2)}) async-start(f32[16,4,128]{2,1,0:T(4,128)} %get-tuple-element.144), calls=%async_computation.6 | async-start | bytes 65536 | tf_op jit(solution)/shard_map/all_to_all | solution.py:1198
  120.6 3.1 %grads_down.1.refs_7_ = bf16[2,480,128]{2,1,0:T(8,128)(2,1)} custom-call(bf16[10,128,256]{2,1,0:T(8,128)(2,1)S(1)} %get-tuple-element.149.refs_0_.refs_4_, bf16[6,128,256]{2,1,0:T(8,128)(2,1)} %get-tuple-element.150.refs_1_, bf16[192,1024]{1,0:T(8,128)(2,1)} %get-tuple-element.151.refs_2_, bf16[256,2048]{1,0:T(8,128)(2,1)} %get-tuple-element.152.refs_3_), custom_call_target="tpu_custom_call" | custom-call | tf_op jit(solution)/shard_map/grads_down/pallas_call | solution.py:1179
  123.7 3.5 %all-to-all-done.6.refs_1_ = f32[16,4,128]{2,1,0:T(4,128)S(1)} async-done(((f32[16,4,128]{2,1,0:T(4,128)}), f32[16,4,128]{2,1,0:T(4,128)S(1)}, u32[]{:S(2)}, u32[]{:S(2)}) %all-to-all-start.6) | async-done | bytes 32800 | tf_op jit(solution)/shard_map/all_to_all | solution.py:1198
  127.2 3.5 %stage_first.1 = (bf16[8,128,256]{2,1,0:T(8,128)(2,1)S(1)}, f32[16,4,128]{2,1,0:T(4,128)}, bf16[10,128,256]{2,1,0:T(8,128)(2,1)S(1)}, f32[8,128]{1,0:T(8,128)S(1)}, f32[1,4,128]{2,1,0:T(4,128)S(1)}) custom-call(f32[1,4,128]{2,1,0:T(4,128)S(1)} %get-tuple-element.143.refs_0_, f32[16,4,128]{2,1,0:T(4,128)S(1)} %all-to-all-done.6.refs_1_, ...), custom_call_target="tpu_custom_call" | custom-call | tf_op jit(solution)/shard_map/stage_first/pallas_call | solution.py:1179
  130.7 3.5 %all-to-all-start.7 = ((f32[16,4,128]{2,1,0:T(4,128)}), f32[16,4,128]{2,1,0:T(4,128)S(1)}, u32[]{:S(2)}, u32[]{:S(2)}) async-start(f32[16,4,128]{2,1,0:T(4,128)} %get-tuple-element.154), calls=%async_computation.7 | async-start | bytes 65536 | tf_op jit(solution)/shard_map/all_to_all | solution.py:1198
  134.8 2.6 %grads_first.1.refs_8_ = bf16[2,224,128]{2,1,0:T(8,128)(2,1)} custom-call(bf16[10,128,256]{2,1,0:T(8,128)(2,1)S(1)} %get-tuple-element.157.refs_0_, f32[8,128]{1,0:T(8,128)S(1)} %get-tuple-element.158.refs_1_, bf16[16,128]{1,0:T(8,128)(2,1)S(1)} %broadcast_in_dim.2.refs_2_, bf16[256,2048]{1,0:T(8,128)(2,1)} %get-tuple-element.159.refs_3_), custom_call_target="tpu_custom_call" | custom-call | tf_op jit(solution)/shard_map/grads_first/pallas_call | solution.py:1179
  137.9 2.9 %all-to-all-done.7.refs_1_ = f32[16,4,128]{2,1,0:T(4,128)S(1)} async-done(((f32[16,4,128]{2,1,0:T(4,128)}), f32[16,4,128]{2,1,0:T(4,128)S(1)}, u32[]{:S(2)}, u32[]{:S(2)}) %all-to-all-start.7) | async-done | bytes 32800 | tf_op jit(solution)/shard_map/all_to_all | solution.py:1198
  140.8 3.1 %stage_last.1 = (bf16[2,896,128]{2,1,0:T(8,128)(2,1)S(1)}, bf16[2,896,128]{2,1,0:T(8,128)(2,1)S(1)}, f32[1,1]{1,0:T(1,128)}) custom-call(f32[1,4,128]{2,1,0:T(4,128)S(1)} %get-tuple-element.153.refs_0_, f32[16,4,128]{2,1,0:T(4,128)S(1)} %all-to-all-done.7.refs_1_, bf16[8,128,256]{2,1,0:T(8,128)(2,1)} %get-tuple-element.148.refs_6_.refs_2_, ...), custom_call_target="tpu_custom_call" | custom-call | tf_op jit(solution)/shard_map/stage_last/pallas_call | solution.py:1179
  144.0 1.8 %collective-permute-done.11.refs_1_ = bf16[2,896,128]{2,1,0:T(8,128)(2,1)S(1)} collective-permute-done((bf16[2,896,128]{2,1,0:T(8,128)(2,1)S(1)}, bf16[2,896,128]{2,1,0:T(8,128)(2,1)S(1)}, u32[]{:S(2)}, u32[]{:S(2)}) %collective-permute-start.11) | collective-permute-done | bytes 458784 | tf_op jit(solution)/shard_map/ppermute | solution.py:1484
  145.9 17.5 %all_to_all.53.refs_0_ = bf16[16,112,128]{2,1,0:T(8,128)(2,1)S(1)} all-to-all(bf16[16,112,128]{2,1,0:T(8,128)(2,1)S(1)} %bitcast.10), channel_id=1, replica_groups={{0,2,4,6,8,10,12,14,16,18,20,22,24,26,28,30},{1,3,5,7,9,11,13,15,17,19,..., dimensions={0} | all-to-all | bytes 917504 | tf_op jit(solution)/shard_map/all_to_all | solution.py:1488
  163.5 11.1 %all_to_all.54 = bf16[8,112,128]{2,1,0:T(8,128)(2,1)S(1)} all-to-all(bf16[8,112,128]{2,1,0:T(8,128)(2,1)S(1)} %add_up.1), channel_id=1, replica_groups={{0,2,4,6,8,10,12,14},{1,3,5,7,9,11,13,15},{16,18,20,22,24,26,28,30},{17..., dimensions={0} | all-to-all | bytes 458752 | tf_op jit(solution)/shard_map/all_to_all | solution.py:1491
  (32 shorter events, 15.1 us)
Async XLA Ops:
  4.5 6.7 %collective-permute-start = (bf16[32,3584]{1,0:T(8,128)(2,1)S(1)}, bf16[32,3584]{1,0:T(8,128)(2,1)S(1)}, u32[]{:S(2)}, u32[]{:S(2)}) collective-permute-start(bf16[32,3584]{1,0:T(8,128)(2,1)S(1)} %get-tuple-element.92), channel_id=1, source_target_pairs={{0,1},{1,0},{2,3},{3,2},{4,5},{5,4},{6,7},{7,6},{8,9},{9,8},{10,11... | collective-permute-start | bytes 688136 | tf_op jit(solution)/shard_map/ppermute | solution.py:1207
  5.0 6.2 %collective-permute-start.1 = (bf16[32,3584]{1,0:T(8,128)(2,1)S(1)}, bf16[32,3584]{1,0:T(8,128)(2,1)S(1)}, u32[]{:S(2)}, u32[]{:S(2)}) collective-permute-start(bf16[32,3584]{1,0:T(8,128)(2,1)S(1)} %get-tuple-element.93), channel_id=1, source_target_pairs={{1,2},{2,1},{3,4},{4,3},{5,6},{6,5},{7,8},{8,7},{9,10},{10,9},{11,... | collective-permute-start | bytes 688136 | tf_op jit(solution)/shard_map/ppermute | solution.py:1207
  5.7 5.5 %collective-permute-start.2 = (bf16[512,128]{1,0:T(8,128)(2,1)S(1)}, bf16[512,128]{1,0:T(8,128)(2,1)S(1)}, u32[]{:S(2)}, u32[]{:S(2)}) collective-permute-start(bf16[512,128]{1,0:T(8,128)(2,1)S(1)} %get-tuple-element.94.refs_4_.refs_3_), channel_id=1, source_target_pairs={{0,16},{16,0},{1,17},{17,1},{2,18},{18,2},{3,19},{19,3},{4,20},{20... | collective-permute-start | bytes 393224 | tf_op jit(solution)/shard_map/ppermute | solution.py:1212
  29.7 10.4 %collective-permute-start.3 = (bf16[1488,128]{1,0:T(8,128)(2,1)S(1)}, bf16[1488,128]{1,0:T(8,128)(2,1)S(1)}, u32[]{:S(2)}, u32[]{:S(2)}) collective-permute-start(bf16[1488,128]{1,0:T(8,128)(2,1)S(1)} %pack_rest.1.refs_3_.refs_0_), channel_id=1, source_target_pairs={{0,16},{16,0},{1,17},{17,1},{2,18},{18,2},{3,19},{19,3},{4,20},{20... | collective-permute-start | bytes 1142792 | tf_op jit(solution)/shard_map/ppermute | solution.py:1212
  35.3 10.1 %all-to-all-start.1 = ((f32[16,4,128]{2,1,0:T(4,128)}), f32[16,4,128]{2,1,0:T(4,128)S(1)}, u32[]{:S(2)}, u32[]{:S(2)}) async-start(f32[16,4,128]{2,1,0:T(4,128)} %get-tuple-element.98), calls=%async_computation.1 | async-start | bytes 65536 | tf_op jit(solution)/shard_map/all_to_all | solution.py:1198
  50.4 11.9 %collective-permute-start.5 = (f32[128,512]{1,0:T(8,128)S(1)}, f32[128,512]{1,0:T(8,128)S(1)}, u32[]{:S(2)}, u32[]{:S(2)}) collective-permute-start(f32[128,512]{1,0:T(8,128)S(1)} %get-tuple-element.106), channel_id=1, source_target_pairs={{1,2},{2,1},{3,4},{4,3},{5,6},{6,5},{7,8},{8,7},{9,10},{10,9},{11,... | collective-permute-start | bytes 786440 | tf_op jit(solution)/shard_map/ppermute | solution.py:1207
  51.1 11.2 %collective-permute-start.4 = (f32[128,512]{1,0:T(8,128)S(1)}, f32[128,512]{1,0:T(8,128)S(1)}, u32[]{:S(2)}, u32[]{:S(2)}) collective-permute-start(f32[128,512]{1,0:T(8,128)S(1)} %get-tuple-element.106), channel_id=1, source_target_pairs={{0,1},{1,0},{2,3},{3,2},{4,5},{5,4},{6,7},{7,6},{8,9},{9,8},{10,11... | collective-permute-start | bytes 786440 | tf_op jit(solution)/shard_map/ppermute | solution.py:1207
  82.9 12.1 %collective-permute-start.6 = (bf16[128,768]{1,0:T(8,128)(2,1)S(1)}, bf16[128,768]{1,0:T(8,128)(2,1)S(1)}, u32[]{:S(2)}, u32[]{:S(2)}) collective-permute-start(bf16[128,768]{1,0:T(8,128)(2,1)S(1)} %get-tuple-element.120), channel_id=1, source_target_pairs={{0,1},{1,0},{2,3},{3,2},{4,5},{5,4},{6,7},{7,6},{8,9},{9,8},{10,11... | collective-permute-start | bytes 589832 | tf_op jit(solution)/shard_map/ppermute | solution.py:1207
  83.0 12.1 %collective-permute-start.7 = (bf16[128,768]{1,0:T(8,128)(2,1)S(1)}, bf16[128,768]{1,0:T(8,128)(2,1)S(1)}, u32[]{:S(2)}, u32[]{:S(2)}) collective-permute-start(bf16[128,768]{1,0:T(8,128)(2,1)S(1)} %get-tuple-element.121), channel_id=1, source_target_pairs={{1,2},{2,1},{3,4},{4,3},{5,6},{6,5},{7,8},{8,7},{9,10},{10,9},{11,... | collective-permute-start | bytes 589832 | tf_op jit(solution)/shard_map/ppermute | solution.py:1207
  83.7 11.4 %all-to-all-start.4 = ((f32[16,4,128]{2,1,0:T(4,128)}), f32[16,4,128]{2,1,0:T(4,128)S(1)}, u32[]{:S(2)}, u32[]{:S(2)}) async-start(f32[16,4,128]{2,1,0:T(4,128)} %get-tuple-element.119), calls=%async_computation.4 | async-start | bytes 65536 | tf_op jit(solution)/shard_map/all_to_all | solution.py:1198
  100.8 12.1 %collective-permute-start.8 = (bf16[128,768]{1,0:T(8,128)(2,1)S(1)}, bf16[128,768]{1,0:T(8,128)(2,1)S(1)}, u32[]{:S(2)}, u32[]{:S(2)}) collective-permute-start(bf16[128,768]{1,0:T(8,128)(2,1)S(1)} %get-tuple-element.132), channel_id=1, source_target_pairs={{0,1},{1,0},{2,3},{3,2},{4,5},{5,4},{6,7},{7,6},{8,9},{9,8},{10,11... | collective-permute-start | bytes 589832 | tf_op jit(solution)/shard_map/ppermute | solution.py:1207
  100.9 12.1 %collective-permute-start.9 = (bf16[128,768]{1,0:T(8,128)(2,1)S(1)}, bf16[128,768]{1,0:T(8,128)(2,1)S(1)}, u32[]{:S(2)}, u32[]{:S(2)}) collective-permute-start(bf16[128,768]{1,0:T(8,128)(2,1)S(1)} %get-tuple-element.133), channel_id=1, source_target_pairs={{1,2},{2,1},{3,4},{4,3},{5,6},{6,5},{7,8},{8,7},{9,10},{10,9},{11,... | collective-permute-start | bytes 589832 | tf_op jit(solution)/shard_map/ppermute | solution.py:1207
  101.6 11.4 %all-to-all-start.5 = ((f32[16,4,128]{2,1,0:T(4,128)}), f32[16,4,128]{2,1,0:T(4,128)S(1)}, u32[]{:S(2)}, u32[]{:S(2)}) async-start(f32[16,4,128]{2,1,0:T(4,128)} %get-tuple-element.131), calls=%async_computation.5 | async-start | bytes 65536 | tf_op jit(solution)/shard_map/all_to_all | solution.py:1198
  117.1 10.1 %all-to-all-start.6 = ((f32[16,4,128]{2,1,0:T(4,128)}), f32[16,4,128]{2,1,0:T(4,128)S(1)}, u32[]{:S(2)}, u32[]{:S(2)}) async-start(f32[16,4,128]{2,1,0:T(4,128)} %get-tuple-element.144), calls=%async_computation.6 | async-start | bytes 65536 | tf_op jit(solution)/shard_map/all_to_all | solution.py:1198
  130.7 10.1 %all-to-all-start.7 = ((f32[16,4,128]{2,1,0:T(4,128)}), f32[16,4,128]{2,1,0:T(4,128)S(1)}, u32[]{:S(2)}, u32[]{:S(2)}) async-start(f32[16,4,128]{2,1,0:T(4,128)} %get-tuple-element.154), calls=%async_computation.7 | async-start | bytes 65536 | tf_op jit(solution)/shard_map/all_to_all | solution.py:1198
  134.2 3.7 %collective-permute-start.10 = (f32[8,128]{1,0:T(8,128)S(1)}, f32[8,128]{1,0:T(8,128)S(1)}, u32[]{:S(2)}, u32[]{:S(2)}) collective-permute-start(f32[8,128]{1,0:T(8,128)S(1)} %get-tuple-element.160.refs_9_), channel_id=1, source_target_pairs={{0,16},{16,0},{1,17},{17,1},{2,18},{18,2},{3,19},{19,3},{4,20},{20... | collective-permute-start | bytes 12296 | tf_op jit(solution)/shard_map/ppermute | solution.py:1420
  143.9 1.9 %collective-permute-start.11 = (bf16[2,896,128]{2,1,0:T(8,128)(2,1)S(1)}, bf16[2,896,128]{2,1,0:T(8,128)(2,1)S(1)}, u32[]{:S(2)}, u32[]{:S(2)}) collective-permute-start(bf16[2,896,128]{2,1,0:T(8,128)(2,1)S(1)} %get-tuple-element.163), channel_id=1, source_target_pairs={{0,1},{1,0},{2,3},{3,2},{4,5},{5,4},{6,7},{7,6},{8,9},{9,8},{10,11... | collective-permute-start | bytes 1376264 | tf_op jit(solution)/shard_map/ppermute | solution.py:1484
  174.6 1.5 collective-permute-start.12

commit v4 on v3

--- a/solution.py
+++ b/solution.py
@@ -316,13 +316,12 @@
     return mm_nt(place(size, size, 0), value).astype(BF16)
 
 
-def tap_of(pieces, offset, index, size, paired=False):
+def tap_of(pieces, offset, index, size, side=1):
     each = size // len(pieces)
-    start = offset + (index // 2 if paired else index) * each
+    start = offset + index // side * each
     tap = jnp.concatenate([piece[start : start + each, :] for piece in pieces], axis=0)
-    if paired:
-        tap = tap[:, 64 * (index % 2) : 64 * (index % 2) + 64]
-    return tap.astype(BF16)
+    width = 128 // side
+    return tap[:, width * (index % side) : width * (index % side + 1)].astype(BF16)
 
 
 def in_order(scal, pieces):
@@ -360,10 +359,11 @@
                 value = shard.spot[t]
                 if swapped:
                     value = mm_nt(place(value.shape[1], value.shape[1], 0), value.astype(BF16))
-                if value.shape[1] == 64:
-                    lanes = slice(64 * (t % 2), 64 * (t % 2) + 64)
-                    scratch[start : start + value.shape[0], lanes] = value
-                    start += rows if t % 2 or t == taps - 1 else 0
+                if value.shape[1] in (24, 64):
+                    side = 4 if value.shape[1] == 24 else 2
+                    low = t % side * (128 // side)
+                    scratch[start : start + value.shape[0], low : low + value.shape[1]] = value
+                    start += rows if t % side == side - 1 or t == taps - 1 else 0
                 else:
                     scratch[start : start + value.shape[0], : value.shape[1]] = value
                     start += rows
@@ -379,7 +379,7 @@
 
     def taps_of(size, paired=False):
         nonlocal start
-        taps = [tap_of(pieces, start, t, size, paired) for t in range(9)]
+        taps = [tap_of(pieces, start, t, size, 2 if paired else 1) for t in range(9)]
         start += (5 if paired else 9) * (size // count)
         return taps
 
@@ -406,7 +406,12 @@
     for a in range(3):
         rows.append(jnp.concatenate(taps[3 * a : 3 * a + 3] + [blank], axis=1))
         rows.append(jnp.concatenate([blank] + taps[3 * a : 3 * a + 3], axis=1))
-    both(jnp.concatenate(rows, axis=0), wup, wup_t)
+    up = jnp.concatenate(rows, axis=0)
+    give(wup, up)
+    turned = flipped(up).astype(F32)
+    turned = jnp.concatenate([turned[:128], turned[128:256] + turned[256:384], turned[384:]], axis=0)
+    a0, a1, a2 = turned[:, :128], turned[:, 128:256], turned[:, 256:]
+    give(wup_t, jnp.concatenate([a0, a0 + a1, a1 + a2, a2], axis=1).astype(BF16))
     taps = []
     width = 64 // count
     for t in range(9):
@@ -475,7 +480,7 @@
 def stage_a(scal, got_a, got_b, own, done, *refs):
     *pieces, act, stats, kept, line_a, line_b, above, below = refs
     pieces = in_order(scal, pieces)
-    weights = fine_matrix([tap_of(pieces, 0, t, 64) for t in range(9)], 32)
+    weights = fine_matrix([tap_of(pieces, 0, t, 64, 4) for t in range(9)], 32)
     give(line_a, marked(scal, got_a))
     give(line_b, marked(scal, got_b))
     above[...] = pick(scal, whole(got_a), whole(got_b))
@@ -524,8 +529,8 @@
     give(totals, total_stats(stats_a)[None])
     count = len(pieces)
     pieces = in_order(scal, pieces)
-    start = 9 * (64 // count)
-    first = fine_matrix([tap_of(pieces, start, t, 64, True) for t in range(9)], 64)
+    start = 3 * (64 // count)
+    first = fine_matrix([tap_of(pieces, start, t, 64, 2) for t in range(9)], 64)
     start += 5 * (64 // count)
     wfirst[...] = first
     give(wfirst_t, flipped(first))
@@ -692,10 +697,10 @@
     value = pairs[...]
     high = value.astype(BF16)
     low = (value - high.astype(F32)).astype(BF16)
-    back_order = interleave(True)
     sigma, skip, out_scale, weight, coef = [
         figures.spot[k : k + 1, 0:1] for k in (0, 1, 2, 4, 5)
     ]
+    back_order = interleave(True)
     pairs[...] = mm(high, back_order) + mm(low, back_order)
     blank = jnp.zeros((4, 512), F32)
     loss_sum = jnp.zeros((12, 512), F32)
@@ -837,14 +842,11 @@
     wup_t.wait(1)
     weights = whole(wup_t)
     gk = {}
-    half = {}
-    for r in range(-2, ROWS + 2):
-        taps = mm(weights, stack_rows(g, r))
-        half[r] = taps[128:256] + taps[256:384] + from_right(taps[:128]) + from_left(taps[384:])
-        if r % 2:
-            value = masked(half.pop(r - 1) + half.pop(r), r // 2, CROWS, scal)
-            gk[r // 2] = value.astype(BF16)
-            put(grad_coarse, r // 2, gk[r // 2])
+    for r in range(-1, CROWS + 1):
+        rows = jnp.concatenate([g[2 * r + 2], g[2 * r + 1], g[2 * r], g[2 * r - 1]], axis=0)
+        value = coarse_untap(mm(weights, rows))
+        gk[r] = masked(value, r, CROWS, scal).astype(BF16)
+        put(grad_coarse, r, gk[r])
     wcoarse_t.wait(1)
     hats_c.wait(1)
     stats_c.wait(1)
@@ -1252,7 +1254,7 @@
         total = 0
         for item, (taps, size, swapped) in zip(shards, widths):
             paired = taps == 9 and item.shape[2] == 64
-            total += (5 if paired else taps) * size
+            total += (3 if swapped else 5 if paired else taps) * size
         return widths, total
 
     fine_o, coarse_o = input_kernel.shape[1], down_kernel.shape[1]
@@ -1314,7 +1316,7 @@
             Saved(shape(384, 256, dtype=BF16)), Saved(shape(256, 384, dtype=BF16)),
             Saved(shape(384, 192, dtype=BF16)), Saved(shape(192, 384, dtype=BF16)),
             Saved(shape(384, 384, dtype=BF16)), Saved(shape(384, 384, dtype=BF16)),
-            Saved(shape(384, 512, dtype=BF16)), Saved(shape(512, 384, dtype=BF16)),
+            Saved(shape(384, 512, dtype=BF16)), Saved(shape(384, 512, dtype=BF16)),
             Saved(shape(96, 256, dtype=BF16)), Saved(shape(256, 96, dtype=BF16)),
         ],
         None,

time: 178 us -> 178 us (level)
  no operation moved by 1% of the time
where the time goes in v4:
time: 178 us; the launch traced here: 177 us
  blocking collectives  63.9 us (36%)
  Pallas kernels  58.3 us (33%)
  starting transfers between devices  29.9 us (17%)
  waiting for transfers between devices  22.3 us (13%)
  between operations  1.94 us (1%)
    pallas_call x19, Pallas kernels, run(): pl.pallas_call(body, out_shape=tuple(out_shapes), in_specs=in_specs, out_...  58.3 us
    all_to_all x3, blocking collectives, sum_parts(): return lax.all_to_all(stats, 'rows', 0, 0)  35.3 us
    all_to_all x5, starting transfers between devices, sum_parts(): return lax.all_to_all(stats, 'rows', 0, 0)  20 us
    all_to_all x1, blocking collectives, per_device(): got = lax.all_to_all(both, ('fsdp', 'rows'), 0, 0, axis_index_groups=cores)  17.5 us
    all_to_all x5, waiting for transfers between devices, sum_parts(): return lax.all_to_all(stats, 'rows', 0, 0)  16.2 us
    all_to_all x1, blocking collectives, per_device(): mine = lax.all_to_all(mine, 'rows', 0, 0, axis_index_groups=cores)  11.1 us
    ppermute x2, starting transfers between devices, gather_packed(): return [packed, lax.ppermute(packed, 'fsdp', [(0, 1), (1, 0)])]  4.07 us
  transfers between devices with their start and end apart: 18, of which 10 were waited for; matrix products, arithmetic and copies ran while one was open for 0% of the time, Pallas kernels for 11%

profile of v4, /device:TPU:0, one launch (start us, length us, event | category | flops | bytes accessed | tf_op | source)
XLA Modules:
  0.0 176.5 jit_solution(152679733841759827)
XLA Ops:
  1.5 3.0 %enter.1 = (bf16[320,128]{1,0:T(8,128)(2,1)S(1)}, bf16[32,4096]{1,0:T(8,128)(2,1)S(1)}, bf16[32,3584]{1,0:T(8,128)(2,1)S(1)}, bf16[32,3584]{1,0:T(8,128)(2,1)S(1)}, f32[8,128]{1,0:T(8,128)}) custom-call(f32[6]{0:T(128)S(1)} %stack.24.refs_0_, f32[96,512]{1,0:T(8,128)} %bitcast.13, f32[96,512]{1,0:T(8,128)} %bitcast.17, f32[96,512]{1,0:T(8,128)} %bitcast.15, ...), custom_call_target="tpu_custom_call" | custom-call | tf_op jit(solution)/shard_map/enter/pallas_call | solution.py:1181
  5.7 2.6 %collective-permute-start.2 = (bf16[320,128]{1,0:T(8,128)(2,1)S(1)}, bf16[320,128]{1,0:T(8,128)(2,1)S(1)}, u32[]{:S(2)}, u32[]{:S(2)}) collective-permute-start(bf16[320,128]{1,0:T(8,128)(2,1)S(1)} %get-tuple-element.94.refs_4_.refs_3_), channel_id=1, source_target_pairs={{0,16},{16,0},{1,17},{17,1},{2,18},{18,2},{3,19},{19,3},{4,20},{20... | collective-permute-start | bytes 245768 | tf_op jit(solution)/shard_map/ppermute | solution.py:1214
  10.7 2.4 %stage_a.1 = (f32[20,128,256]{2,1,0:T(8,128)S(1)}, f32[16,4,128]{2,1,0:T(4,128)S(1)}, bf16[128,2560]{1,0:T(8,128)(2,1)}, f32[16,512]{1,0:T(8,128)}, f32[16,512]{1,0:T(8,128)}) custom-call(bf16[32,3584]{1,0:T(8,128)(2,1)S(1)} %collective-permute-done.refs_0_, bf16[32,3584]{1,0:T(8,128)(2,1)S(1)} %collective-permute-done.1.refs_1_, ...), custom_call_target="tpu_custom_call" | custom-call | tf_op jit(solution)/shard_map/stage_a/pallas_call | solution.py:1181
  13.2 16.6 %all_to_all.50.refs_0_ = f32[16,4,128]{2,1,0:T(4,128)S(1)} all-to-all(f32[16,4,128]{2,1,0:T(4,128)S(1)} %get-tuple-element.95), channel_id=1, replica_groups=mesh['fsdp'=2,'rows'=16] {'rows'}, dimensions={0} | all-to-all | bytes 65536 | tf_op jit(solution)/shard_map/all_to_all | solution.py:1200
  31.5 3.9 %stage_b.1 = (f32[18,128,256]{2,1,0:T(8,128)S(1)}, f32[16,4,128]{2,1,0:T(4,128)}, bf16[256,2048]{1,0:T(8,128)(2,1)}, bf16[8,128,256]{2,1,0:T(8,128)(2,1)}, f32[1...) custom-call(f32[16,4,128]{2,1,0:T(4,128)S(1)} %all_to_all.50.refs_0_, ...), custom_call_target="tpu_custom_call" | custom-call | tf_op jit(solution)/shard_map/stage_b/pallas_call | solution.py:1181
  35.4 3.5 %all-to-all-start.1 = ((f32[16,4,128]{2,1,0:T(4,128)}), f32[16,4,128]{2,1,0:T(4,128)S(1)}, u32[]{:S(2)}, u32[]{:S(2)}) async-start(f32[16,4,128]{2,1,0:T(4,128)} %get-tuple-element.98), calls=%async_computation.1 | async-start | bytes 65536 | tf_op jit(solution)/shard_map/all_to_all | solution.py:1200
  40.2 2.7 %prepare_rest.1 = (bf16[384,256]{1,0:T(8,128)(2,1)}, bf16[256,384]{1,0:T(8,128)(2,1)}, bf16[384,192]{1,0:T(8,128)(2,1)}, bf16[192,384]{1,0:T(8,128)(2,1)}, bf16[...) custom-call(bf16[1488,128]{1,0:T(8,128)(2,1)S(1)} %pack_rest.1.refs_, ...), custom_call_target="tpu_custom_call" | custom-call | tf_op jit(solution)/shard_map/prepare_rest/pallas_call | solution.py:1181
  42.9 2.6 %all-to-all-done.1.refs_0_ = f32[16,4,128]{2,1,0:T(4,128)S(1)} async-done(((f32[16,4,128]{2,1,0:T(4,128)}), f32[16,4,128]{2,1,0:T(4,128)S(1)}, u32[]{:S(2)}, u32[]{:S(2)}) %all-to-all-start.1) | async-done | bytes 32800 | tf_op jit(solution)/shard_map/all_to_all | solution.py:1200
  45.5 5.0 %stage_c.1 = (f32[14,128,256]{2,1,0:T(8,128)S(1)}, f32[6,128,256]{2,1,0:T(8,128)S(1)}, f32[128,512]{1,0:T(8,128)S(1)}, f32[16,4,128]{2,1,0:T(4,128)S(1)}, bf16[2...) custom-call(f32[16,4,128]{2,1,0:T(4,128)S(1)} %all-to-all-done.1.refs_0_,, ...), custom_call_target="tpu_custom_call" | custom-call | tf_op jit(solution)/shard_map/stage_c/pallas_call | solution.py:1181
  53.0 9.4 %all_to_all.51.refs_0_ = f32[16,4,128]{2,1,0:T(4,128)S(1)} all-to-all(f32[16,4,128]{2,1,0:T(4,128)S(1)} %get-tuple-element.104), channel_id=1, replica_groups=mesh['fsdp'=2,'rows'=16] {'rows'}, dimensions={0} | all-to-all | bytes 65536 | tf_op jit(solution)/shard_map/all_to_all | solution.py:1200
  62.4 5.7 %stage_d.1 = (f32[14,128,256]{2,1,0:T(8,128)S(1)}, bf16[8,128,256]{2,1,0:T(8,128)(2,1)}, f32[16,4,128]{2,1,0:T(4,128)S(1)}, bf16[384,1024]{1,0:T(8,128)(2,1)}, b...) custom-call(f32[16,4,128]{2,1,0:T(4,128)S(1)} %all_to_all.51.refs_0_, bf16[384,384]{1,0:T(8,128)(2,1)} %get-tuple-element.105.refs_1_, ...), custom_call_target="tpu_custom_call" | custom-call | tf_op jit(solution)/shard_map/stage_d/pallas_call | solution.py:1181
  68.1 9.2 %all_to_all.52.refs_0_ = f32[16,4,128]{2,1,0:T(4,128)S(1)} all-to-all(f32[16,4,128]{2,1,0:T(4,128)S(1)} %get-tuple-element.110), channel_id=1, replica_groups=mesh['fsdp'=2,'rows'=16] {'rows'}, dimensions={0} | all-to-all | bytes 65536 | tf_op jit(solution)/shard_map/all_to_all | solution.py:1200
  77.3 5.7 %stage_out.1 = (f32[96,512]{1,0:T(8,128)}, bf16[8,128,256]{2,1,0:T(8,128)(2,1)S(1)}, bf16[128,768]{1,0:T(8,128)(2,1)S(1)}, bf16[128,768]{1,0:T(8,128)(2,1)S(1)},...) custom-call(f32[16,4,128]{2,1,0:T(4,128)S(1)} %all_to_all.52.refs_0_, ...), custom_call_target="tpu_custom_call" | custom-call | tf_op jit(solution)/shard_map/stage_out/pallas_call | solution.py:1181
  83.8 4.7 %all-to-all-start.4 = ((f32[16,4,128]{2,1,0:T(4,128)}), f32[16,4,128]{2,1,0:T(4,128)S(1)}, u32[]{:S(2)}, u32[]{:S(2)}) async-start(f32[16,4,128]{2,1,0:T(4,128)} %get-tuple-element.119), calls=%async_computation.4 | async-start | bytes 65536 | tf_op jit(solution)/shard_map/all_to_all | solution.py:1200
  88.6 2.4 %grads_out.1.refs_10_.refs_4_ = bf16[2,80,128]{2,1,0:T(8,128)(2,1)} custom-call(bf16[10,32,256]{2,1,0:T(8,128)(2,1)S(1)} %get-tuple-element.128.refs_0_, bf16[256,2048]{1,0:T(8,128)(2,1)} %get-tuple-element.129.refs_1_), custom_call_target="tpu_custom_call" | custom-call | tf_op jit(solution)/shard_map/grads_out/pallas_call | solution.py:1181
  91.0 4.2 %all-to-all-done.4.refs_1_ = f32[16,4,128]{2,1,0:T(4,128)S(1)} async-done(((f32[16,4,128]{2,1,0:T(4,128)}), f32[16,4,128]{2,1,0:T(4,128)S(1)}, u32[]{:S(2)}, u32[]{:S(2)}) %all-to-all-start.4) | async-done | bytes 32800 | tf_op jit(solution)/shard_map/all_to_all | solution.py:1200
  95.2 4.7 %stage_up.1 = (bf16[12,128,256]{2,1,0:T(8,128)(2,1)S(1)}, bf16[4,128,256]{2,1,0:T(8,128)(2,1)S(1)}, bf16[6,128,256]{2,1,0:T(8,128)(2,1)S(1)}, bf16[128,768]{1,0:...) custom-call(f32[1,4,128]{2,1,0:T(4,128)S(1)} %get-tuple-element.118., ...), custom_call_target="tpu_custom_call" | custom-call | tf_op jit(solution)/shard_map/stage_up/pallas_call | solution.py:1181
  100.6 4.8 %all-to-all-start.5 = ((f32[16,4,128]{2,1,0:T(4,128)}), f32[16,4,128]{2,1,0:T(4,128)S(1)}, u32[]{:S(2)}, u32[]{:S(2)}) async-start(f32[16,4,128]{2,1,0:T(4,128)} %get-tuple-element.131), calls=%async_computation.5 | async-start | bytes 65536 | tf_op jit(solution)/shard_map/all_to_all | solution.py:1200
  105.4 3.6 %grads_up.1.refs_12_.refs_6_ = bf16[2,944,128]{2,1,0:T(8,128)(2,1)} custom-call(bf16[12,128,256]{2,1,0:T(8,128)(2,1)S(1)} %get-tuple-element.137.refs_0_.refs_8_, bf16[6,128,256]{2,1,0:T(8,128)(2,1)S(1)} %get-tuple-element.135.refs_1_.refs_6_, bf16[384,1024]{1,0:T(8,128)(2,1)} %get-tuple-element.141.refs_2_, bf16[384,1024]{1,0:T(8,128)(2,1)} %get-tuple-element.142.refs_3_, ...), custom_call_target="tpu_custom_call" | custom-call | tf_op jit(solution)/shard_map/grads_up/pallas_call | solution.py:1181
  109.0 3.0 %all-to-all-done.5.refs_1_ = f32[16,4,128]{2,1,0:T(4,128)S(1)} async-done(((f32[16,4,128]{2,1,0:T(4,128)}), f32[16,4,128]{2,1,0:T(4,128)S(1)}, u32[]{:S(2)}, u32[]{:S(2)}) %all-to-all-start.5) | async-done | bytes 32800 | tf_op jit(solution)/shard_map/all_to_all | solution.py:1200
  112.0 4.1 %stage_down.1 = (bf16[10,128,256]{2,1,0:T(8,128)(2,1)S(1)}, bf16[10,128,256]{2,1,0:T(8,128)(2,1)S(1)}, f32[16,4,128]{2,1,0:T(4,128)}, bf16[6,128,256]{2,1,0:T(8,128)(2,1)}, f32[1,4,128]{2,1,0:T(4,128)S(1)}) custom-call(f32[1,4,128]{2,1,0:T(4,128)S(1)} %get-tuple-element.130.refs_0_, f32[16,4,128]{2,1,0:T(4,128)S(1)} %all-to-all-done.5.refs_1_, ...), custom_call_target="tpu_custom_call" | custom-call | tf_op jit(solution)/shard_map/stage_down/pallas_call | solution.py:1181
  116.2 3.5 %all-to-all-start.6 = ((f32[16,4,128]{2,1,0:T(4,128)}), f32[16,4,128]{2,1,0:T(4,128)S(1)}, u32[]{:S(2)}, u32[]{:S(2)}) async-start(f32[16,4,128]{2,1,0:T(4,128)} %get-tuple-element.144), calls=%async_computation.6 | async-start | bytes 65536 | tf_op jit(solution)/shard_map/all_to_all | solution.py:1200
  119.7 3.1 %grads_down.1.refs_7_ = bf16[2,480,128]{2,1,0:T(8,128)(2,1)} custom-call(bf16[10,128,256]{2,1,0:T(8,128)(2,1)S(1)} %get-tuple-element.149.refs_0_.refs_4_, bf16[6,128,256]{2,1,0:T(8,128)(2,1)} %get-tuple-element.150.refs_1_, bf16[192,1024]{1,0:T(8,128)(2,1)} %get-tuple-element.151.refs_2_, bf16[256,2048]{1,0:T(8,128)(2,1)} %get-tuple-element.152.refs_3_), custom_call_target="tpu_custom_call" | custom-call | tf_op jit(solution)/shard_map/grads_down/pallas_call | solution.py:1181
  122.8 3.5 %all-to-all-done.6.refs_1_ = f32[16,4,128]{2,1,0:T(4,128)S(1)} async-done(((f32[16,4,128]{2,1,0:T(4,128)}), f32[16,4,128]{2,1,0:T(4,128)S(1)}, u32[]{:S(2)}, u32[]{:S(2)}) %all-to-all-start.6) | async-done | bytes 32800 | tf_op jit(solution)/shard_map/all_to_all | solution.py:1200
  126.3 3.5 %stage_first.1 = (bf16[8,128,256]{2,1,0:T(8,128)(2,1)S(1)}, f32[16,4,128]{2,1,0:T(4,128)}, bf16[10,128,256]{2,1,0:T(8,128)(2,1)S(1)}, f32[8,128]{1,0:T(8,128)S(1)}, f32[1,4,128]{2,1,0:T(4,128)S(1)}) custom-call(f32[1,4,128]{2,1,0:T(4,128)S(1)} %get-tuple-element.143.refs_0_, f32[16,4,128]{2,1,0:T(4,128)S(1)} %all-to-all-done.6.refs_1_, ...), custom_call_target="tpu_custom_call" | custom-call | tf_op jit(solution)/shard_map/stage_first/pallas_call | solution.py:1181
  129.8 3.5 %all-to-all-start.7 = ((f32[16,4,128]{2,1,0:T(4,128)}), f32[16,4,128]{2,1,0:T(4,128)S(1)}, u32[]{:S(2)}, u32[]{:S(2)}) async-start(f32[16,4,128]{2,1,0:T(4,128)} %get-tuple-element.154), calls=%async_computation.7 | async-start | bytes 65536 | tf_op jit(solution)/shard_map/all_to_all | solution.py:1200
  133.9 2.6 %grads_first.1.refs_8_ = bf16[2,224,128]{2,1,0:T(8,128)(2,1)} custom-call(bf16[10,128,256]{2,1,0:T(8,128)(2,1)S(1)} %get-tuple-element.157.refs_0_, f32[8,128]{1,0:T(8,128)S(1)} %get-tuple-element.158.refs_1_, bf16[16,128]{1,0:T(8,128)(2,1)S(1)} %broadcast_in_dim.2.refs_2_, bf16[256,2048]{1,0:T(8,128)(2,1)} %get-tuple-element.159.refs_3_), custom_call_target="tpu_custom_call" | custom-call | tf_op jit(solution)/shard_map/grads_first/pallas_call | solution.py:1181
  137.0 2.9 %all-to-all-done.7.refs_1_ = f32[16,4,128]{2,1,0:T(4,128)S(1)} async-done(((f32[16,4,128]{2,1,0:T(4,128)}), f32[16,4,128]{2,1,0:T(4,128)S(1)}, u32[]{:S(2)}, u32[]{:S(2)}) %all-to-all-start.7) | async-done | bytes 32800 | tf_op jit(solution)/shard_map/all_to_all | solution.py:1200
  139.9 3.1 %stage_last.1 = (bf16[2,896,128]{2,1,0:T(8,128)(2,1)S(1)}, bf16[2,896,128]{2,1,0:T(8,128)(2,1)S(1)}, f32[1,1]{1,0:T(1,128)}) custom-call(f32[1,4,128]{2,1,0:T(4,128)S(1)} %get-tuple-element.153.refs_0_, f32[16,4,128]{2,1,0:T(4,128)S(1)} %all-to-all-done.7.refs_1_, bf16[8,128,256]{2,1,0:T(8,128)(2,1)} %get-tuple-element.148.refs_6_.refs_2_, ...), custom_call_target="tpu_custom_call" | custom-call | tf_op jit(solution)/shard_map/stage_last/pallas_call | solution.py:1181
  143.1 1.8 %collective-permute-done.11.refs_1_ = bf16[2,896,128]{2,1,0:T(8,128)(2,1)S(1)} collective-permute-done((bf16[2,896,128]{2,1,0:T(8,128)(2,1)S(1)}, bf16[2,896,128]{2,1,0:T(8,128)(2,1)S(1)}, u32[]{:S(2)}, u32[]{:S(2)}) %collective-permute-start.11) | collective-permute-done | bytes 458784 | tf_op jit(solution)/shard_map/ppermute | solution.py:1486
  145.0 17.5 %all_to_all.53.refs_0_ = bf16[16,112,128]{2,1,0:T(8,128)(2,1)S(1)} all-to-all(bf16[16,112,128]{2,1,0:T(8,128)(2,1)S(1)} %bitcast.10), channel_id=1, replica_groups={{0,2,4,6,8,10,12,14,16,18,20,22,24,26,28,30},{1,3,5,7,9,11,13,15,17,19,..., dimensions={0} | all-to-all | bytes 917504 | tf_op jit(solution)/shard_map/all_to_all | solution.py:1490
  162.6 11.1 %all_to_all.54 = bf16[8,112,128]{2,1,0:T(8,128)(2,1)S(1)} all-to-all(bf16[8,112,128]{2,1,0:T(8,128)(2,1)S(1)} %add_up.1), channel_id=1, replica_groups={{0,2,4,6,8,10,12,14},{1,3,5,7,9,11,13,15},{16,18,20,22,24,26,28,30},{17..., dimensions={0} | all-to-all | bytes 458752 | tf_op jit(solution)/shard_map/all_to_all | solution.py:1493
  (32 shorter events, 14.5 us)
Async XLA Ops:
  4.5 6.2 %collective-permute-start = (bf16[32,3584]{1,0:T(8,128)(2,1)S(1)}, bf16[32,3584]{1,0:T(8,128)(2,1)S(1)}, u32[]{:S(2)}, u32[]{:S(2)}) collective-permute-start(bf16[32,3584]{1,0:T(8,128)(2,1)S(1)} %get-tuple-element.92), channel_id=1, source_target_pairs={{0,1},{1,0},{2,3},{3,2},{4,5},{5,4},{6,7},{7,6},{8,9},{9,8},{10,11... | collective-permute-start | bytes 688136 | tf_op jit(solution)/shard_map/ppermute | solution.py:1209
  5.0 5.7 %collective-permute-start.1 = (bf16[32,3584]{1,0:T(8,128)(2,1)S(1)}, bf16[32,3584]{1,0:T(8,128)(2,1)S(1)}, u32[]{:S(2)}, u32[]{:S(2)}) collective-permute-start(bf16[32,3584]{1,0:T(8,128)(2,1)S(1)} %get-tuple-element.93), channel_id=1, source_target_pairs={{1,2},{2,1},{3,4},{4,3},{5,6},{6,5},{7,8},{8,7},{9,10},{10,9},{11,... | collective-permute-start | bytes 688136 | tf_op jit(solution)/shard_map/ppermute | solution.py:1209
  5.7 5.0 %collective-permute-start.2 = (bf16[320,128]{1,0:T(8,128)(2,1)S(1)}, bf16[320,128]{1,0:T(8,128)(2,1)S(1)}, u32[]{:S(2)}, u32[]{:S(2)}) collective-permute-start(bf16[320,128]{1,0:T(8,128)(2,1)S(1)} %get-tuple-element.94.refs_4_.refs_3_), channel_id=1, source_target_pairs={{0,16},{16,0},{1,17},{17,1},{2,18},{18,2},{3,19},{19,3},{4,20},{20... | collective-permute-start | bytes 245768 | tf_op jit(solution)/shard_map/ppermute | solution.py:1214
  29.8 10.4 %collective-permute-start.3 = (bf16[1488,128]{1,0:T(8,128)(2,1)S(1)}, bf16[1488,128]{1,0:T(8,128)(2,1)S(1)}, u32[]{:S(2)}, u32[]{:S(2)}) collective-permute-start(bf16[1488,128]{1,0:T(8,128)(2,1)S(1)} %pack_rest.1.refs_3_.refs_0_), channel_id=1, source_target_pairs={{0,16},{16,0},{1,17},{17,1},{2,18},{18,2},{3,19},{19,3},{4,20},{20... | collective-permute-start | bytes 1142792 | tf_op jit(solution)/shard_map/ppermute | solution.py:1214
  35.4 10.1 %all-to-all-start.1 = ((f32[16,4,128]{2,1,0:T(4,128)}), f32[16,4,128]{2,1,0:T(4,128)S(1)}, u32[]{:S(2)}, u32[]{:S(2)}) async-start(f32[16,4,128]{2,1,0:T(4,128)} %get-tuple-element.98), calls=%async_computation.1 | async-start | bytes 65536 | tf_op jit(solution)/shard_map/all_to_all | solution.py:1200
  50.6 11.9 %collective-permute-start.5 = (f32[128,512]{1,0:T(8,128)S(1)}, f32[128,512]{1,0:T(8,128)S(1)}, u32[]{:S(2)}, u32[]{:S(2)}) collective-permute-start(f32[128,512]{1,0:T(8,128)S(1)} %get-tuple-element.106), channel_id=1, source_target_pairs={{1,2},{2,1},{3,4},{4,3},{5,6},{6,5},{7,8},{8,7},{9,10},{10,9},{11,... | collective-permute-start | bytes 786440 | tf_op jit(solution)/shard_map/ppermute | solution.py:1209
  51.2 11.2 %collective-permute-start.4 = (f32[128,512]{1,0:T(8,128)S(1)}, f32[128,512]{1,0:T(8,128)S(1)}, u32[]{:S(2)}, u32[]{:S(2)}) collective-permute-start(f32[128,512]{1,0:T(8,128)S(1)} %get-tuple-element.106), channel_id=1, source_target_pairs={{0,1},{1,0},{2,3},{3,2},{4,5},{5,4},{6,7},{7,6},{8,9},{9,8},{10,11... | collective-permute-start | bytes 786440 | tf_op jit(solution)/shard_map/ppermute | solution.py:1209
  83.0 12.1 %collective-permute-start.6 = (bf16[128,768]{1,0:T(8,128)(2,1)S(1)}, bf16[128,768]{1,0:T(8,128)(2,1)S(1)}, u32[]{:S(2)}, u32[]{:S(2)}) collective-permute-start(bf16[128,768]{1,0:T(8,128)(2,1)S(1)} %get-tuple-element.120), channel_id=1, source_target_pairs={{0,1},{1,0},{2,3},{3,2},{4,5},{5,4},{6,7},{7,6},{8,9},{9,8},{10,11... | collective-permute-start | bytes 589832 | tf_op jit(solution)/shard_map/ppermute | solution.py:1209
  83.1 12.1 %collective-permute-start.7 = (bf16[128,768]{1,0:T(8,128)(2,1)S(1)}, bf16[128,768]{1,0:T(8,128)(2,1)S(1)}, u32[]{:S(2)}, u32[]{:S(2)}) collective-permute-start(bf16[128,768]{1,0:T(8,128)(2,1)S(1)} %get-tuple-element.121), channel_id=1, source_target_pairs={{1,2},{2,1},{3,4},{4,3},{5,6},{6,5},{7,8},{8,7},{9,10},{10,9},{11,... | collective-permute-start | bytes 589832 | tf_op jit(solution)/shard_map/ppermute | solution.py:1209
  83.8 11.4 %all-to-all-start.4 = ((f32[16,4,128]{2,1,0:T(4,128)}), f32[16,4,128]{2,1,0:T(4,128)S(1)}, u32[]{:S(2)}, u32[]{:S(2)}) async-start(f32[16,4,128]{2,1,0:T(4,128)} %get-tuple-element.119), calls=%async_computation.4 | async-start | bytes 65536 | tf_op jit(solution)/shard_map/all_to_all | solution.py:1200
  99.9 12.1 %collective-permute-start.8 = (bf16[128,768]{1,0:T(8,128)(2,1)S(1)}, bf16[128,768]{1,0:T(8,128)(2,1)S(1)}, u32[]{:S(2)}, u32[]{:S(2)}) collective-permute-start(bf16[128,768]{1,0:T(8,128)(2,1)S(1)} %get-tuple-element.132), channel_id=1, source_target_pairs={{0,1},{1,0},{2,3},{3,2},{4,5},{5,4},{6,7},{7,6},{8,9},{9,8},{10,11... | collective-permute-start | bytes 589832 | tf_op jit(solution)/shard_map/ppermute | solution.py:1209
  100.0 12.1 %collective-permute-start.9 = (bf16[128,768]{1,0:T(8,128)(2,1)S(1)}, bf16[128,768]{1,0:T(8,128)(2,1)S(1)}, u32[]{:S(2)}, u32[]{:S(2)}) collective-permute-start(bf16[128,768]{1,0:T(8,128)(2,1)S(1)} %get-tuple-element.133), channel_id=1, source_target_pairs={{1,2},{2,1},{3,4},{4,3},{5,6},{6,5},{7,8},{8,7},{9,10},{10,9},{11,... | collective-permute-start | bytes 589832 | tf_op jit(solution)/shard_map/ppermute | solution.py:1209
  100.6 11.4 %all-to-all-start.5 = ((f32[16,4,128]{2,1,0:T(4,128)}), f32[16,4,128]{2,1,0:T(4,128)S(1)}, u32[]{:S(2)}, u32[]{:S(2)}) async-start(f32[16,4,128]{2,1,0:T(4,128)} %get-tuple-element.131), calls=%async_computation.5 | async-start | bytes 65536 | tf_op jit(solution)/shard_map/all_to_all | solution.py:1200
  116.2 10.1 %all-to-all-start.6 = ((f32[16,4,128]{2,1,0:T(4,128)}), f32[16,4,128]{2,1,0:T(4,128)S(1)}, u32[]{:S(2)}, u32[]{:S(2)}) async-start(f32[16,4,128]{2,1,0:T(4,128)} %get-tuple-element.144), calls=%async_computation.6 | async-start | bytes 65536 | tf_op jit(solution)/shard_map/all_to_all | solution.py:1200
  129.8 10.1 %all-to-all-start.7 = ((f32[16,4,128]{2,1,0:T(4,128)}), f32[16,4,128]{2,1,0:T(4,128)S(1)}, u32[]{:S(2)}, u32[]{:S(2)}) async-start(f32[16,4,128]{2,1,0:T(4,128)} %get-tuple-element.154), calls=%async_computation.7 | async-start | bytes 65536 | tf_op jit(solution)/shard_map/all_to_all | solution.py:1200
  133.3 3.7 %collective-permute-start.10 = (f32[8,128]{1,0:T(8,128)S(1)}, f32[8,128]{1,0:T(8,128)S(1)}, u32[]{:S(2)}, u32[]{:S(2)}) collective-permute-start(f32[8,128]{1,0:T(8,128)S(1)} %get-tuple-element.160.refs_9_), channel_id=1, source_target_pairs={{0,16},{16,0},{1,17},{17,1},{2,18},{18,2},{3,19},{19,3},{4,20},{20... | collective-permute-start | bytes 12296 | tf_op jit(solution)/shard_map/ppermute | solution.py:1422
  143.0 1.9 %collective-permute-start.11 = (bf16[2,896,128]{2,1,0:T(8,128)(2,1)S(1)}, bf16[2,896,128]{2,1,0:T(8,128)(2,1)S(1)}, u32[]{:S(2)}, u32[]{:S(2)}) collective-permute-start(bf16[2,896,128]{2,1,0:T(8,128)(2,1)S(1)} %get-tuple-element.163), channel_id=1, source_target_pairs={{0,1},{1,0},{2,3},{3,2},{4,5},{5,4},{6,7},{7,6},{8,9},{9,8},{10,11... | collective-permute-start | bytes 1376264 | tf_op jit(solution)/shard_map/ppermute | solution.py:1486
  173.7 1.5 collective-permute-start.12

commit v5 on v4

--- a/solution.py
+++ b/solution.py
@@ -116,12 +116,12 @@
 
 def from_left(value):
     moved = pltpu.roll(value, 1, 1)
-    return jnp.where(lane(value.shape) == 0, 0.0, moved)
+    return jnp.where(lane(value.shape) == 0, jnp.zeros_like(moved), moved)
 
 
 def from_right(value):
     moved = pltpu.roll(value, value.shape[1] - 1, 1)
-    return jnp.where(lane(value.shape) == value.shape[1] - 1, 0.0, moved)
+    return jnp.where(lane(value.shape) == value.shape[1] - 1, jnp.zeros_like(moved), moved)
 
 
 def mm(left, right):
@@ -134,12 +134,14 @@
 
 def fine_taps(value):
     half = value.shape[0] // 2
+    value = value.astype(BF16)
     even, odd = value[:half], value[half:]
-    return jnp.concatenate([from_left(odd), value, from_right(even)], axis=0).astype(BF16)
+    return jnp.concatenate([from_left(odd), value, from_right(even)], axis=0)
 
 
 def coarse_taps(value):
-    return jnp.concatenate([from_left(value), value, from_right(value)], axis=0).astype(BF16)
+    value = value.astype(BF16)
+    return jnp.concatenate([from_left(value), value, from_right(value)], axis=0)
 
 
 def fine_untap(taps):
@@ -219,6 +221,7 @@
     if third is None:
         third = jnp.zeros((1, 128), F32)
     block = jnp.concatenate([first, second, third, jnp.zeros((1, 128), F32)], axis=0)
+    block = block[: ref.shape[1]]
     for index in range(ref.shape[0]):
         ref.spot[index] = block
     ref.finish()
@@ -499,7 +502,6 @@
             value = own.spot[:, r * 512 : (r + 1) * 512]
         else:
             value = below[:, (r - ROWS) * 512 : (r - ROWS + 1) * 512]
-        value = value.astype(F32)
         z = fine_taps(jnp.concatenate([value[:, :HALF], value[:, HALF:]], axis=0))
         if -1 <= r <= ROWS:
             put(kept, r, z)
@@ -594,7 +596,7 @@
         if i % 2:
             value = 0.25 * (half.pop(i - 1) + half.pop(i))
             value = masked(value, i // 2, CROWS, scal)
-            pooled[i // 2] = value.astype(BF16).astype(F32)
+            pooled[i // 2] = value
     weights = whole(wdown)
     parts = {}
     total = jnp.zeros((128, HALF), F32)
@@ -646,7 +648,7 @@
         if i > -3:
             value = spread(parts, i, i)[i] + ring[i]
             del parts[i - 1]
-            lifted[i] = masked(value, i, CROWS, scal).astype(BF16).astype(F32)
+            lifted[i] = masked(value, i, CROWS, scal)
     weights = whole(wup)
     parts = {}
     total = jnp.zeros((128, HALF), F32)
@@ -1292,8 +1294,8 @@
         scratch=[((packed_rows, 128), F32)],
     )
     vector = jnp.broadcast_to(embedded[None, :], (16, embedded.shape[0]))
-    stat = shape(bands, 4, 128)
-    total = Saved(shape(1, 4, 128))
+    stat = shape(bands, 2, 128)
+    total = Saved(shape(1, 2, 128))
     act_a, stats_a, kept_in, line_a, line_b = run(
         "stage_a",
         stage_a,
@@ -1369,10 +1371,10 @@
         "stage_out",
         functools.partial(stage_out, members),
         [
-            Saved(shape(96, 512)), rows_of(0, 8, BF16), edge, edge, stat,
+            Saved(shape(96, 512)), rows_of(0, 8, BF16), edge, edge, shape(bands, 4, 128),
             Saved(rows_of(-3, 14, BF16)),
             Field(shape(10, 32, HALF, dtype=BF16), -1),
-            Saved(flat_rows(0, 8, 256), when=None), shape(1, 4, 128),
+            Saved(flat_rows(0, 8, 256), when=None), shape(1, 2, 128),
         ],
         None,
         stats_d, Saved(wout, when=1), merged, Saved(line_a, when=1), Saved(line_b, when=1),
@@ -1399,7 +1401,7 @@
         functools.partial(stage_up, members, members_c),
         [
             rows_of(-2, 12, BF16), rows_of(0, 4, BF16), rows_of(-1, 6, BF16), edge, edge, stat,
-            shape(8, 128), shape(1, 4, 128),
+            shape(8, 128), shape(1, 2, 128),
         ],
         None,
         total_d, stats_ed, got_a, got_b, Saved(hats_d, when=1), back_d, Saved(wup_t, when=1),
@@ -1427,7 +1429,7 @@
         functools.partial(stage_down, members, members_c),
         [
             rows_of(-1, 10, BF16), rows_of(-1, 10, BF16), stat, Saved(rows_of(-1, 6, BF16)),
-            shape(1, 4, 128),
+            shape(1, 2, 128),
         ],
         None,
         total_c, stats_ec, got_a, got_b, Saved(hats_c, when=1), back_c, grad_coarse,
@@ -1448,7 +1450,7 @@
         functools.partial(stage_first, members),
         [
             rows_of(0, 8, BF16), stat, rows_of(-1, 10, BF16), shape(8, 128),
-            shape(1, 4, 128),
+            shape(1, 2, 128),
         ],
         None,
         total_b, stats_eb, Saved(hats_b, when=1), back_b, Saved(wfirst_t, when=1), Saved(total_a, when=1),

time: 178 us -> 175 us (0.983)
  no operation moved by 1% of the time
where the time goes in v5:
time: 175 us; the launch traced here: 174 us
  blocking collectives  63.5 us (36%)
  Pallas kernels  56.9 us (33%)
  starting transfers between devices  30 us (17%)
  waiting for transfers between devices  21.7 us (12%)
  between operations  1.94 us (1%)
    pallas_call x19, Pallas kernels, run(): pl.pallas_call(body, out_shape=tuple(out_shapes), in_specs=in_specs, out_...  56.9 us
    all_to_all x3, blocking collectives, sum_parts(): return lax.all_to_all(stats, 'rows', 0, 0)  34.7 us
    all_to_all x5, starting transfers between devices, sum_parts(): return lax.all_to_all(stats, 'rows', 0, 0)  20 us
    all_to_all x1, blocking collectives, per_device(): got = lax.all_to_all(both, ('fsdp', 'rows'), 0, 0, axis_index_groups=cores)  17.6 us
    all_to_all x5, waiting for transfers between devices, sum_parts(): return lax.all_to_all(stats, 'rows', 0, 0)  15.4 us
    all_to_all x1, blocking collectives, per_device(): mine = lax.all_to_all(mine, 'rows', 0, 0, axis_index_groups=cores)  11.1 us
    ppermute x2, starting transfers between devices, gather_packed(): return [packed, lax.ppermute(packed, 'fsdp', [(0, 1), (1, 0)])]  4.07 us
  transfers between devices with their start and end apart: 18, of which 10 were waited for; matrix products, arithmetic and copies ran while one was open for 0% of the time, Pallas kernels for 11%

profile of v5, /device:TPU:0, one launch (start us, length us, event | category | flops | bytes accessed | tf_op | source)
XLA Modules:
  0.0 174.3 jit_solution(843395195963765683)
XLA Ops:
  1.5 3.0 %enter.1 = (bf16[320,128]{1,0:T(8,128)(2,1)S(1)}, bf16[32,4096]{1,0:T(8,128)(2,1)S(1)}, bf16[32,3584]{1,0:T(8,128)(2,1)S(1)}, bf16[32,3584]{1,0:T(8,128)(2,1)S(1)}, f32[8,128]{1,0:T(8,128)}) custom-call(f32[6]{0:T(128)S(1)} %stack.24.refs_0_, f32[96,512]{1,0:T(8,128)} %bitcast.13, f32[96,512]{1,0:T(8,128)} %bitcast.17, f32[96,512]{1,0:T(8,128)} %bitcast.15, ...), custom_call_target="tpu_custom_call" | custom-call | tf_op jit(solution)/shard_map/enter/pallas_call | solution.py:1183
  5.7 2.6 %collective-permute-start.2 = (bf16[320,128]{1,0:T(8,128)(2,1)S(1)}, bf16[320,128]{1,0:T(8,128)(2,1)S(1)}, u32[]{:S(2)}, u32[]{:S(2)}) collective-permute-start(bf16[320,128]{1,0:T(8,128)(2,1)S(1)} %get-tuple-element.94.refs_4_.refs_3_), channel_id=1, source_target_pairs={{0,16},{16,0},{1,17},{17,1},{2,18},{18,2},{3,19},{19,3},{4,20},{20... | collective-permute-start | bytes 245768 | tf_op jit(solution)/shard_map/ppermute | solution.py:1216
  10.7 2.4 %stage_a.1 = (f32[20,128,256]{2,1,0:T(8,128)S(1)}, f32[16,2,128]{2,1,0:T(2,128)S(1)}, bf16[128,2560]{1,0:T(8,128)(2,1)}, f32[16,512]{1,0:T(8,128)}, f32[16,512]{1,0:T(8,128)}) custom-call(bf16[32,3584]{1,0:T(8,128)(2,1)S(1)} %collective-permute-done.refs_0_, bf16[32,3584]{1,0:T(8,128)(2,1)S(1)} %collective-permute-done.1.refs_1_, ...), custom_call_target="tpu_custom_call" | custom-call | tf_op jit(solution)/shard_map/stage_a/pallas_call | solution.py:1183
  13.2 16.5 %all_to_all.50.refs_0_ = f32[16,2,128]{2,1,0:T(2,128)S(1)} all-to-all(f32[16,2,128]{2,1,0:T(2,128)S(1)} %get-tuple-element.95), channel_id=1, replica_groups=mesh['fsdp'=2,'rows'=16] {'rows'}, dimensions={0} | all-to-all | bytes 32768 | tf_op jit(solution)/shard_map/all_to_all | solution.py:1202
  31.3 3.8 %stage_b.1 = (f32[18,128,256]{2,1,0:T(8,128)S(1)}, f32[16,2,128]{2,1,0:T(2,128)}, bf16[256,2048]{1,0:T(8,128)(2,1)}, bf16[8,128,256]{2,1,0:T(8,128)(2,1)}, f32[1...) custom-call(f32[16,2,128]{2,1,0:T(2,128)S(1)} %all_to_all.50.refs_0_, ...), custom_call_target="tpu_custom_call" | custom-call | tf_op jit(solution)/shard_map/stage_b/pallas_call | solution.py:1183
  35.1 3.5 %all-to-all-start.1 = ((f32[16,2,128]{2,1,0:T(2,128)}), f32[16,2,128]{2,1,0:T(2,128)S(1)}, u32[]{:S(2)}, u32[]{:S(2)}) async-start(f32[16,2,128]{2,1,0:T(2,128)} %get-tuple-element.98), calls=%async_computation.1 | async-start | bytes 32768 | tf_op jit(solution)/shard_map/all_to_all | solution.py:1202
  40.2 2.7 %prepare_rest.1 = (bf16[384,256]{1,0:T(8,128)(2,1)}, bf16[256,384]{1,0:T(8,128)(2,1)}, bf16[384,192]{1,0:T(8,128)(2,1)}, bf16[192,384]{1,0:T(8,128)(2,1)}, bf16[...) custom-call(bf16[1488,128]{1,0:T(8,128)(2,1)S(1)} %pack_rest.1.refs_, ...), custom_call_target="tpu_custom_call" | custom-call | tf_op jit(solution)/shard_map/prepare_rest/pallas_call | solution.py:1183
  42.9 2.3 %all-to-all-done.1.refs_0_ = f32[16,2,128]{2,1,0:T(2,128)S(1)} async-done(((f32[16,2,128]{2,1,0:T(2,128)}), f32[16,2,128]{2,1,0:T(2,128)S(1)}, u32[]{:S(2)}, u32[]{:S(2)}) %all-to-all-start.1) | async-done | bytes 16416 | tf_op jit(solution)/shard_map/all_to_all | solution.py:1202
  45.1 4.9 %stage_c.1 = (f32[14,128,256]{2,1,0:T(8,128)S(1)}, f32[6,128,256]{2,1,0:T(8,128)S(1)}, f32[128,512]{1,0:T(8,128)S(1)}, f32[16,2,128]{2,1,0:T(2,128)S(1)}, bf16[2...) custom-call(f32[16,2,128]{2,1,0:T(2,128)S(1)} %all-to-all-done.1.refs_0_,, ...), custom_call_target="tpu_custom_call" | custom-call | tf_op jit(solution)/shard_map/stage_c/pallas_call | solution.py:1183
  50.8 1.9 %collective-permute-start.4 = (f32[128,512]{1,0:T(8,128)S(1)}, f32[128,512]{1,0:T(8,128)S(1)}, u32[]{:S(2)}, u32[]{:S(2)}) collective-permute-start(f32[128,512]{1,0:T(8,128)S(1)} %get-tuple-element.106), channel_id=1, source_target_pairs={{0,1},{1,0},{2,3},{3,2},{4,5},{5,4},{6,7},{7,6},{8,9},{9,8},{10,11... | collective-permute-start | bytes 786440 | tf_op jit(solution)/shard_map/ppermute | solution.py:1211
  52.6 9.2 %all_to_all.51.refs_0_ = f32[16,2,128]{2,1,0:T(2,128)S(1)} all-to-all(f32[16,2,128]{2,1,0:T(2,128)S(1)} %get-tuple-element.104), channel_id=1, replica_groups=mesh['fsdp'=2,'rows'=16] {'rows'}, dimensions={0} | all-to-all | bytes 32768 | tf_op jit(solution)/shard_map/all_to_all | solution.py:1202
  61.8 4.6 %stage_d.1 = (f32[14,128,256]{2,1,0:T(8,128)S(1)}, bf16[8,128,256]{2,1,0:T(8,128)(2,1)}, f32[16,2,128]{2,1,0:T(2,128)S(1)}, bf16[384,1024]{1,0:T(8,128)(2,1)}, b...) custom-call(f32[16,2,128]{2,1,0:T(2,128)S(1)} %all_to_all.51.refs_0_, bf16[384,384]{1,0:T(8,128)(2,1)} %get-tuple-element.105.refs_1_, ...), custom_call_target="tpu_custom_call" | custom-call | tf_op jit(solution)/shard_map/stage_d/pallas_call | solution.py:1183
  66.4 9.1 %all_to_all.52.refs_0_ = f32[16,2,128]{2,1,0:T(2,128)S(1)} all-to-all(f32[16,2,128]{2,1,0:T(2,128)S(1)} %get-tuple-element.110), channel_id=1, replica_groups=mesh['fsdp'=2,'rows'=16] {'rows'}, dimensions={0} | all-to-all | bytes 32768 | tf_op jit(solution)/shard_map/all_to_all | solution.py:1202
  75.4 5.7 %stage_out.1 = (f32[96,512]{1,0:T(8,128)}, bf16[8,128,256]{2,1,0:T(8,128)(2,1)S(1)}, bf16[128,768]{1,0:T(8,128)(2,1)S(1)}, bf16[128,768]{1,0:T(8,128)(2,1)S(1)},...) custom-call(f32[16,2,128]{2,1,0:T(2,128)S(1)} %all_to_all.52.refs_0_, ...), custom_call_target="tpu_custom_call" | custom-call | tf_op jit(solution)/shard_map/stage_out/pallas_call | solution.py:1183
  81.9 4.7 %all-to-all-start.4 = ((f32[16,4,128]{2,1,0:T(4,128)}), f32[16,4,128]{2,1,0:T(4,128)S(1)}, u32[]{:S(2)}, u32[]{:S(2)}) async-start(f32[16,4,128]{2,1,0:T(4,128)} %get-tuple-element.119), calls=%async_computation.4 | async-start | bytes 65536 | tf_op jit(solution)/shard_map/all_to_all | solution.py:1202
  86.6 2.4 %grads_out.1.refs_10_.refs_4_ = bf16[2,80,128]{2,1,0:T(8,128)(2,1)} custom-call(bf16[10,32,256]{2,1,0:T(8,128)(2,1)S(1)} %get-tuple-element.128.refs_0_, bf16[256,2048]{1,0:T(8,128)(2,1)} %get-tuple-element.129.refs_1_), custom_call_target="tpu_custom_call" | custom-call | tf_op jit(solution)/shard_map/grads_out/pallas_call | solution.py:1183
  89.1 4.2 %all-to-all-done.4.refs_1_ = f32[16,4,128]{2,1,0:T(4,128)S(1)} async-done(((f32[16,4,128]{2,1,0:T(4,128)}), f32[16,4,128]{2,1,0:T(4,128)S(1)}, u32[]{:S(2)}, u32[]{:S(2)}) %all-to-all-start.4) | async-done | bytes 32800 | tf_op jit(solution)/shard_map/all_to_all | solution.py:1202
  93.3 4.7 %stage_up.1 = (bf16[12,128,256]{2,1,0:T(8,128)(2,1)S(1)}, bf16[4,128,256]{2,1,0:T(8,128)(2,1)S(1)}, bf16[6,128,256]{2,1,0:T(8,128)(2,1)S(1)}, bf16[128,768]{1,0:...) custom-call(f32[1,2,128]{2,1,0:T(2,128)S(1)} %get-tuple-element.118., ...), custom_call_target="tpu_custom_call" | custom-call | tf_op jit(solution)/shard_map/stage_up/pallas_call | solution.py:1183
  98.7 4.8 %all-to-all-start.5 = ((f32[16,2,128]{2,1,0:T(2,128)}), f32[16,2,128]{2,1,0:T(2,128)S(1)}, u32[]{:S(2)}, u32[]{:S(2)}) async-start(f32[16,2,128]{2,1,0:T(2,128)} %get-tuple-element.131), calls=%async_computation.5 | async-start | bytes 32768 | tf_op jit(solution)/shard_map/all_to_all | solution.py:1202
  103.4 3.6 %grads_up.1.refs_12_.refs_6_ = bf16[2,944,128]{2,1,0:T(8,128)(2,1)} custom-call(bf16[12,128,256]{2,1,0:T(8,128)(2,1)S(1)} %get-tuple-element.137.refs_0_.refs_8_, bf16[6,128,256]{2,1,0:T(8,128)(2,1)S(1)} %get-tuple-element.135.refs_1_.refs_6_, bf16[384,1024]{1,0:T(8,128)(2,1)} %get-tuple-element.141.refs_2_, bf16[384,1024]{1,0:T(8,128)(2,1)} %get-tuple-element.142.refs_3_, ...), custom_call_target="tpu_custom_call" | custom-call | tf_op jit(solution)/shard_map/grads_up/pallas_call | solution.py:1183
  107.1 2.9 %all-to-all-done.5.refs_1_ = f32[16,2,128]{2,1,0:T(2,128)S(1)} async-done(((f32[16,2,128]{2,1,0:T(2,128)}), f32[16,2,128]{2,1,0:T(2,128)S(1)}, u32[]{:S(2)}, u32[]{:S(2)}) %all-to-all-start.5) | async-done | bytes 16416 | tf_op jit(solution)/shard_map/all_to_all | solution.py:1202
  109.9 4.1 %stage_down.1 = (bf16[10,128,256]{2,1,0:T(8,128)(2,1)S(1)}, bf16[10,128,256]{2,1,0:T(8,128)(2,1)S(1)}, f32[16,2,128]{2,1,0:T(2,128)}, bf16[6,128,256]{2,1,0:T(8,128)(2,1)}, f32[1,2,128]{2,1,0:T(2,128)S(1)}) custom-call(f32[1,2,128]{2,1,0:T(2,128)S(1)} %get-tuple-element.130.refs_0_, f32[16,2,128]{2,1,0:T(2,128)S(1)} %all-to-all-done.5.refs_1_, ...), custom_call_target="tpu_custom_call" | custom-call | tf_op jit(solution)/shard_map/stage_down/pallas_call | solution.py:1183
  114.1 3.5 %all-to-all-start.6 = ((f32[16,2,128]{2,1,0:T(2,128)}), f32[16,2,128]{2,1,0:T(2,128)S(1)}, u32[]{:S(2)}, u32[]{:S(2)}) async-start(f32[16,2,128]{2,1,0:T(2,128)} %get-tuple-element.144), calls=%async_computation.6 | async-start | bytes 32768 | tf_op jit(solution)/shard_map/all_to_all | solution.py:1202
  117.6 3.1 %grads_down.1.refs_7_ = bf16[2,480,128]{2,1,0:T(8,128)(2,1)} custom-call(bf16[10,128,256]{2,1,0:T(8,128)(2,1)S(1)} %get-tuple-element.149.refs_0_.refs_4_, bf16[6,128,256]{2,1,0:T(8,128)(2,1)} %get-tuple-element.150.refs_1_, bf16[192,1024]{1,0:T(8,128)(2,1)} %get-tuple-element.151.refs_2_, bf16[256,2048]{1,0:T(8,128)(2,1)} %get-tuple-element.152.refs_3_), custom_call_target="tpu_custom_call" | custom-call | tf_op jit(solution)/shard_map/grads_down/pallas_call | solution.py:1183
  120.7 3.4 %all-to-all-done.6.refs_1_ = f32[16,2,128]{2,1,0:T(2,128)S(1)} async-done(((f32[16,2,128]{2,1,0:T(2,128)}), f32[16,2,128]{2,1,0:T(2,128)S(1)}, u32[]{:S(2)}, u32[]{:S(2)}) %all-to-all-start.6) | async-done | bytes 16416 | tf_op jit(solution)/shard_map/all_to_all | solution.py:1202
  124.0 3.5 %stage_first.1 = (bf16[8,128,256]{2,1,0:T(8,128)(2,1)S(1)}, f32[16,2,128]{2,1,0:T(2,128)}, bf16[10,128,256]{2,1,0:T(8,128)(2,1)S(1)}, f32[8,128]{1,0:T(8,128)S(1)}, f32[1,2,128]{2,1,0:T(2,128)S(1)}) custom-call(f32[1,2,128]{2,1,0:T(2,128)S(1)} %get-tuple-element.143.refs_0_, f32[16,2,128]{2,1,0:T(2,128)S(1)} %all-to-all-done.6.refs_1_, ...), custom_call_target="tpu_custom_call" | custom-call | tf_op jit(solution)/shard_map/stage_first/pallas_call | solution.py:1183
  127.5 3.5 %all-to-all-start.7 = ((f32[16,2,128]{2,1,0:T(2,128)}), f32[16,2,128]{2,1,0:T(2,128)S(1)}, u32[]{:S(2)}, u32[]{:S(2)}) async-start(f32[16,2,128]{2,1,0:T(2,128)} %get-tuple-element.154), calls=%async_computation.7 | async-start | bytes 32768 | tf_op jit(solution)/shard_map/all_to_all | solution.py:1202
  131.6 2.6 %grads_first.1.refs_8_ = bf16[2,224,128]{2,1,0:T(8,128)(2,1)} custom-call(bf16[10,128,256]{2,1,0:T(8,128)(2,1)S(1)} %get-tuple-element.157.refs_0_, f32[8,128]{1,0:T(8,128)S(1)} %get-tuple-element.158.refs_1_, bf16[16,128]{1,0:T(8,128)(2,1)S(1)} %broadcast_in_dim.2.refs_2_, bf16[256,2048]{1,0:T(8,128)(2,1)} %get-tuple-element.159.refs_3_), custom_call_target="tpu_custom_call" | custom-call | tf_op jit(solution)/shard_map/grads_first/pallas_call | solution.py:1183
  134.7 2.8 %all-to-all-done.7.refs_1_ = f32[16,2,128]{2,1,0:T(2,128)S(1)} async-done(((f32[16,2,128]{2,1,0:T(2,128)}), f32[16,2,128]{2,1,0:T(2,128)S(1)}, u32[]{:S(2)}, u32[]{:S(2)}) %all-to-all-start.7) | async-done | bytes 16416 | tf_op jit(solution)/shard_map/all_to_all | solution.py:1202
  137.5 3.1 %stage_last.1 = (bf16[2,896,128]{2,1,0:T(8,128)(2,1)S(1)}, bf16[2,896,128]{2,1,0:T(8,128)(2,1)S(1)}, f32[1,1]{1,0:T(1,128)}) custom-call(f32[1,2,128]{2,1,0:T(2,128)S(1)} %get-tuple-element.153.refs_0_, f32[16,2,128]{2,1,0:T(2,128)S(1)} %all-to-all-done.7.refs_1_, bf16[8,128,256]{2,1,0:T(8,128)(2,1)} %get-tuple-element.148.refs_6_.refs_2_, ...), custom_call_target="tpu_custom_call" | custom-call | tf_op jit(solution)/shard_map/stage_last/pallas_call | solution.py:1183
  142.6 17.6 %all_to_all.53.refs_0_ = bf16[16,112,128]{2,1,0:T(8,128)(2,1)S(1)} all-to-all(bf16[16,112,128]{2,1,0:T(8,128)(2,1)S(1)} %bitcast.10), channel_id=1, replica_groups={{0,2,4,6,8,10,12,14,16,18,20,22,24,26,28,30},{1,3,5,7,9,11,13,15,17,19,..., dimensions={0} | all-to-all | bytes 917504 | tf_op jit(solution)/shard_map/all_to_all | solution.py:1492
  160.3 11.1 %all_to_all.54 = bf16[8,112,128]{2,1,0:T(8,128)(2,1)S(1)} all-to-all(bf16[8,112,128]{2,1,0:T(8,128)(2,1)S(1)} %add_up.1), channel_id=1, replica_groups={{0,2,4,6,8,10,12,14},{1,3,5,7,9,11,13,15},{16,18,20,22,24,26,28,30},{17..., dimensions={0} | all-to-all | bytes 458752 | tf_op jit(solution)/shard_map/all_to_all | solution.py:1495
  (32 shorter events, 14.8 us)
Async XLA Ops:
  4.5 6.2 %collective-permute-start = (bf16[32,3584]{1,0:T(8,128)(2,1)S(1)}, bf16[32,3584]{1,0:T(8,128)(2,1)S(1)}, u32[]{:S(2)}, u32[]{:S(2)}) collective-permute-start(bf16[32,3584]{1,0:T(8,128)(2,1)S(1)} %get-tuple-element.92), channel_id=1, source_target_pairs={{0,1},{1,0},{2,3},{3,2},{4,5},{5,4},{6,7},{7,6},{8,9},{9,8},{10,11... | collective-permute-start | bytes 688136 | tf_op jit(solution)/shard_map/ppermute | solution.py:1211
  5.0 5.7 %collective-permute-start.1 = (bf16[32,3584]{1,0:T(8,128)(2,1)S(1)}, bf16[32,3584]{1,0:T(8,128)(2,1)S(1)}, u32[]{:S(2)}, u32[]{:S(2)}) collective-permute-start(bf16[32,3584]{1,0:T(8,128)(2,1)S(1)} %get-tuple-element.93), channel_id=1, source_target_pairs={{1,2},{2,1},{3,4},{4,3},{5,6},{6,5},{7,8},{8,7},{9,10},{10,9},{11,... | collective-permute-start | bytes 688136 | tf_op jit(solution)/shard_map/ppermute | solution.py:1211
  5.7 5.0 %collective-permute-start.2 = (bf16[320,128]{1,0:T(8,128)(2,1)S(1)}, bf16[320,128]{1,0:T(8,128)(2,1)S(1)}, u32[]{:S(2)}, u32[]{:S(2)}) collective-permute-start(bf16[320,128]{1,0:T(8,128)(2,1)S(1)} %get-tuple-element.94.refs_4_.refs_3_), channel_id=1, source_target_pairs={{0,16},{16,0},{1,17},{17,1},{2,18},{18,2},{3,19},{19,3},{4,20},{20... | collective-permute-start | bytes 245768 | tf_op jit(solution)/shard_map/ppermute | solution.py:1216
  29.7 10.5 %collective-permute-start.3 = (bf16[1488,128]{1,0:T(8,128)(2,1)S(1)}, bf16[1488,128]{1,0:T(8,128)(2,1)S(1)}, u32[]{:S(2)}, u32[]{:S(2)}) collective-permute-start(bf16[1488,128]{1,0:T(8,128)(2,1)S(1)} %pack_rest.1.refs_3_.refs_0_), channel_id=1, source_target_pairs={{0,16},{16,0},{1,17},{17,1},{2,18},{18,2},{3,19},{19,3},{4,20},{20... | collective-permute-start | bytes 1142792 | tf_op jit(solution)/shard_map/ppermute | solution.py:1216
  35.1 10.0 %all-to-all-start.1 = ((f32[16,2,128]{2,1,0:T(2,128)}), f32[16,2,128]{2,1,0:T(2,128)S(1)}, u32[]{:S(2)}, u32[]{:S(2)}) async-start(f32[16,2,128]{2,1,0:T(2,128)} %get-tuple-element.98), calls=%async_computation.1 | async-start | bytes 32768 | tf_op jit(solution)/shard_map/all_to_all | solution.py:1202
  50.1 11.7 %collective-permute-start.5 = (f32[128,512]{1,0:T(8,128)S(1)}, f32[128,512]{1,0:T(8,128)S(1)}, u32[]{:S(2)}, u32[]{:S(2)}) collective-permute-start(f32[128,512]{1,0:T(8,128)S(1)} %get-tuple-element.106), channel_id=1, source_target_pairs={{1,2},{2,1},{3,4},{4,3},{5,6},{6,5},{7,8},{8,7},{9,10},{10,9},{11,... | collective-permute-start | bytes 786440 | tf_op jit(solution)/shard_map/ppermute | solution.py:1211
  50.8 11.0 %collective-permute-start.4 = (f32[128,512]{1,0:T(8,128)S(1)}, f32[128,512]{1,0:T(8,128)S(1)}, u32[]{:S(2)}, u32[]{:S(2)}) collective-permute-start(f32[128,512]{1,0:T(8,128)S(1)} %get-tuple-element.106), channel_id=1, source_target_pairs={{0,1},{1,0},{2,3},{3,2},{4,5},{5,4},{6,7},{7,6},{8,9},{9,8},{10,11... | collective-permute-start | bytes 786440 | tf_op jit(solution)/shard_map/ppermute | solution.py:1211
  81.1 12.1 %collective-permute-start.6 = (bf16[128,768]{1,0:T(8,128)(2,1)S(1)}, bf16[128,768]{1,0:T(8,128)(2,1)S(1)}, u32[]{:S(2)}, u32[]{:S(2)}) collective-permute-start(bf16[128,768]{1,0:T(8,128)(2,1)S(1)} %get-tuple-element.120), channel_id=1, source_target_pairs={{0,1},{1,0},{2,3},{3,2},{4,5},{5,4},{6,7},{7,6},{8,9},{9,8},{10,11... | collective-permute-start | bytes 589832 | tf_op jit(solution)/shard_map/ppermute | solution.py:1211
  81.2 12.1 %collective-permute-start.7 = (bf16[128,768]{1,0:T(8,128)(2,1)S(1)}, bf16[128,768]{1,0:T(8,128)(2,1)S(1)}, u32[]{:S(2)}, u32[]{:S(2)}) collective-permute-start(bf16[128,768]{1,0:T(8,128)(2,1)S(1)} %get-tuple-element.121), channel_id=1, source_target_pairs={{1,2},{2,1},{3,4},{4,3},{5,6},{6,5},{7,8},{8,7},{9,10},{10,9},{11,... | collective-permute-start | bytes 589832 | tf_op jit(solution)/shard_map/ppermute | solution.py:1211
  81.9 11.4 %all-to-all-start.4 = ((f32[16,4,128]{2,1,0:T(4,128)}), f32[16,4,128]{2,1,0:T(4,128)S(1)}, u32[]{:S(2)}, u32[]{:S(2)}) async-start(f32[16,4,128]{2,1,0:T(4,128)} %get-tuple-element.119), calls=%async_computation.4 | async-start | bytes 65536 | tf_op jit(solution)/shard_map/all_to_all | solution.py:1202
  97.9 12.0 %collective-permute-start.8 = (bf16[128,768]{1,0:T(8,128)(2,1)S(1)}, bf16[128,768]{1,0:T(8,128)(2,1)S(1)}, u32[]{:S(2)}, u32[]{:S(2)}) collective-permute-start(bf16[128,768]{1,0:T(8,128)(2,1)S(1)} %get-tuple-element.132), channel_id=1, source_target_pairs={{0,1},{1,0},{2,3},{3,2},{4,5},{5,4},{6,7},{7,6},{8,9},{9,8},{10,11... | collective-permute-start | bytes 589832 | tf_op jit(solution)/shard_map/ppermute | solution.py:1211
  98.0 11.9 %collective-permute-start.9 = (bf16[128,768]{1,0:T(8,128)(2,1)S(1)}, bf16[128,768]{1,0:T(8,128)(2,1)S(1)}, u32[]{:S(2)}, u32[]{:S(2)}) collective-permute-start(bf16[128,768]{1,0:T(8,128)(2,1)S(1)} %get-tuple-element.133), channel_id=1, source_target_pairs={{1,2},{2,1},{3,4},{4,3},{5,6},{6,5},{7,8},{8,7},{9,10},{10,9},{11,... | collective-permute-start | bytes 589832 | tf_op jit(solution)/shard_map/ppermute | solution.py:1211
  98.7 11.2 %all-to-all-start.5 = ((f32[16,2,128]{2,1,0:T(2,128)}), f32[16,2,128]{2,1,0:T(2,128)S(1)}, u32[]{:S(2)}, u32[]{:S(2)}) async-start(f32[16,2,128]{2,1,0:T(2,128)} %get-tuple-element.131), calls=%async_computation.5 | async-start | bytes 32768 | tf_op jit(solution)/shard_map/all_to_all | solution.py:1202
  114.1 10.0 %all-to-all-start.6 = ((f32[16,2,128]{2,1,0:T(2,128)}), f32[16,2,128]{2,1,0:T(2,128)S(1)}, u32[]{:S(2)}, u32[]{:S(2)}) async-start(f32[16,2,128]{2,1,0:T(2,128)} %get-tuple-element.144), calls=%async_computation.6 | async-start | bytes 32768 | tf_op jit(solution)/shard_map/all_to_all | solution.py:1202
  127.5 10.0 %all-to-all-start.7 = ((f32[16,2,128]{2,1,0:T(2,128)}), f32[16,2,128]{2,1,0:T(2,128)S(1)}, u32[]{:S(2)}, u32[]{:S(2)}) async-start(f32[16,2,128]{2,1,0:T(2,128)} %get-tuple-element.154), calls=%async_computation.7 | async-start | bytes 32768 | tf_op jit(solution)/shard_map/all_to_all | solution.py:1202
  131.0 3.7 %collective-permute-start.10 = (f32[8,128]{1,0:T(8,128)S(1)}, f32[8,128]{1,0:T(8,128)S(1)}, u32[]{:S(2)}, u32[]{:S(2)}) collective-permute-start(f32[8,128]{1,0:T(8,128)S(1)} %get-tuple-element.160.refs_9_), channel_id=1, source_target_pairs={{0,16},{16,0},{1,17},{17,1},{2,18},{18,2},{3,19},{19,3},{4,20},{20... | collective-permute-start | bytes 12296 | tf_op jit(solution)/shard_map/ppermute | solution.py:1424
  140.6 1.9 %collective-permute-start.11 = (bf16[2,896,128]{2,1,0:T(8,128)(2,1)S(1)}, bf16[2,896,128]{2,1,0:T(8,128)(2,1)S(1)}, u32[]{:S(2)}, u32[]{:S(2)}) collective-permute-start(bf16[2,896,128]{2,1,0:T(8,128)(2,1)S(1)} %get-tuple-element.163), channel_id=1, source_target_pairs={{0,1},{1,0},{2,3},{3,2},{4,5},{5,4},{6,7},{7,6},{8,9},{9,8},{10,11... | collective-permute-start | bytes 1376264 | tf_op jit(solution)/shard_map/ppermute | solution.py:1488
  171.4 1.5 collective-permute-start.12

commit v6 on v5

--- a/solution.py
+++ b/solution.py
@@ -721,7 +721,7 @@
         mismatch = estimate - goal
         loss_sum = loss_sum + weight * mismatch * mismatch
         cells[16 * (i + 1) : 16 * (i + 2), :] = jnp.concatenate([coef * mismatch, blank], axis=0)
-    give(denoised, jnp.concatenate([found[t] for t in range(4)], axis=1))
+    give(denoised, jnp.concatenate([found[t, :96, :] for t in range(4)], axis=1))
     loss_sum = jnp.broadcast_to(
         jnp.sum(jnp.sum(loss_sum, axis=1, keepdims=True), axis=0, keepdims=True), (1, 128)
     )
@@ -1382,7 +1382,7 @@
         Saved(figures, when=1),
         scratch=[
             ((160, 512), F32), ((160, 512), F32),
-            ((4, 96, 128), F32), ((4, 96, 128), F32), ((4, 96, 128), F32),
+            ((4, 128, 128), F32), ((4, 128, 128), F32), ((4, 128, 128), F32),
             ((256, 12 * HALF), BF16), pltpu.SemaphoreType.DMA((1,)),
         ],
     )

time: 175 us -> 175 us (level)
  no operation moved by 1% of the time
where the time goes in v6:
time: 175 us; the launch traced here: 174 us
  blocking collectives  63.5 us (36%)
  Pallas kernels  56.9 us (33%)
  starting transfers between devices  30 us (17%)
  waiting for transfers between devices  21.7 us (12%)
  between operations  1.94 us (1%)
    pallas_call x19, Pallas kernels, run(): pl.pallas_call(body, out_shape=tuple(out_shapes), in_specs=in_specs, out_...  56.9 us
    all_to_all x3, blocking collectives, sum_parts(): return lax.all_to_all(stats, 'rows', 0, 0)  34.7 us
    all_to_all x5, starting transfers between devices, sum_parts(): return lax.all_to_all(stats, 'rows', 0, 0)  20 us
    all_to_all x1, blocking collectives, per_device(): got = lax.all_to_all(both, ('fsdp', 'rows'), 0, 0, axis_index_groups=cores)  17.6 us
    all_to_all x5, waiting for transfers between devices, sum_parts(): return lax.all_to_all(stats, 'rows', 0, 0)  15.4 us
    all_to_all x1, blocking collectives, per_device(): mine = lax.all_to_all(mine, 'rows', 0, 0, axis_index_groups=cores)  11.1 us
    ppermute x2, starting transfers between devices, gather_packed(): return [packed, lax.ppermute(packed, 'fsdp', [(0, 1), (1, 0)])]  4.07 us
  transfers between devices with their start and end apart: 18, of which 10 were waited for; matrix products, arithmetic and copies ran while one was open for 0% of the time, Pallas kernels for 11%

profile of v6, /device:TPU:0, one launch (start us, length us, event | category | flops | bytes accessed | tf_op | source)
XLA Modules:
  0.0 174.3 jit_solution(2666202921726229857)
XLA Ops:
  1.5 3.0 %enter.1 = (bf16[320,128]{1,0:T(8,128)(2,1)S(1)}, bf16[32,4096]{1,0:T(8,128)(2,1)S(1)}, bf16[32,3584]{1,0:T(8,128)(2,1)S(1)}, bf16[32,3584]{1,0:T(8,128)(2,1)S(1)}, f32[8,128]{1,0:T(8,128)}) custom-call(f32[6]{0:T(128)S(1)} %stack.24.refs_0_, f32[96,512]{1,0:T(8,128)} %bitcast.13, f32[96,512]{1,0:T(8,128)} %bitcast.17, f32[96,512]{1,0:T(8,128)} %bitcast.15, ...), custom_call_target="tpu_custom_call" | custom-call | tf_op jit(solution)/shard_map/enter/pallas_call | solution.py:1183
  5.7 2.6 %collective-permute-start.2 = (bf16[320,128]{1,0:T(8,128)(2,1)S(1)}, bf16[320,128]{1,0:T(8,128)(2,1)S(1)}, u32[]{:S(2)}, u32[]{:S(2)}) collective-permute-start(bf16[320,128]{1,0:T(8,128)(2,1)S(1)} %get-tuple-element.94.refs_4_.refs_3_), channel_id=1, source_target_pairs={{0,16},{16,0},{1,17},{17,1},{2,18},{18,2},{3,19},{19,3},{4,20},{20... | collective-permute-start | bytes 245768 | tf_op jit(solution)/shard_map/ppermute | solution.py:1216
  10.7 2.4 %stage_a.1 = (f32[20,128,256]{2,1,0:T(8,128)S(1)}, f32[16,2,128]{2,1,0:T(2,128)S(1)}, bf16[128,2560]{1,0:T(8,128)(2,1)}, f32[16,512]{1,0:T(8,128)}, f32[16,512]{1,0:T(8,128)}) custom-call(bf16[32,3584]{1,0:T(8,128)(2,1)S(1)} %collective-permute-done.refs_0_, bf16[32,3584]{1,0:T(8,128)(2,1)S(1)} %collective-permute-done.1.refs_1_, ...), custom_call_target="tpu_custom_call" | custom-call | tf_op jit(solution)/shard_map/stage_a/pallas_call | solution.py:1183
  13.2 16.5 %all_to_all.50.refs_0_ = f32[16,2,128]{2,1,0:T(2,128)S(1)} all-to-all(f32[16,2,128]{2,1,0:T(2,128)S(1)} %get-tuple-element.95), channel_id=1, replica_groups=mesh['fsdp'=2,'rows'=16] {'rows'}, dimensions={0} | all-to-all | bytes 32768 | tf_op jit(solution)/shard_map/all_to_all | solution.py:1202
  31.3 3.8 %stage_b.1 = (f32[18,128,256]{2,1,0:T(8,128)S(1)}, f32[16,2,128]{2,1,0:T(2,128)}, bf16[256,2048]{1,0:T(8,128)(2,1)}, bf16[8,128,256]{2,1,0:T(8,128)(2,1)}, f32[1...) custom-call(f32[16,2,128]{2,1,0:T(2,128)S(1)} %all_to_all.50.refs_0_, ...), custom_call_target="tpu_custom_call" | custom-call | tf_op jit(solution)/shard_map/stage_b/pallas_call | solution.py:1183
  35.1 3.5 %all-to-all-start.1 = ((f32[16,2,128]{2,1,0:T(2,128)}), f32[16,2,128]{2,1,0:T(2,128)S(1)}, u32[]{:S(2)}, u32[]{:S(2)}) async-start(f32[16,2,128]{2,1,0:T(2,128)} %get-tuple-element.98), calls=%async_computation.1 | async-start | bytes 32768 | tf_op jit(solution)/shard_map/all_to_all | solution.py:1202
  40.2 2.7 %prepare_rest.1 = (bf16[384,256]{1,0:T(8,128)(2,1)}, bf16[256,384]{1,0:T(8,128)(2,1)}, bf16[384,192]{1,0:T(8,128)(2,1)}, bf16[192,384]{1,0:T(8,128)(2,1)}, bf16[...) custom-call(bf16[1488,128]{1,0:T(8,128)(2,1)S(1)} %pack_rest.1.refs_, ...), custom_call_target="tpu_custom_call" | custom-call | tf_op jit(solution)/shard_map/prepare_rest/pallas_call | solution.py:1183
  42.9 2.3 %all-to-all-done.1.refs_0_ = f32[16,2,128]{2,1,0:T(2,128)S(1)} async-done(((f32[16,2,128]{2,1,0:T(2,128)}), f32[16,2,128]{2,1,0:T(2,128)S(1)}, u32[]{:S(2)}, u32[]{:S(2)}) %all-to-all-start.1) | async-done | bytes 16416 | tf_op jit(solution)/shard_map/all_to_all | solution.py:1202
  45.1 4.9 %stage_c.1 = (f32[14,128,256]{2,1,0:T(8,128)S(1)}, f32[6,128,256]{2,1,0:T(8,128)S(1)}, f32[128,512]{1,0:T(8,128)S(1)}, f32[16,2,128]{2,1,0:T(2,128)S(1)}, bf16[2...) custom-call(f32[16,2,128]{2,1,0:T(2,128)S(1)} %all-to-all-done.1.refs_0_,, ...), custom_call_target="tpu_custom_call" | custom-call | tf_op jit(solution)/shard_map/stage_c/pallas_call | solution.py:1183
  50.8 1.9 %collective-permute-start.4 = (f32[128,512]{1,0:T(8,128)S(1)}, f32[128,512]{1,0:T(8,128)S(1)}, u32[]{:S(2)}, u32[]{:S(2)}) collective-permute-start(f32[128,512]{1,0:T(8,128)S(1)} %get-tuple-element.106), channel_id=1, source_target_pairs={{0,1},{1,0},{2,3},{3,2},{4,5},{5,4},{6,7},{7,6},{8,9},{9,8},{10,11... | collective-permute-start | bytes 786440 | tf_op jit(solution)/shard_map/ppermute | solution.py:1211
  52.6 9.2 %all_to_all.51.refs_0_ = f32[16,2,128]{2,1,0:T(2,128)S(1)} all-to-all(f32[16,2,128]{2,1,0:T(2,128)S(1)} %get-tuple-element.104), channel_id=1, replica_groups=mesh['fsdp'=2,'rows'=16] {'rows'}, dimensions={0} | all-to-all | bytes 32768 | tf_op jit(solution)/shard_map/all_to_all | solution.py:1202
  61.8 4.6 %stage_d.1 = (f32[14,128,256]{2,1,0:T(8,128)S(1)}, bf16[8,128,256]{2,1,0:T(8,128)(2,1)}, f32[16,2,128]{2,1,0:T(2,128)S(1)}, bf16[384,1024]{1,0:T(8,128)(2,1)}, b...) custom-call(f32[16,2,128]{2,1,0:T(2,128)S(1)} %all_to_all.51.refs_0_, bf16[384,384]{1,0:T(8,128)(2,1)} %get-tuple-element.105.refs_1_, ...), custom_call_target="tpu_custom_call" | custom-call | tf_op jit(solution)/shard_map/stage_d/pallas_call | solution.py:1183
  66.4 9.1 %all_to_all.52.refs_0_ = f32[16,2,128]{2,1,0:T(2,128)S(1)} all-to-all(f32[16,2,128]{2,1,0:T(2,128)S(1)} %get-tuple-element.110), channel_id=1, replica_groups=mesh['fsdp'=2,'rows'=16] {'rows'}, dimensions={0} | all-to-all | bytes 32768 | tf_op jit(solution)/shard_map/all_to_all | solution.py:1202
  75.4 5.7 %stage_out.1 = (f32[96,512]{1,0:T(8,128)}, bf16[8,128,256]{2,1,0:T(8,128)(2,1)S(1)}, bf16[128,768]{1,0:T(8,128)(2,1)S(1)}, bf16[128,768]{1,0:T(8,128)(2,1)S(1)},...) custom-call(f32[16,2,128]{2,1,0:T(2,128)S(1)} %all_to_all.52.refs_0_, ...), custom_call_target="tpu_custom_call" | custom-call | tf_op jit(solution)/shard_map/stage_out/pallas_call | solution.py:1183
  81.9 4.7 %all-to-all-start.4 = ((f32[16,4,128]{2,1,0:T(4,128)}), f32[16,4,128]{2,1,0:T(4,128)S(1)}, u32[]{:S(2)}, u32[]{:S(2)}) async-start(f32[16,4,128]{2,1,0:T(4,128)} %get-tuple-element.119), calls=%async_computation.4 | async-start | bytes 65536 | tf_op jit(solution)/shard_map/all_to_all | solution.py:1202
  86.6 2.4 %grads_out.1.refs_10_.refs_4_ = bf16[2,80,128]{2,1,0:T(8,128)(2,1)} custom-call(bf16[10,32,256]{2,1,0:T(8,128)(2,1)S(1)} %get-tuple-element.128.refs_0_, bf16[256,2048]{1,0:T(8,128)(2,1)} %get-tuple-element.129.refs_1_), custom_call_target="tpu_custom_call" | custom-call | tf_op jit(solution)/shard_map/grads_out/pallas_call | solution.py:1183
  89.1 4.2 %all-to-all-done.4.refs_1_ = f32[16,4,128]{2,1,0:T(4,128)S(1)} async-done(((f32[16,4,128]{2,1,0:T(4,128)}), f32[16,4,128]{2,1,0:T(4,128)S(1)}, u32[]{:S(2)}, u32[]{:S(2)}) %all-to-all-start.4) | async-done | bytes 32800 | tf_op jit(solution)/shard_map/all_to_all | solution.py:1202
  93.3 4.7 %stage_up.1 = (bf16[12,128,256]{2,1,0:T(8,128)(2,1)S(1)}, bf16[4,128,256]{2,1,0:T(8,128)(2,1)S(1)}, bf16[6,128,256]{2,1,0:T(8,128)(2,1)S(1)}, bf16[128,768]{1,0:...) custom-call(f32[1,2,128]{2,1,0:T(2,128)S(1)} %get-tuple-element.118., ...), custom_call_target="tpu_custom_call" | custom-call | tf_op jit(solution)/shard_map/stage_up/pallas_call | solution.py:1183
  98.7 4.8 %all-to-all-start.5 = ((f32[16,2,128]{2,1,0:T(2,128)}), f32[16,2,128]{2,1,0:T(2,128)S(1)}, u32[]{:S(2)}, u32[]{:S(2)}) async-start(f32[16,2,128]{2,1,0:T(2,128)} %get-tuple-element.131), calls=%async_computation.5 | async-start | bytes 32768 | tf_op jit(solution)/shard_map/all_to_all | solution.py:1202
  103.4 3.6 %grads_up.1.refs_12_.refs_6_ = bf16[2,944,128]{2,1,0:T(8,128)(2,1)} custom-call(bf16[12,128,256]{2,1,0:T(8,128)(2,1)S(1)} %get-tuple-element.137.refs_0_.refs_8_, bf16[6,128,256]{2,1,0:T(8,128)(2,1)S(1)} %get-tuple-element.135.refs_1_.refs_6_, bf16[384,1024]{1,0:T(8,128)(2,1)} %get-tuple-element.141.refs_2_, bf16[384,1024]{1,0:T(8,128)(2,1)} %get-tuple-element.142.refs_3_, ...), custom_call_target="tpu_custom_call" | custom-call | tf_op jit(solution)/shard_map/grads_up/pallas_call | solution.py:1183
  107.1 2.9 %all-to-all-done.5.refs_1_ = f32[16,2,128]{2,1,0:T(2,128)S(1)} async-done(((f32[16,2,128]{2,1,0:T(2,128)}), f32[16,2,128]{2,1,0:T(2,128)S(1)}, u32[]{:S(2)}, u32[]{:S(2)}) %all-to-all-start.5) | async-done | bytes 16416 | tf_op jit(solution)/shard_map/all_to_all | solution.py:1202
  109.9 4.1 %stage_down.1 = (bf16[10,128,256]{2,1,0:T(8,128)(2,1)S(1)}, bf16[10,128,256]{2,1,0:T(8,128)(2,1)S(1)}, f32[16,2,128]{2,1,0:T(2,128)}, bf16[6,128,256]{2,1,0:T(8,128)(2,1)}, f32[1,2,128]{2,1,0:T(2,128)S(1)}) custom-call(f32[1,2,128]{2,1,0:T(2,128)S(1)} %get-tuple-element.130.refs_0_, f32[16,2,128]{2,1,0:T(2,128)S(1)} %all-to-all-done.5.refs_1_, ...), custom_call_target="tpu_custom_call" | custom-call | tf_op jit(solution)/shard_map/stage_down/pallas_call | solution.py:1183
  114.1 3.5 %all-to-all-start.6 = ((f32[16,2,128]{2,1,0:T(2,128)}), f32[16,2,128]{2,1,0:T(2,128)S(1)}, u32[]{:S(2)}, u32[]{:S(2)}) async-start(f32[16,2,128]{2,1,0:T(2,128)} %get-tuple-element.144), calls=%async_computation.6 | async-start | bytes 32768 | tf_op jit(solution)/shard_map/all_to_all | solution.py:1202
  117.6 3.1 %grads_down.1.refs_7_ = bf16[2,480,128]{2,1,0:T(8,128)(2,1)} custom-call(bf16[10,128,256]{2,1,0:T(8,128)(2,1)S(1)} %get-tuple-element.149.refs_0_.refs_4_, bf16[6,128,256]{2,1,0:T(8,128)(2,1)} %get-tuple-element.150.refs_1_, bf16[192,1024]{1,0:T(8,128)(2,1)} %get-tuple-element.151.refs_2_, bf16[256,2048]{1,0:T(8,128)(2,1)} %get-tuple-element.152.refs_3_), custom_call_target="tpu_custom_call" | custom-call | tf_op jit(solution)/shard_map/grads_down/pallas_call | solution.py:1183
  120.7 3.4 %all-to-all-done.6.refs_1_ = f32[16,2,128]{2,1,0:T(2,128)S(1)} async-done(((f32[16,2,128]{2,1,0:T(2,128)}), f32[16,2,128]{2,1,0:T(2,128)S(1)}, u32[]{:S(2)}, u32[]{:S(2)}) %all-to-all-start.6) | async-done | bytes 16416 | tf_op jit(solution)/shard_map/all_to_all | solution.py:1202
  124.0 3.5 %stage_first.1 = (bf16[8,128,256]{2,1,0:T(8,128)(2,1)S(1)}, f32[16,2,128]{2,1,0:T(2,128)}, bf16[10,128,256]{2,1,0:T(8,128)(2,1)S(1)}, f32[8,128]{1,0:T(8,128)S(1)}, f32[1,2,128]{2,1,0:T(2,128)S(1)}) custom-call(f32[1,2,128]{2,1,0:T(2,128)S(1)} %get-tuple-element.143.refs_0_, f32[16,2,128]{2,1,0:T(2,128)S(1)} %all-to-all-done.6.refs_1_, ...), custom_call_target="tpu_custom_call" | custom-call | tf_op jit(solution)/shard_map/stage_first/pallas_call | solution.py:1183
  127.5 3.5 %all-to-all-start.7 = ((f32[16,2,128]{2,1,0:T(2,128)}), f32[16,2,128]{2,1,0:T(2,128)S(1)}, u32[]{:S(2)}, u32[]{:S(2)}) async-start(f32[16,2,128]{2,1,0:T(2,128)} %get-tuple-element.154), calls=%async_computation.7 | async-start | bytes 32768 | tf_op jit(solution)/shard_map/all_to_all | solution.py:1202
  131.6 2.6 %grads_first.1.refs_8_ = bf16[2,224,128]{2,1,0:T(8,128)(2,1)} custom-call(bf16[10,128,256]{2,1,0:T(8,128)(2,1)S(1)} %get-tuple-element.157.refs_0_, f32[8,128]{1,0:T(8,128)S(1)} %get-tuple-element.158.refs_1_, bf16[16,128]{1,0:T(8,128)(2,1)S(1)} %broadcast_in_dim.2.refs_2_, bf16[256,2048]{1,0:T(8,128)(2,1)} %get-tuple-element.159.refs_3_), custom_call_target="tpu_custom_call" | custom-call | tf_op jit(solution)/shard_map/grads_first/pallas_call | solution.py:1183
  134.7 2.8 %all-to-all-done.7.refs_1_ = f32[16,2,128]{2,1,0:T(2,128)S(1)} async-done(((f32[16,2,128]{2,1,0:T(2,128)}), f32[16,2,128]{2,1,0:T(2,128)S(1)}, u32[]{:S(2)}, u32[]{:S(2)}) %all-to-all-start.7) | async-done | bytes 16416 | tf_op jit(solution)/shard_map/all_to_all | solution.py:1202
  137.5 3.1 %stage_last.1 = (bf16[2,896,128]{2,1,0:T(8,128)(2,1)S(1)}, bf16[2,896,128]{2,1,0:T(8,128)(2,1)S(1)}, f32[1,1]{1,0:T(1,128)}) custom-call(f32[1,2,128]{2,1,0:T(2,128)S(1)} %get-tuple-element.153.refs_0_, f32[16,2,128]{2,1,0:T(2,128)S(1)} %all-to-all-done.7.refs_1_, bf16[8,128,256]{2,1,0:T(8,128)(2,1)} %get-tuple-element.148.refs_6_.refs_2_, ...), custom_call_target="tpu_custom_call" | custom-call | tf_op jit(solution)/shard_map/stage_last/pallas_call | solution.py:1183
  142.6 17.6 %all_to_all.53.refs_0_ = bf16[16,112,128]{2,1,0:T(8,128)(2,1)S(1)} all-to-all(bf16[16,112,128]{2,1,0:T(8,128)(2,1)S(1)} %bitcast.10), channel_id=1, replica_groups={{0,2,4,6,8,10,12,14,16,18,20,22,24,26,28,30},{1,3,5,7,9,11,13,15,17,19,..., dimensions={0} | all-to-all | bytes 917504 | tf_op jit(solution)/shard_map/all_to_all | solution.py:1492
  160.3 11.1 %all_to_all.54 = bf16[8,112,128]{2,1,0:T(8,128)(2,1)S(1)} all-to-all(bf16[8,112,128]{2,1,0:T(8,128)(2,1)S(1)} %add_up.1), channel_id=1, replica_groups={{0,2,4,6,8,10,12,14},{1,3,5,7,9,11,13,15},{16,18,20,22,24,26,28,30},{17..., dimensions={0} | all-to-all | bytes 458752 | tf_op jit(solution)/shard_map/all_to_all | solution.py:1495
  (32 shorter events, 14.8 us)
Async XLA Ops:
  4.5 6.2 %collective-permute-start = (bf16[32,3584]{1,0:T(8,128)(2,1)S(1)}, bf16[32,3584]{1,0:T(8,128)(2,1)S(1)}, u32[]{:S(2)}, u32[]{:S(2)}) collective-permute-start(bf16[32,3584]{1,0:T(8,128)(2,1)S(1)} %get-tuple-element.92), channel_id=1, source_target_pairs={{0,1},{1,0},{2,3},{3,2},{4,5},{5,4},{6,7},{7,6},{8,9},{9,8},{10,11... | collective-permute-start | bytes 688136 | tf_op jit(solution)/shard_map/ppermute | solution.py:1211
  5.0 5.7 %collective-permute-start.1 = (bf16[32,3584]{1,0:T(8,128)(2,1)S(1)}, bf16[32,3584]{1,0:T(8,128)(2,1)S(1)}, u32[]{:S(2)}, u32[]{:S(2)}) collective-permute-start(bf16[32,3584]{1,0:T(8,128)(2,1)S(1)} %get-tuple-element.93), channel_id=1, source_target_pairs={{1,2},{2,1},{3,4},{4,3},{5,6},{6,5},{7,8},{8,7},{9,10},{10,9},{11,... | collective-permute-start | bytes 688136 | tf_op jit(solution)/shard_map/ppermute | solution.py:1211
  5.7 5.0 %collective-permute-start.2 = (bf16[320,128]{1,0:T(8,128)(2,1)S(1)}, bf16[320,128]{1,0:T(8,128)(2,1)S(1)}, u32[]{:S(2)}, u32[]{:S(2)}) collective-permute-start(bf16[320,128]{1,0:T(8,128)(2,1)S(1)} %get-tuple-element.94.refs_4_.refs_3_), channel_id=1, source_target_pairs={{0,16},{16,0},{1,17},{17,1},{2,18},{18,2},{3,19},{19,3},{4,20},{20... | collective-permute-start | bytes 245768 | tf_op jit(solution)/shard_map/ppermute | solution.py:1216
  29.7 10.5 %collective-permute-start.3 = (bf16[1488,128]{1,0:T(8,128)(2,1)S(1)}, bf16[1488,128]{1,0:T(8,128)(2,1)S(1)}, u32[]{:S(2)}, u32[]{:S(2)}) collective-permute-start(bf16[1488,128]{1,0:T(8,128)(2,1)S(1)} %pack_rest.1.refs_3_.refs_0_), channel_id=1, source_target_pairs={{0,16},{16,0},{1,17},{17,1},{2,18},{18,2},{3,19},{19,3},{4,20},{20... | collective-permute-start | bytes 1142792 | tf_op jit(solution)/shard_map/ppermute | solution.py:1216
  35.1 10.0 %all-to-all-start.1 = ((f32[16,2,128]{2,1,0:T(2,128)}), f32[16,2,128]{2,1,0:T(2,128)S(1)}, u32[]{:S(2)}, u32[]{:S(2)}) async-start(f32[16,2,128]{2,1,0:T(2,128)} %get-tuple-element.98), calls=%async_computation.1 | async-start | bytes 32768 | tf_op jit(solution)/shard_map/all_to_all | solution.py:1202
  50.1 11.7 %collective-permute-start.5 = (f32[128,512]{1,0:T(8,128)S(1)}, f32[128,512]{1,0:T(8,128)S(1)}, u32[]{:S(2)}, u32[]{:S(2)}) collective-permute-start(f32[128,512]{1,0:T(8,128)S(1)} %get-tuple-element.106), channel_id=1, source_target_pairs={{1,2},{2,1},{3,4},{4,3},{5,6},{6,5},{7,8},{8,7},{9,10},{10,9},{11,... | collective-permute-start | bytes 786440 | tf_op jit(solution)/shard_map/ppermute | solution.py:1211
  50.8 11.0 %collective-permute-start.4 = (f32[128,512]{1,0:T(8,128)S(1)}, f32[128,512]{1,0:T(8,128)S(1)}, u32[]{:S(2)}, u32[]{:S(2)}) collective-permute-start(f32[128,512]{1,0:T(8,128)S(1)} %get-tuple-element.106), channel_id=1, source_target_pairs={{0,1},{1,0},{2,3},{3,2},{4,5},{5,4},{6,7},{7,6},{8,9},{9,8},{10,11... | collective-permute-start | bytes 786440 | tf_op jit(solution)/shard_map/ppermute | solution.py:1211
  81.1 12.1 %collective-permute-start.6 = (bf16[128,768]{1,0:T(8,128)(2,1)S(1)}, bf16[128,768]{1,0:T(8,128)(2,1)S(1)}, u32[]{:S(2)}, u32[]{:S(2)}) collective-permute-start(bf16[128,768]{1,0:T(8,128)(2,1)S(1)} %get-tuple-element.120), channel_id=1, source_target_pairs={{0,1},{1,0},{2,3},{3,2},{4,5},{5,4},{6,7},{7,6},{8,9},{9,8},{10,11... | collective-permute-start | bytes 589832 | tf_op jit(solution)/shard_map/ppermute | solution.py:1211
  81.2 12.1 %collective-permute-start.7 = (bf16[128,768]{1,0:T(8,128)(2,1)S(1)}, bf16[128,768]{1,0:T(8,128)(2,1)S(1)}, u32[]{:S(2)}, u32[]{:S(2)}) collective-permute-start(bf16[128,768]{1,0:T(8,128)(2,1)S(1)} %get-tuple-element.121), channel_id=1, source_target_pairs={{1,2},{2,1},{3,4},{4,3},{5,6},{6,5},{7,8},{8,7},{9,10},{10,9},{11,... | collective-permute-start | bytes 589832 | tf_op jit(solution)/shard_map/ppermute | solution.py:1211
  81.9 11.4 %all-to-all-start.4 = ((f32[16,4,128]{2,1,0:T(4,128)}), f32[16,4,128]{2,1,0:T(4,128)S(1)}, u32[]{:S(2)}, u32[]{:S(2)}) async-start(f32[16,4,128]{2,1,0:T(4,128)} %get-tuple-element.119), calls=%async_computation.4 | async-start | bytes 65536 | tf_op jit(solution)/shard_map/all_to_all | solution.py:1202
  97.9 12.0 %collective-permute-start.8 = (bf16[128,768]{1,0:T(8,128)(2,1)S(1)}, bf16[128,768]{1,0:T(8,128)(2,1)S(1)}, u32[]{:S(2)}, u32[]{:S(2)}) collective-permute-start(bf16[128,768]{1,0:T(8,128)(2,1)S(1)} %get-tuple-element.132), channel_id=1, source_target_pairs={{0,1},{1,0},{2,3},{3,2},{4,5},{5,4},{6,7},{7,6},{8,9},{9,8},{10,11... | collective-permute-start | bytes 589832 | tf_op jit(solution)/shard_map/ppermute | solution.py:1211
  98.0 11.9 %collective-permute-start.9 = (bf16[128,768]{1,0:T(8,128)(2,1)S(1)}, bf16[128,768]{1,0:T(8,128)(2,1)S(1)}, u32[]{:S(2)}, u32[]{:S(2)}) collective-permute-start(bf16[128,768]{1,0:T(8,128)(2,1)S(1)} %get-tuple-element.133), channel_id=1, source_target_pairs={{1,2},{2,1},{3,4},{4,3},{5,6},{6,5},{7,8},{8,7},{9,10},{10,9},{11,... | collective-permute-start | bytes 589832 | tf_op jit(solution)/shard_map/ppermute | solution.py:1211
  98.7 11.2 %all-to-all-start.5 = ((f32[16,2,128]{2,1,0:T(2,128)}), f32[16,2,128]{2,1,0:T(2,128)S(1)}, u32[]{:S(2)}, u32[]{:S(2)}) async-start(f32[16,2,128]{2,1,0:T(2,128)} %get-tuple-element.131), calls=%async_computation.5 | async-start | bytes 32768 | tf_op jit(solution)/shard_map/all_to_all | solution.py:1202
  114.1 10.0 %all-to-all-start.6 = ((f32[16,2,128]{2,1,0:T(2,128)}), f32[16,2,128]{2,1,0:T(2,128)S(1)}, u32[]{:S(2)}, u32[]{:S(2)}) async-start(f32[16,2,128]{2,1,0:T(2,128)} %get-tuple-element.144), calls=%async_computation.6 | async-start | bytes 32768 | tf_op jit(solution)/shard_map/all_to_all | solution.py:1202
  127.5 10.0 %all-to-all-start.7 = ((f32[16,2,128]{2,1,0:T(2,128)}), f32[16,2,128]{2,1,0:T(2,128)S(1)}, u32[]{:S(2)}, u32[]{:S(2)}) async-start(f32[16,2,128]{2,1,0:T(2,128)} %get-tuple-element.154), calls=%async_computation.7 | async-start | bytes 32768 | tf_op jit(solution)/shard_map/all_to_all | solution.py:1202
  131.0 3.7 %collective-permute-start.10 = (f32[8,128]{1,0:T(8,128)S(1)}, f32[8,128]{1,0:T(8,128)S(1)}, u32[]{:S(2)}, u32[]{:S(2)}) collective-permute-start(f32[8,128]{1,0:T(8,128)S(1)} %get-tuple-element.160.refs_9_), channel_id=1, source_target_pairs={{0,16},{16,0},{1,17},{17,1},{2,18},{18,2},{3,19},{19,3},{4,20},{20... | collective-permute-start | bytes 12296 | tf_op jit(solution)/shard_map/ppermute | solution.py:1424
  140.6 1.9 %collective-permute-start.11 = (bf16[2,896,128]{2,1,0:T(8,128)(2,1)S(1)}, bf16[2,896,128]{2,1,0:T(8,128)(2,1)S(1)}, u32[]{:S(2)}, u32[]{:S(2)}) collective-permute-start(bf16[2,896,128]{2,1,0:T(8,128)(2,1)S(1)} %get-tuple-element.163), channel_id=1, source_target_pairs={{0,1},{1,0},{2,3},{3,2},{4,5},{5,4},{6,7},{7,6},{8,9},{9,8},{10,11... | collective-permute-start | bytes 1376264 | tf_op jit(solution)/shard_map/ppermute | solution.py:1488
  171.4 1.5 collective-permute-start.12
